TPU v7x, 32 devices: a whole 2x2x4 slice. The times are simulated.
32 devices in a mesh: ens: 2 (over x), face: 16 (over z, y, core).
Axes of the slice: x: 2, y: 2, z: 4, core: 2. Of those that a mesh axis runs over, the one named last changes fastest.
Arguments:
- tracer_adjoint: float32 [2, 50, 128, 2048], P(None, None, 'face', 'ens'), parts along dimension 3, may hold values from -6 to 6
- eta_adjoint: float32 [128, 2048], P('face', 'ens'), parts along dimension 1, may hold values from -18 to 18
- velocity_x: float32 [50, 128, 2048], P(None, 'face', 'ens'), parts along dimension 2, may hold values from -3 to 3
- velocity_y: float32 [50, 128, 2048], P(None, 'face', 'ens'), parts along dimension 2, may hold values from -3 to 3
- mixing: float32 [49, 128, 2048], P(None, 'face', 'ens'), parts along dimension 2, may hold values from 0.05 to 5
- thickness: float32 [50], replicated, may hold values from 0.5 to 4
- surface_damping: float32 [128, 1024], P('face'), may hold values from 0.01 to 0.2
- wet_levels: int32 [128, 1024], P('face'), may hold values from 0 to 50
- seam_codes: int32 [16], P('face'), may hold values from 0 to 1
Outputs:
- tracer_start_adjoint: float32 [2, 50, 128, 2048], P(None, None, 'face', 'ens'), parts along dimension 3
- surface_adjoint: float32 [128, 2048], P('face', 'ens'), parts along dimension 1
There are 2 independent parts, one for each index of `ens`. A program takes and returns all parts, laid end to end along the dimension named above; an argument that names none is the same for every part. Nothing has to cross between parts.
All inputs are finite; a program needn't handle non-finite values.
Results may differ from a plain program's by a relative error of at most 0.00017.
Values sent between devices are 32-bit elements; how exact they have to be, the bound alone decides.
No kernel may reach another device: no remote copies, remote signals or barrier semaphores. Data moves between devices by JAX's collectives and lax.ppermute only.
A program may use at most 128 MiB of HBM per device.

v0:
```python
import jax
import jax.numpy as jnp
from jax import lax
from jax.sharding import PartitionSpec as P

ITERS = 4


diffusion = 0.1
advection = 0.5


def with_halo(x, sides, width):
    for axis, dim in sides:
        count, length = (lax.axis_size(axis), x.shape[dim])
        up = [(i, (i + 1) % count) for i in range(count)]
        down = [(j, i) for i, j in up]
        last = lax.slice_in_dim(x, length - width, length, axis=dim)
        initial = lax.slice_in_dim(x, 0, width, axis=dim)
        before = lax.ppermute(last, axis, up)
        after = lax.ppermute(initial, axis, down)
        x = jnp.concatenate([before, x, after], axis=dim)
    return x


def raised(block_rows, turned):
    upper_row = block_rows[..., -1:, :]
    upper_row = jnp.where(turned, jnp.flip(upper_row, -1), upper_row)
    return jnp.concatenate([block_rows[..., :-1, :], upper_row], axis=-2)


def settled(block_rows, padded, turned):
    lower_rim = padded[..., :1, :]
    upper_rim = padded[..., -1:, :]
    upper_rim = jnp.where(turned, jnp.flip(upper_rim, -1), upper_rim)
    southern = jnp.concatenate([lower_rim, block_rows[..., :-1, :]], axis=-2)
    northern = jnp.concatenate([block_rows[..., 1:, :], upper_rim], axis=-2)
    return (southern, northern)


def surface_apply(values_in, damping, turned):
    padded = with_halo(raised(values_in, turned), (("face", 0),), 1)
    southern, northern = settled(values_in, padded, turned)
    return (4.0 + damping) * values_in - (
        southern + northern + jnp.roll(values_in, 1, -1) + jnp.roll(values_in, -1, -1)
    )


def squares(residual):
    return lax.psum(jnp.sum(residual * residual), "face")


def transposed_solve(right_side, coupling, thickness):
    levels = right_side.shape[1]
    ratios = []
    scaled = []
    for level in range(levels):
        inward = jnp.zeros_like(coupling[0])
        if level > 0:
            inward = coupling[level - 1]
        if level < levels - 1:
            inward = inward + coupling[level]
        pivots = 1.0 + inward / thickness[level]
        numer_term = right_side[:, level]
        if level > 0:
            below_term = -coupling[level - 1] / thickness[level - 1]
            pivots = pivots - below_term * ratios[level - 1]
            numer_term = numer_term - below_term * scaled[level - 1]
        if level < levels - 1:
            ratios.append(-coupling[level] / thickness[level + 1] / pivots)
        scaled.append(numer_term / pivots)
    solved = [scaled[levels - 1]]
    for level in range(levels - 2, -1, -1):
        solved.insert(0, scaled[level] - ratios[level] * solved[0])
    return jnp.stack(solved, axis=1)


def shards(
    tracer_adjoint,
    eta_adjoint,
    velocity_x,
    velocity_y,
    mixing,
    thickness,
    surface_damping,
    wet_levels,
    seam_codes,
):
    turned = seam_codes[0] == 1
    surface = jnp.zeros_like(eta_adjoint)
    residual = eta_adjoint
    direction = eta_adjoint
    norm_now = squares(residual)
    for step in range(ITERS):
        applied = surface_apply(direction, surface_damping, turned)
        step_size = norm_now / lax.psum(jnp.sum(direction * applied), "face")
        surface = surface + step_size * direction
        residual = residual - step_size * applied
        norm_next = squares(residual)
        direction = residual + norm_next / norm_now * direction
        norm_now = norm_next
    levels = tracer_adjoint.shape[1]
    wet_mask = (jnp.arange(levels, dtype=jnp.int32)[:, None, None] < wet_levels[None]).astype(
        jnp.float32
    )
    coupling = mixing * wet_mask[1:]
    first_tracer = tracer_adjoint[0] + thickness[:, None, None] * wet_mask * surface[None]
    loaded = jnp.concatenate([first_tracer[None], tracer_adjoint[1:]], axis=0)
    carried = transposed_solve(loaded, coupling, thickness)
    xflux = velocity_x[None] * carried
    moving = jnp.stack([carried, velocity_y[None] * carried])
    padded = with_halo(raised(moving, turned), (("face", 3),), 1)
    below_all, above_all = settled(moving, padded, turned)
    southern, northern = (below_all[0], above_all[0])
    yflux_south, yflux_north = (below_all[1], above_all[1])
    eastern = jnp.roll(carried, -1, -1)
    western = jnp.roll(carried, 1, -1)
    spread = eastern + western + northern + southern - 4.0 * carried
    moved = (jnp.roll(xflux, -1, -1) - jnp.roll(xflux, 1, -1)) * advection + (
        yflux_north - yflux_south
    ) * advection
    result = wet_mask * (carried + diffusion * spread + moved)
    return (result, surface)


def solution(mesh):
    placed = (
        P(None, None, "face", "ens"),
        P("face", "ens"),
        P(None, "face", "ens"),
        P(None, "face", "ens"),
        P(None, "face", "ens"),
        P(),
        P("face", None),
        P("face", None),
        P("face"),
    )
    return jax.shard_map(
        shards,
        mesh=mesh,
        in_specs=placed,
        out_specs=(P(None, None, "face", "ens"), P("face", "ens")),
        check_vma=False,
    )
```

profile of v0, /device:TPU:0, one launch (start us, length us, event | category | flops | bytes accessed | tf_op | source)
XLA Modules:
  0.0 529.8 jit_solution(5112996241879628083)
XLA Ops:
  3.6 5.5 %collective-permute-start.1 = (f32[1,1024]{1,0:T(1,128)S(1)}, f32[1,1024]{1,0:T(1,128)S(1)}, u32[]{:S(2)}, u32[]{:S(2)}) collective-permute-start(f32[1,1024]{1,0:T(1,128)S(1)} %get-tuple-element.294), channel_id=1, source_target_pairs={{1,0},{2,1},{3,2},{4,3},{5,4},{6,5},{7,6},{8,7},{9,8},{10,9},{11,1... | collective-permute-start | bytes 12296 | tf_op jit(solution)/shard_map/ppermute | solution.py:21
  12.0 1.8 fusion.442
  13.8 2.1 fusion.441
  15.9 2.1 fusion.440
  19.0 2.4 slice_multiply_fusion
  21.3 2.4 fusion.361
  23.7 2.4 fusion.362
  26.1 2.5 fusion.363
  28.6 2.6 fusion.364
  31.2 2.5 fusion.365
  33.7 2.6 fusion.366
  36.3 2.6 fusion.367
  38.8 3.4 fusion.368
  42.2 4.0 fusion.369
  46.2 3.5 fusion.370
  49.7 3.4 fusion.371
  53.1 3.3 fusion.372
  56.4 3.2 fusion.373
  59.6 3.2 fusion.374
  62.9 3.2 fusion.375
  66.1 3.2 fusion.376
  69.3 7.3 %fusion.377 = (f32[8,1024]{1,0:T(8,128)}, f32[1,8,1024]{2,1,0:T(8,128)S(1)}, f32[8,1024]{1,0:T(8,128)}, f32[8,1024]{1,0:T(8,128)}, f32[8,1024]{1,0:T(8,128)}, /*...) fusion(f32[]{:T(128)} %bitcast.71, f32[49,8,1024]{2,1,0:T(8,128)} %copy-done.4, ...), kind=kLoop, calls=%fused_computation.1004 | loop fusion | flops 196608 | bytes 557092 | tf_op jit(solution)/shard_map/mul | solution.py:74
  76.6 6.9 %fusion.378 = (f32[8,1024]{1,0:T(8,128)}, f32[1,8,1024]{2,1,0:T(8,128)S(1)}, f32[8,1024]{1,0:T(8,128)}, f32[8,1024]{1,0:T(8,128)}, f32[8,1024]{1,0:T(8,128)}, /*...) fusion(f32[]{:T(128)} %bitcast.75, f32[49,8,1024]{2,1,0:T(8,128)} %copy-done.4, ...), kind=kLoop, calls=%fused_computation.1005 | loop fusion | flops 196608 | bytes 557092 | tf_op jit(solution)/shard_map/mul | solution.py:74
  83.6 7.4 %fusion.379 = (f32[8,1024]{1,0:T(8,128)}, f32[1,8,1024]{2,1,0:T(8,128)S(1)}, f32[8,1024]{1,0:T(8,128)}, f32[8,1024]{1,0:T(8,128)}, f32[8,1024]{1,0:T(8,128)}, /*...) fusion(f32[]{:T(128)} %bitcast.79, f32[49,8,1024]{2,1,0:T(8,128)} %copy-done.4, ...), kind=kLoop, calls=%fused_computation.1006 | loop fusion | flops 196608 | bytes 557092 | tf_op jit(solution)/shard_map/mul | solution.py:74
  91.0 6.3 %fusion.380 = (f32[8,1024]{1,0:T(8,128)}, f32[1,8,1024]{2,1,0:T(8,128)S(1)}, f32[8,1024]{1,0:T(8,128)}, f32[8,1024]{1,0:T(8,128)}, f32[8,1024]{1,0:T(8,128)}, /*...) fusion(f32[]{:T(128)} %bitcast.83, f32[49,8,1024]{2,1,0:T(8,128)S(1)} %copy-done.5, ...), kind=kLoop, calls=%fused_computation.1007 | loop fusion | flops 196608 | bytes 557092 | tf_op jit(solution)/shard_map/mul | solution.py:74
  97.3 6.2 %fusion.381 = (f32[8,1024]{1,0:T(8,128)}, f32[1,8,1024]{2,1,0:T(8,128)S(1)}, f32[8,1024]{1,0:T(8,128)}, f32[8,1024]{1,0:T(8,128)}, f32[8,1024]{1,0:T(8,128)}, /*...) fusion(f32[]{:T(128)} %bitcast.87, f32[49,8,1024]{2,1,0:T(8,128)S(1)} %copy-done.5, ...), kind=kLoop, calls=%fused_computation.1008 | loop fusion | flops 196608 | bytes 557092 | tf_op jit(solution)/shard_map/mul | solution.py:74
  103.5 6.3 %fusion.382 = (f32[8,1024]{1,0:T(8,128)}, f32[1,8,1024]{2,1,0:T(8,128)S(1)}, f32[8,1024]{1,0:T(8,128)}, f32[8,1024]{1,0:T(8,128)}, f32[8,1024]{1,0:T(8,128)}, /*...) fusion(f32[]{:T(128)} %bitcast.91, f32[49,8,1024]{2,1,0:T(8,128)S(1)} %copy-done.5, ...), kind=kLoop, calls=%fused_computation.1009 | loop fusion | flops 196608 | bytes 557092 | tf_op jit(solution)/shard_map/mul | solution.py:74
  109.8 3.1 fusion.383
  112.9 3.2 fusion.384
  116.1 2.5 fusion.385
  118.7 2.5 fusion.386
  121.2 2.4 fusion.387
  124.1 2.4 fusion.388
  126.7 32.8 %bitcast_subtract_fusion.27 = (f32[8,1024]{1,0:T(8,128)}, f32[8,1024]{1,0:T(8,128)}, f32[8,1024]{1,0:T(8,128)}, f32[8,1024]{1,0:T(8,128)}, f32[8,1024]{1,0:T(8,1...) fusion(f32[49,8,1024]{2,1,0:T(8,128)S(1)} %copy-done.5, ...), kind=kLoop, calls=%fused_computation.517 | loop fusion | flops 3620864 | bytes 2835968 | tf_op jit(solution)/shard_map/sub | solution.py:67
  161.9 34.6 %all-reduce = (f32[]{:T(128)}, f32[]{:T(128)}) all-reduce(f32[]{:T(128)} %get-tuple-element.3, f32[]{:T(128)} %get-tuple-element.2), channel_id=1, replica_groups=mesh['ens'=2,'face'=16] {'face'}, use_global_device_ids=true, to_apply=%region_1.0 | all-reduce | flops 2 | bytes 16 | tf_op jit(solution)/shard_map/psum | solution.py:50
  198.4 2.4 fusion.389
  200.8 30.1 %psum.58 = f32[]{:T(128)} all-reduce(f32[]{:T(128)} %multiply_reduce_fusion.4), channel_id=1, replica_groups=mesh['ens'=2,'face'=16] {'face'}, use_global_device_ids=true, to_apply=%region_5.6 | all-reduce | flops 1 | bytes 8 | tf_op jit(solution)/shard_map/psum | solution.py:50
  236.9 2.7 rev.35
  239.7 2.1 collective-permute-done.2
  241.7 2.1 multiply_reduce_fusion.3
  243.9 32.4 %psum.59 = f32[]{:T(128)} all-reduce(f32[]{:T(128)} %get-tuple-element.206), channel_id=1, replica_groups=mesh['ens'=2,'face'=16] {'face'}, use_global_device_ids=true, to_apply=%region_7.8 | all-reduce | flops 1 | bytes 8 | tf_op jit(solution)/shard_map/psum | solution.py:96
  279.0 30.2 %psum.60 = f32[]{:T(128)} all-reduce(f32[]{:T(128)} %get-tuple-element.204), channel_id=1, replica_groups=mesh['ens'=2,'face'=16] {'face'}, use_global_device_ids=true, to_apply=%region_9.10 | all-reduce | flops 1 | bytes 8 | tf_op jit(solution)/shard_map/psum | solution.py:50
  314.5 2.6 rev.37
  317.2 2.1 collective-permute-done.4
  319.3 2.1 multiply_reduce_fusion.1
  321.4 32.4 %psum.61 = f32[]{:T(128)} all-reduce(f32[]{:T(128)} %get-tuple-element.202), channel_id=1, replica_groups=mesh['ens'=2,'face'=16] {'face'}, use_global_device_ids=true, to_apply=%region_11.12 | all-reduce | flops 1 | bytes 8 | tf_op jit(solution)/shard_map/psum | solution.py:96
  356.6 5.7 %fusion.390 = (f32[8,1024]{1,0:T(8,128)}, f32[1,8,1024]{2,1,0:T(8,128)}, f32[8,1024]{1,0:T(8,128)}, f32[8,1024]{1,0:T(8,128)}, f32[8,1024]{1,0:T(8,128)}, /*index=5*/f32[8,1024]{1,0:T(8,128)}, f32[8,1024]{1,0:T(8,128)S(1)}) fusion(f32[]{:T(128)} %bitcast.123, f32[49,8,1024]{2,1,0:T(8,128)S(1)} %copy-done.5, f32[1,8,1024]{2,1,0:T(8,128)S(1)} %get-tuple-element.120, ...), kind=kLoop, calls=%fused_computation.1017 | loop fusion | flops 180224 | bytes 491552 | tf_op jit(solution)/shard_map/mul | solution.py:74
  362.3 30.1 %psum.62 = f32[]{:T(128)} all-reduce(f32[]{:T(128)} %multiply_reduce_fusion), channel_id=1, replica_groups=mesh['ens'=2,'face'=16] {'face'}, use_global_device_ids=true, to_apply=%region_13.14 | all-reduce | flops 1 | bytes 8 | tf_op jit(solution)/shard_map/psum | solution.py:50
  399.2 4.7 collective-permute-done.6
  405.4 6.9 %divide_bitcast_fusion.18 = (f32[8,1024]{1,0:T(8,128)}, f32[1,8,1024]{2,1,0:T(8,128)}, f32[8,1024]{1,0:T(8,128)}, f32[8,1024]{1,0:T(8,128)}, f32[8,1024]{1,0:T(8...) fusion(f32[49,8,1024]{2,1,0:T(8,128)S(1)} %copy-done.5, f32[]{:T(128)} %bitcast.127, ...), kind=kLoop, calls=%fused_computation.759 | loop fusion | flops 229376 | bytes 589860 | tf_op jit(solution)/shard_map/mul | solution.py:74
  412.7 30.3 %psum.63 = f32[]{:T(128)} all-reduce(f32[]{:T(128)} %fusion.172), channel_id=1, replica_groups=mesh['ens'=2,'face'=16] {'face'}, use_global_device_ids=true, to_apply=%region_15.16 | all-reduce | flops 1 | bytes 8 | tf_op jit(solution)/shard_map/psum | solution.py:96
  446.4 2.3 subtract_divide_fusion
  448.8 2.5 constant_dynamic-update-slice_fusion.99
  454.4 2.4 fusion.68
  462.4 2.2 fusion.15
  464.6 10.2 %rev.41 = f32[2,2,50,1,1024]{4,3,2,1,0:T(1,128)} reverse(f32[2,2,50,1,1024]{4,3,2,1,0:T(1,128)} %get-tuple-element.209), dimensions={4} | reverse | bytes 1638400 | tf_op jit(solution)/shard_map/jit(_flip)/rev | solution.py:28
  474.9 2.9 broadcast_select_fusion
  477.8 6.2 %fusion = f32[2,2,50,7,1024]{4,3,2,1,0:T(8,128)} fusion(f32[1,2,50,8,1024]{4,3,2,1,0:T(8,128)S(1)} %bitcast.1858, f32[1,2,50,8,1024]{4,3,2,1,0:T(8,128)} %copy-done), kind=kLoop, calls=%fused_computation.104 | loop fusion | flops 1433600 | bytes 12288000 | tf_op jit(solution)/shard_map/stack | solution.py:111
  484.0 4.4 collective-permute-start.8
  488.5 9.5 %fusion.424 = (f32[2,50,8,1023]{3,2,1,0:T(8,128)}, f32[2,50,8,1023]{3,2,1,0:T(8,128)}, f32[2,50,8,1023]{3,2,1,0:T(8,128)}, f32[2,50,8,1023]{3,2,1,0:T(8,128)}) fusion(f32[2,50,8,1024]{3,2,1,0:T(8,128)} %copy-done.3, f32[2,50,8,1024]{3,2,1,0:T(8,128)S(1)} %constant_dynamic-update-slice_fusion), kind=kLoop, calls=%fused_computation.1020 | loop fusion | bytes 26188800 | tf_op jit(solution)/shard_map/jit(_roll_static)/slice | solution.py:119
  497.9 6.6 %fusion.1 = f32[2,2,50,8,1024]{4,3,2,1,0:T(8,128)} fusion(f32[1,2,50,8,1024]{4,3,2,1,0:T(8,128)} %copy-done, f32[1,2,50,8,1024]{4,3,2,1,0:T(8,128)S(1)} %bitcast.1859, f32[2,2,50,1,1024]{4,3,2,1,0:T(1,128)} %collective-permute-done.9), kind=kLoop, calls=%fused_computation.106 | loop fusion | flops 3276800 | bytes 13926400 | tf_op jit(solution)/shard_map/concatenate | solution.py:36
  504.6 10.2 %rev.40 = f32[2,2,50,1,1024]{4,3,2,1,0:T(1,128)} reverse(f32[2,2,50,1,1024]{4,3,2,1,0:T(1,128)} %collective-permute-done.8), dimensions={4} | reverse | bytes 1638400 | tf_op jit(solution)/shard_map/jit(_flip)/rev | solution.py:35
  514.8 2.1 broadcast_select_fusion.1
  516.9 12.9 %fusion.10 = f32[2,50,8,1024]{3,2,1,0:T(8,128)} fusion(f32[2,50,8,1024]{3,2,1,0:T(8,128)S(1)} %constant_dynamic-update-slice_fusion, f32[2,2,50,7,1024]{4,3,2,1,0:T(8,128)} %fusion, f32[2,2,50,1,1024]{4,3,2,1,0:T(1,128)S(1)} %broadcast_select_fusion.1, f32[2,2,50,8,1024]{4,3,2,1,0:T(8,128)} %fusion.1, f32[2,50,8,1]{3,2,1,0:T(8,128)} %get-tuple-element.351, ...), kind=kLoop, calls=%fused_computation.117 | loop fusion | flops 15564800 | bytes 34406400 | tf_op jit(solution)/shard_map/mul | solution.py:122
  (401 shorter events, 37.8 us)
Async XLA Ops:
  3.6 156.0 %collective-permute-start.1 = (f32[1,1024]{1,0:T(1,128)S(1)}, f32[1,1024]{1,0:T(1,128)S(1)}, u32[]{:S(2)}, u32[]{:S(2)}) collective-permute-start(f32[1,1024]{1,0:T(1,128)S(1)} %get-tuple-element.294), channel_id=1, source_target_pairs={{1,0},{2,1},{3,2},{4,3},{5,4},{6,5},{7,6},{8,7},{9,8},{10,9},{11,1... | collective-permute-start | bytes 12296 | tf_op jit(solution)/shard_map/ppermute | solution.py:21
  9.1 151.2 %collective-permute-start = (f32[1,1024]{1,0:T(1,128)S(1)}, f32[1,1024]{1,0:T(1,128)S(1)}, u32[]{:S(2)}, u32[]{:S(2)}) collective-permute-start(f32[1,1024]{1,0:T(1,128)S(1)} %get-tuple-element.293), channel_id=1, source_target_pairs={{0,1},{1,2},{2,3},{3,4},{4,5},{5,6},{6,7},{7,8},{8,9},{9,10},{10,1... | collective-permute-start | bytes 12296 | tf_op jit(solution)/shard_map/ppermute | solution.py:20
  18.9 34.1 %copy-start.6 = (f32[50,8,1024]{2,1,0:T(8,128)}, f32[50,8,1024]{2,1,0:T(8,128)S(1)}, u32[]{:S(2)}) copy-start(f32[50,8,1024]{2,1,0:T(8,128)S(1)} %fusion.14) | copy-start | bytes 4915204
  33.7 89.9 %copy-start.101 = (f32[1,8,1024]{2,1,0:T(8,128)}, f32[1,8,1024]{2,1,0:T(8,128)S(1)}, u32[]{:S(2)}) copy-start(f32[1,8,1024]{2,1,0:T(8,128)S(1)} %get-tuple-element.72) | copy-start | bytes 98308
  38.8 84.7 %copy-start.103 = (f32[1,8,1024]{2,1,0:T(8,128)}, f32[1,8,1024]{2,1,0:T(8,128)S(1)}, u32[]{:S(2)}) copy-start(f32[1,8,1024]{2,1,0:T(8,128)S(1)} %get-tuple-element.76) | copy-start | bytes 98308
  42.2 48.8 %copy-start.5 = (f32[49,8,1024]{2,1,0:T(8,128)S(1)}, f32[49,8,1024]{2,1,0:T(8,128)}, u32[]{:S(2)}) copy-start(f32[49,8,1024]{2,1,0:T(8,128)} %copy-done.4) | copy-start | bytes 4816900
  42.2 84.3 %copy-start.8 = (f32[2,50,8,1024]{3,2,1,0:T(8,128)S(1)}, f32[2,50,8,1024]{3,2,1,0:T(8,128)}, u32[]{:S(2)}) copy-start(f32[2,50,8,1024]{3,2,1,0:T(8,128)} %param.9) | copy-start | bytes 9830404
  46.2 77.3 %copy-start.104 = (f32[1,8,1024]{2,1,0:T(8,128)}, f32[1,8,1024]{2,1,0:T(8,128)S(1)}, u32[]{:S(2)}) copy-start(f32[1,8,1024]{2,1,0:T(8,128)S(1)} %get-tuple-element.80) | copy-start | bytes 98308
  49.7 69.0 %copy-start.13 = (f32[1,8,1024]{2,1,0:T(8,128)}, f32[1,8,1024]{2,1,0:T(8,128)S(1)}, u32[]{:S(2)}) copy-start(f32[1,8,1024]{2,1,0:T(8,128)S(1)} %get-tuple-element.82) | copy-start | bytes 98308
  53.1 70.5 %copy-start.105 = (f32[1,8,1024]{2,1,0:T(8,128)}, f32[1,8,1024]{2,1,0:T(8,128)S(1)}, u32[]{:S(2)}) copy-start(f32[1,8,1024]{2,1,0:T(8,128)S(1)} %get-tuple-element.84) | copy-start | bytes 98308
  56.4 67.1 %copy-start.16 = (f32[1,8,1024]{2,1,0:T(8,128)}, f32[1,8,1024]{2,1,0:T(8,128)S(1)}, u32[]{:S(2)}) copy-start(f32[1,8,1024]{2,1,0:T(8,128)S(1)} %get-tuple-element.86) | copy-start | bytes 98308
  62.9 60.7 %copy-start.19 = (f32[1,8,1024]{2,1,0:T(8,128)}, f32[1,8,1024]{2,1,0:T(8,128)S(1)}, u32[]{:S(2)}) copy-start(f32[1,8,1024]{2,1,0:T(8,128)S(1)} %get-tuple-element.90) | copy-start | bytes 98308
  69.3 54.3 %copy-start.22 = (f32[1,8,1024]{2,1,0:T(8,128)}, f32[1,8,1024]{2,1,0:T(8,128)S(1)}, u32[]{:S(2)}) copy-start(f32[1,8,1024]{2,1,0:T(8,128)S(1)} %get-tuple-element.94) | copy-start | bytes 98308
  83.6 40.0 %copy-start.25 = (f32[1,8,1024]{2,1,0:T(8,128)}, f32[1,8,1024]{2,1,0:T(8,128)S(1)}, u32[]{:S(2)}) copy-start(f32[1,8,1024]{2,1,0:T(8,128)S(1)} %get-tuple-element.98) | copy-start | bytes 98308
  121.2 38.4 %copy-start.9 = (f32[8,1024]{1,0:T(8,128)S(1)}, f32[8,1024]{1,0:T(8,128)}, u32[]{:S(2)}) copy-start(f32[8,1024]{1,0:T(8,128)} %param.10) | copy-start | bytes 98308
  121.2 39.2 %copy-start.116 = (f32[8,1024]{1,0:T(8,128)S(1)}, f32[8,1024]{1,0:T(8,128)}, u32[]{:S(2)}) copy-start(f32[8,1024]{1,0:T(8,128)} %param.15) | copy-start | bytes 98308
  126.5 74.3 %copy-start.40 = (f32[1,8,1024]{2,1,0:T(8,128)}, f32[1,8,1024]{2,1,0:T(8,128)S(1)}, u32[]{:S(2)}) copy-start(f32[1,8,1024]{2,1,0:T(8,128)S(1)} %get-tuple-element.118) | copy-start | bytes 98308
  126.7 322.0 %copy-start.1 = (f32[1,50,8,1024]{3,2,0,1:T(8,128)}, f32[1,50,8,1024]{3,2,0,1:T(8,128)S(1)}, u32[]{:S(2)}) copy-start(f32[1,50,8,1024]{3,2,0,1:T(8,128)S(1)} %slice_bitcast_fusion.1) | copy-start | bytes 4915204
  126.7 317.6 %copy-start.12 = (f32[50]{0:T(128)S(1)}, f32[50]{0:T(128)}, u32[]{:S(2)}) copy-start(f32[50]{0:T(128)} %param.14) | copy-start | bytes 604
  161.9 69.1 %copy-start.117 = (f32[8,1024]{1,0:T(8,128)}, f32[8,1024]{1,0:T(8,128)S(1)}, u32[]{:S(2)}) copy-start(f32[8,1024]{1,0:T(8,128)S(1)} %get-tuple-element.208) | copy-start | bytes 98308
  200.8 191.6 %copy-start.115 = (f32[1,8,1024]{2,1,0:T(8,128)}, f32[1,8,1024]{2,1,0:T(8,128)S(1)}, u32[]{:S(2)}) copy-start(f32[1,8,1024]{2,1,0:T(8,128)S(1)} %get-tuple-element.120) | copy-start | bytes 98308
  235.6 1.3 collective-permute-start.3
  235.7 6.0 %collective-permute-start.2 = (f32[1,1024]{1,0:T(1,128)}, f32[1,1024]{1,0:T(1,128)}, u32[]{:S(2)}, u32[]{:S(2)}) collective-permute-start(f32[1,1024]{1,0:T(1,128)} %get-tuple-element.285), channel_id=1, source_target_pairs={{0,1},{1,2},{2,3},{3,4},{4,5},{5,6},{6,7},{7,8},{8,9},{9,10},{10,1... | collective-permute-start | bytes 12296 | tf_op jit(solution)/shard_map/ppermute | solution.py:20
  279.0 77.6 %copy-start.118 = (f32[8,1024]{1,0:T(8,128)}, f32[8,1024]{1,0:T(8,128)S(1)}, u32[]{:S(2)}) copy-start(f32[8,1024]{1,0:T(8,128)S(1)} %get-tuple-element.205) | copy-start | bytes 98308
  313.2 1.3 collective-permute-start.5
  313.2 6.0 %collective-permute-start.4 = (f32[1,1024]{1,0:T(1,128)}, f32[1,1024]{1,0:T(1,128)}, u32[]{:S(2)}, u32[]{:S(2)}) collective-permute-start(f32[1,1024]{1,0:T(1,128)} %get-tuple-element.277), channel_id=1, source_target_pairs={{0,1},{1,2},{2,3},{3,4},{4,5},{5,6},{6,7},{7,8},{8,9},{9,10},{10,1... | collective-permute-start | bytes 12296 | tf_op jit(solution)/shard_map/ppermute | solution.py:20
  397.1 1.3 collective-permute-start.7
  397.8 6.0 %collective-permute-start.6 = (f32[1,1024]{1,0:T(1,128)}, f32[1,1024]{1,0:T(1,128)}, u32[]{:S(2)}, u32[]{:S(2)}) collective-permute-start(f32[1,1024]{1,0:T(1,128)} %get-tuple-element.276), channel_id=1, source_target_pairs={{0,1},{1,2},{2,3},{3,4},{4,5},{5,6},{6,7},{7,8},{8,9},{9,10},{10,1... | collective-permute-start | bytes 12296 | tf_op jit(solution)/shard_map/ppermute | solution.py:20
  412.4 33.7 %copy-start.20 = (f32[1,8,1024]{2,1,0:T(8,128)S(1)}, f32[1,8,1024]{2,1,0:T(8,128)}, u32[]{:S(2)}) copy-start(f32[1,8,1024]{2,1,0:T(8,128)} %copy-done.19) | copy-start | bytes 98308
  412.4 33.7 %copy-start.23 = (f32[1,8,1024]{2,1,0:T(8,128)S(1)}, f32[1,8,1024]{2,1,0:T(8,128)}, u32[]{:S(2)}) copy-start(f32[1,8,1024]{2,1,0:T(8,128)} %copy-done.22) | copy-start | bytes 98308
  412.4 33.7 %copy-start.26 = (f32[1,8,1024]{2,1,0:T(8,128)S(1)}, f32[1,8,1024]{2,1,0:T(8,128)}, u32[]{:S(2)}) copy-start(f32[1,8,1024]{2,1,0:T(8,128)} %copy-done.25) | copy-start | bytes 98308
  412.4 33.7 %copy-start.29 = (f32[1,8,1024]{2,1,0:T(8,128)S(1)}, f32[1,8,1024]{2,1,0:T(8,128)}, u32[]{:S(2)}) copy-start(f32[1,8,1024]{2,1,0:T(8,128)} %copy-done.28) | copy-start | bytes 98308
  412.4 33.7 %copy-start.32 = (f32[1,8,1024]{2,1,0:T(8,128)S(1)}, f32[1,8,1024]{2,1,0:T(8,128)}, u32[]{:S(2)}) copy-start(f32[1,8,1024]{2,1,0:T(8,128)} %copy-done.31) | copy-start | bytes 98308
  412.4 33.7 %copy-start.35 = (f32[1,8,1024]{2,1,0:T(8,128)S(1)}, f32[1,8,1024]{2,1,0:T(8,128)}, u32[]{:S(2)}) copy-start(f32[1,8,1024]{2,1,0:T(8,128)} %copy-done.34) | copy-start | bytes 98308
  412.4 33.7 %copy-start.38 = (f32[1,8,1024]{2,1,0:T(8,128)S(1)}, f32[1,8,1024]{2,1,0:T(8,128)}, u32[]{:S(2)}) copy-start(f32[1,8,1024]{2,1,0:T(8,128)} %copy-done.37) | copy-start | bytes 98308
  412.4 33.7 %copy-start.41 = (f32[1,8,1024]{2,1,0:T(8,128)S(1)}, f32[1,8,1024]{2,1,0:T(8,128)}, u32[]{:S(2)}) copy-start(f32[1,8,1024]{2,1,0:T(8,128)} %copy-done.40) | copy-start | bytes 98308
  412.4 33.7 %copy-start.43 = (f32[1,8,1024]{2,1,0:T(8,128)S(1)}, f32[1,8,1024]{2,1,0:T(8,128)}, u32[]{:S(2)}) copy-start(f32[1,8,1024]{2,1,0:T(8,128)} %get-tuple-element.122) | copy-start | bytes 98308
  412.4 33.7 %copy-start.45 = (f32[8,1024]{1,0:T(8,128)S(1)}, f32[8,1024]{1,0:T(8,128)}, u32[]{:S(2)}) copy-start(f32[8,1024]{1,0:T(8,128)} %get-tuple-element.143) | copy-start | bytes 98308
  412.4 33.7 %copy-start.47 = (f32[8,1024]{1,0:T(8,128)S(1)}, f32[8,1024]{1,0:T(8,128)}, u32[]{:S(2)}) copy-start(f32[8,1024]{1,0:T(8,128)} %get-tuple-element.147) | copy-start | bytes 98308
  412.5 33.7 %copy-start.49 = (f32[8,1024]{1,0:T(8,128)S(1)}, f32[8,1024]{1,0:T(8,128)}, u32[]{:S(2)}) copy-start(f32[8,1024]{1,0:T(8,128)} %get-tuple-element.151) | copy-start | bytes 98308
  412.5 33.7 %copy-start.51 = (f32[8,1024]{1,0:T(8,128)S(1)}, f32[8,1024]{1,0:T(8,128)}, u32[]{:S(2)}) copy-start(f32[8,1024]{1,0:T(8,128)} %get-tuple-element.155) | copy-start | bytes 98308
  412.5 33.7 %copy-start.53 = (f32[8,1024]{1,0:T(8,128)S(1)}, f32[8,1024]{1,0:T(8,128)}, u32[]{:S(2)}) copy-start(f32[8,1024]{1,0:T(8,128)} %get-tuple-element.159) | copy-start | bytes 98308
  412.5 33.7 %copy-start.57 = (f32[8,1024]{1,0:T(8,128)S(1)}, f32[8,1024]{1,0:T(8,128)}, u32[]{:S(2)}) copy-start(f32[8,1024]{1,0:T(8,128)} %get-tuple-element.228) | copy-start | bytes 98308
  412.5 33.7 %copy-start.59 = (f32[8,1024]{1,0:T(8,128)S(1)}, f32[8,1024]{1,0:T(8,128)}, u32[]{:S(2)}) copy-start(f32[8,1024]{1,0:T(8,128)} %get-tuple-element.230) | copy-start | bytes 98308
  412.5 33.7 %copy-start.61 = (f32[8,1024]{1,0:T(8,128)S(1)}, f32[8,1024]{1,0:T(8,128)}, u32[]{:S(2)}) copy-start(f32[8,1024]{1,0:T(8,128)} %get-tuple-element.232) | copy-start | bytes 98308
  412.5 33.7 %copy-start.63 = (f32[8,1024]{1,0:T(8,128)S(1)}, f32[8,1024]{1,0:T(8,128)}, u32[]{:S(2)}) copy-start(f32[8,1024]{1,0:T(8,128)} %get-tuple-element.234) | copy-start | bytes 98308
  412.5 33.7 %copy-start.65 = (f32[8,1024]{1,0:T(8,128)S(1)}, f32[8,1024]{1,0:T(8,128)}, u32[]{:S(2)}) copy-start(f32[8,1024]{1,0:T(8,128)} %get-tuple-element.236) | copy-start | bytes 98308
  412.5 33.7 %copy-start.67 = (f32[8,1024]{1,0:T(8,128)S(1)}, f32[8,1024]{1,0:T(8,128)}, u32[]{:S(2)}) copy-start(f32[8,1024]{1,0:T(8,128)} %get-tuple-element.238) | copy-start | bytes 98308
  412.5 33.7 %copy-start.69 = (f32[8,1024]{1,0:T(8,128)S(1)}, f32[8,1024]{1,0:T(8,128)}, u32[]{:S(2)}) copy-start(f32[8,1024]{1,0:T(8,128)} %get-tuple-element.240) | copy-start | bytes 98308
  412.6 33.7 %copy-start.71 = (f32[8,1024]{1,0:T(8,128)S(1)}, f32[8,1024]{1,0:T(8,128)}, u32[]{:S(2)}) copy-start(f32[8,1024]{1,0:T(8,128)} %get-tuple-element.242) | copy-start | bytes 98308
  412.6 33.7 %copy-start.73 = (f32[8,1024]{1,0:T(8,128)S(1)}, f32[8,1024]{1,0:T(8,128)}, u32[]{:S(2)}) copy-start(f32[8,1024]{1,0:T(8,128)} %get-tuple-element.244) | copy-start | bytes 98308
  412.6 33.7 %copy-start.75 = (f32[8,1024]{1,0:T(8,128)S(1)}, f32[8,1024]{1,0:T(8,128)}, u32[]{:S(2)}) copy-start(f32[8,1024]{1,0:T(8,128)} %get-tuple-element.246) | copy-start | bytes 98308
  412.6 33.7 %copy-start.77 = (f32[8,1024]{1,0:T(8,128)S(1)}, f32[8,1024]{1,0:T(8,128)}, u32[]{:S(2)}) copy-start(f32[8,1024]{1,0:T(8,128)} %get-tuple-element.250) | copy-start | bytes 98308
  412.6 33.7 %copy-start.79 = (f32[8,1024]{1,0:T(8,128)S(1)}, f32[8,1024]{1,0:T(8,128)}, u32[]{:S(2)}) copy-start(f32[8,1024]{1,0:T(8,128)} %get-tuple-element.252) | copy-start | bytes 98308
  412.6 33.7 %copy-start.81 = (f32[8,1024]{1,0:T(8,128)S(1)}, f32[8,1024]{1,0:T(8,128)}, u32[]{:S(2)}) copy-start(f32[8,1024]{1,0:T(8,128)} %get-tuple-element.254) | copy-start | bytes 98308
  412.6 33.7 %copy-start.83 = (f32[8,1024]{1,0:T(8,128)S(1)}, f32[8,1024]{1,0:T(8,128)}, u32[]{:S(2)}) copy-start(f32[8,1024]{1,0:T(8,128)} %get-tuple-element.256) | copy-start | bytes 98308
  412.6 33.7 %copy-start.85 = (f32[8,1024]{1,0:T(8,128)S(1)}, f32[8,1024]{1,0:T(8,128)}, u32[]{:S(2)}) copy-start(f32[8,1024]{1,0:T(8,128)} %get-tuple-element.248) | copy-start | bytes 98308
  412.6 33.7 %copy-start.87 = (f32[8,1024]{1,0:T(8,128)S(1)}, f32[8,1024]{1,0:T(8,128)}, u32[]{:S(2)}) copy-start(f32[8,1024]{1,0:T(8,128)} %get-tuple-element.264) | copy-start | bytes 98308
  412.6 33.7 %copy-start.89 = (f32[8,1024]{1,0:T(8,128)S(1)}, f32[8,1024]{1,0:T(8,128)}, u32[]{:S(2)}) copy-start(f32[8,1024]{1,0:T(8,128)} %get-tuple-element.266) | copy-start | bytes 98308
  412.7 33.7 %copy-start.91 = (f32[8,1024]{1,0:T(8,128)S(1)}, f32[8,1024]{1,0:T(8,128)}, u32[]{:S(2)}) copy-start(f32[8,1024]{1,0:T(8,128)} %get-tuple-element.258) | copy-start | bytes 98308
  412.7 33.7 %copy-start.93 = (f32[8,1024]{1,0:T(8,128)S(1)}, f32[8,1024]{1,0:T(8,128)}, u32[]{:S(2)}) copy-start(f32[8,1024]{1,0:T(8,128)} %get-tuple-element.260) | copy-start | bytes 98308
  412.7 33.7 %copy-start.95 = (f32[8,1024]{1,0:T(8,128)S(1)}, f32[8,1024]{1,0:T(8,128)}, u32[]{:S(2)}) copy-start(f32[8,1024]{1,0:T(8,128)} %get-tuple-element.262) | copy-start | bytes 98308
  477.8 20.2 %collective-permute-start.9 = (f32[2,2,50,1,1024]{4,3,2,1,0:T(1,128)}, f32[2,2,50,1,1024]{4,3,2,1,0:T(1,128)}, u32[]{:S(2)}, u32[]{:S(2)}) collective-permute-start(f32[2,2,50,1,1024]{4,3,2,1,0:T(1,128)} %broadcast_select_fusion), channel_id=1, source_target_pairs={{0,1},{1,2},{2,3},{3,4},{4,5},{5,6},{6,7},{7,8},{8,9},{9,10},{10,1... | collective-permute-start | bytes 2457608 | tf_op jit(solution)/shard_map/ppermute | solution.py:20
  484.0 20.6 %collective-permute-start.8 = (f32[2,2,50,1,1024]{4,3,2,1,0:T(1,128)}, f32[2,2,50,1,1024]{4,3,2,1,0:T(1,128)}, u32[]{:S(2)}, u32[]{:S(2)}) collective-permute-start(f32[2,2,50,1,1024]{4,3,2,1,0:T(1,128)} %get-tuple-element.210), channel_id=1, source_target_pairs={{1,0},{2,1},{3,2},{4,3},{5,4},{6,5},{7,6},{8,7},{9,8},{10,9},{11,1... | collective-permute-start | bytes 2457608 | tf_op jit(solution)/shard_map/ppermute | solution.py:21
  (67 other events, 301.2 us)
where the time goes:
time: 537 us; the launch traced here: 530 us
  blocking collectives  220 us (41%)
  other arithmetic  216 us (40%)
  local copies, waits for them, and re-layouts  58.6 us (11%)
  between operations  12.8 us (2%)
  starting transfers between devices  11.5 us (2%)
  waiting for transfers between devices  10.5 us (2%)
    psum x4, blocking collectives, squares(): return lax.psum(jnp.sum(residual * residual), 'face')  125 us
    mul x31, other arithmetic, transposed_solve(): solved.insert(0, scaled[level] - ratios[level] * solved[0])  120 us
    psum x3, blocking collectives, shards(): step_size = norm_now / lax.psum(jnp.sum(direction * applied), 'face')  95.1 us
    sub x1, other arithmetic, transposed_solve(): pivots = pivots - below_term * ratios[level - 1]  32.8 us
    rev x5, local copies, waits for them, and re-layouts, settled(): upper_rim = jnp.where(turned, jnp.flip(upper_rim, -1), upper_rim)  16.9 us
    rev x5, local copies, waits for them, and re-layouts, raised(): upper_row = jnp.where(turned, jnp.flip(upper_row, -1), upper_row)  13 us
    mul x1, other arithmetic, shards(): result = wet_mask * (carried + diffusion * spread + moved)  12.9 us
    slice x2, local copies, waits for them, and re-layouts, shards(): jnp.roll(xflux, 1, -1)  10.9 us
  transfers between devices with their start and end apart: 10, of which 6 were waited for; matrix products, arithmetic and copies ran while one was open for 34% of the time, Pallas kernels for 0%

commit v1 on v0

v1 whole, which is shorter than its diff:
```python
import functools
import jax
import jax.numpy as jnp
from jax import lax
from jax.experimental import pallas as pl
from jax.experimental.pallas import tpu as pltpu
from jax.sharding import PartitionSpec as P

ITERS = 4
LANES = 128
SUBLANES = 8
diffusion = 0.1
advection = 0.5

MIDDLE = 4.1
LOSS = 1000.0

SMEM = pl.BlockSpec(memory_space=pltpu.SMEM)
VMEM = pl.BlockSpec(memory_space=pltpu.VMEM)
PARAMS = pltpu.CompilerParams(vmem_limit_bytes=56 * 2**20)


def with_halo(x, sides, width):
    for axis, dim in sides:
        count, length = (lax.axis_size(axis), x.shape[dim])
        up = [(i, (i + 1) % count) for i in range(count)]
        down = [(j, i) for i, j in up]
        last = lax.slice_in_dim(x, length - width, length, axis=dim)
        initial = lax.slice_in_dim(x, 0, width, axis=dim)
        before = lax.ppermute(last, axis, up)
        after = lax.ppermute(initial, axis, down)
        x = jnp.concatenate([before, x, after], axis=dim)
    return x


def raised(block_rows, turned):
    upper_row = block_rows[..., -1:, :]
    upper_row = jnp.where(turned, jnp.flip(upper_row, -1), upper_row)
    return jnp.concatenate([block_rows[..., :-1, :], upper_row], axis=-2)


def settled(block_rows, padded, turned):
    lower_rim = padded[..., :1, :]
    upper_rim = padded[..., -1:, :]
    upper_rim = jnp.where(turned, jnp.flip(upper_rim, -1), upper_rim)
    southern = jnp.concatenate([lower_rim, block_rows[..., :-1, :]], axis=-2)
    northern = jnp.concatenate([block_rows[..., 1:, :], upper_rim], axis=-2)
    return (southern, northern)


def surface_apply(values_in, damping, turned):
    padded = with_halo(raised(values_in, turned), (("face", 0),), 1)
    southern, northern = settled(values_in, padded, turned)
    return (4.0 + damping) * values_in - (
        southern + northern + jnp.roll(values_in, 1, -1) + jnp.roll(values_in, -1, -1)
    )


def stepwise_surface(eta_adjoint, surface_damping, turned):
    surface = jnp.zeros_like(eta_adjoint)
    residual = eta_adjoint
    direction = eta_adjoint
    norm_now = lax.psum(jnp.sum(residual * residual), "face")
    for step in range(ITERS):
        applied = surface_apply(direction, surface_damping, turned)
        step_size = norm_now / lax.psum(jnp.sum(direction * applied), "face")
        surface = surface + step_size * direction
        residual = residual - step_size * applied
        norm_next = lax.psum(jnp.sum(residual * residual), "face")
        direction = residual + norm_next / norm_now * direction
        norm_now = norm_next
    return surface


def flip_lanes(rows):
    width = rows.shape[1]
    back = LANES - 1 - lax.broadcasted_iota(jnp.int32, (SUBLANES, LANES), 1)
    tiles = []
    for start in range(width - LANES, -1, -LANES):
        tiles.append(
            jnp.take_along_axis(
                rows[:, start : start + LANES], back, axis=1, mode="promise_in_bounds"
            )
        )
    return jnp.concatenate(tiles, axis=1)


def flip_rows_in_place(ref):
    def body(i, _):
        at = pl.ds(pl.multiple_of(i * SUBLANES, SUBLANES), SUBLANES)
        ref[at, :] = flip_lanes(ref[at, :])
        return 0

    lax.fori_loop(0, ref.shape[0] // SUBLANES, body, 0)


def outer_kernel(seam, eta, damping, up, down):
    half = SUBLANES // 2
    down[:half, :] = eta[:half, :]
    down[half:, :] = damping[:half, :]
    up[:half, :] = eta[half:, :]
    up[half:, :] = damping[half:, :]

    @pl.when(seam[0] == 1)
    def _():
        up[...] = flip_lanes(up[...])


def basis_kernel(seam, eta, damping, below, above, basis, sums):
    half = SUBLANES // 2
    rows = 2 * SUBLANES
    beyond = above[...]
    beyond = jnp.where(seam[0] == 1, flip_lanes(beyond), beyond)
    width = beyond.shape[1]
    v = jnp.concatenate([below[:half, :], eta[...], beyond[:half, :]], axis=0)
    d = jnp.concatenate([below[half:, :], damping[...], beyond[half:, :]], axis=0)
    d = (d + (4.0 - MIDDLE)) * (1.0 / MIDDLE)
    vectors = [v]
    for j in range(ITERS):
        now = vectors[-1]
        near = (
            pltpu.roll(now, 1, 0)
            + pltpu.roll(now, rows - 1, 0)
            + pltpu.roll(now, 1, 1)
            + pltpu.roll(now, width - 1, 1)
        )
        image = d * now - near * (1.0 / MIDDLE)
        vectors.append(image if j == 0 else 2.0 * image - vectors[-2])
    for j in range(ITERS):
        basis[j] = vectors[j]
    row = lax.broadcasted_iota(jnp.int32, (rows, LANES), 0)
    own = (row >= half) & (row < half + SUBLANES)
    for j in range(2 * ITERS):
        product = vectors[j // 2] * vectors[j // 2 + j % 2]
        total = product[:, :LANES]
        for start in range(LANES, width, LANES):
            total = total + product[:, start : start + LANES]
        sums[j : j + 1, :] = jnp.sum(jnp.where(own, total, 0.0), axis=0, keepdims=True)


def coefficients(moments):
    def dot(a, b):
        total = None
        for i, x in enumerate(a):
            for j, y in enumerate(b):
                term = x * y * (moments[i + j] + moments[abs(i - j)])
                total = term if total is None else total + term
        return 0.5 * total

    def image(p):
        q = [MIDDLE * x for x in p] + [jnp.zeros_like(p[0])]
        for i, x in enumerate(p):
            if i == 0:
                q[1] = q[1] + MIDDLE * x
            else:
                q[i + 1] = q[i + 1] + (0.5 * MIDDLE) * x
                q[i - 1] = q[i - 1] + (0.5 * MIDDLE) * x
        return q

    def size(p):
        return functools.reduce(lambda a, b: a + b, [jnp.abs(x) for x in p])

    def plus(a, b):
        return [x + y for x, y in zip(a, b)] + list(a[len(b) :]) + list(b[len(a) :])

    norm_first = moments[0]
    p = [jnp.ones_like(norm_first)]
    r = p
    norm_now = norm_first
    s = []
    sound = norm_first > 0.0
    for step in range(ITERS):
        q = image(p)
        curve = dot(p, q)
        sound = sound & (curve * LOSS >= size(p) * size(q) * norm_first)
        rate = norm_now / curve
        s = plus(s, [rate * x for x in p])
        if step < ITERS - 1:
            r = plus(r, [-rate * x for x in q])
            norm_next = dot(r, r)
            sound = sound & (norm_next * LOSS >= size(r) * size(r) * norm_first)
            ratio = norm_next / norm_now
            p = plus(r, [ratio * x for x in p])
            norm_now = norm_next
    return s, sound


def surface_kernel(sums, basis, surface, rims, sound):
    half = SUBLANES // 2
    sets = sums.shape[0]
    total = sums[0]
    for i in range(1, sets):
        total = total + sums[i]
    total = jnp.sum(total, axis=1, keepdims=True)
    raw = [total[j : j + 1, :] for j in range(2 * ITERS)]
    moments = raw[:2]
    for j in range(2, 2 * ITERS):
        moments.append(2.0 * raw[j] - raw[j % 2])
    s, good = coefficients(moments)
    value = s[0] * basis[0]
    for j in range(1, ITERS):
        value = value + s[j] * basis[j]
    surface[...] = value[half : half + SUBLANES, :]
    rims[0:1, :] = value[half - 1 : half, :]
    rims[1:2, :] = value[half + SUBLANES : half + SUBLANES + 1, :]
    sound[...] = jnp.broadcast_to(jnp.where(good, 1, 0), sound.shape)


def column_kernel(
    seam, thickness, tracer, mixing, velocity_y, wet, solved, up, down, ratio_at
):
    levels = tracer.shape[1]
    depth = wet[...]
    zero = jnp.zeros(depth.shape, jnp.float32)

    def forward(k, carry):
        c_before, g_before, y0, y1, y2 = carry
        th = thickness[k]
        c = jnp.where(k + 1 < depth, mixing[jnp.minimum(k, levels - 2)], 0.0)
        inverse = 1.0 / (th + c + c_before * (1.0 - g_before))
        g = c * inverse
        y0 = (tracer[0, k] + c_before * y0) * inverse
        y1 = (tracer[1, k] + c_before * y1) * inverse
        y2 = (jnp.where(k < depth, th, 0.0) + c_before * y2) * inverse
        ratio_at[k] = g
        solved[0, k] = y0
        solved[1, k] = y1
        solved[2, k] = y2
        return c, g, y0, y1, y2

    lax.fori_loop(0, levels, forward, (zero,) * 5, unroll=2)

    def backward(i, carry):
        k = levels - 1 - i
        th = thickness[k]
        g = ratio_at[k]
        flow = advection * velocity_y[k]
        upward = diffusion - flow
        downward = diffusion + flow
        after = []
        for t in range(3):
            u = solved[t, k] + g * carry[t]
            x = th * u
            solved[t, k] = x
            up[pl.ds(t * levels + k, 1), :] = (x * upward)[SUBLANES - 1 :, :]
            down[pl.ds(t * levels + k, 1), :] = (x * downward)[:1, :]
            after.append(u)
        return tuple(after)

    lax.fori_loop(0, levels, backward, (zero,) * 3, unroll=2)

    @pl.when(seam[0] == 1)
    def _():
        flip_rows_in_place(up)


def transport_kernel(
    seam, solved, velocity_x, velocity_y, wet, surface, rims, below, above, result, beyond
):
    levels_here = velocity_x.shape[0]
    levels = levels_here * pl.num_programs(0)
    first = pl.program_id(0) * levels_here
    width = wet.shape[1]

    @pl.when(pl.program_id(0) == 0)
    def _():
        beyond[...] = above[...]

        @pl.when(seam[0] == 1)
        def _():
            flip_rows_in_place(beyond)

    depth = wet[...]
    s = surface[...]
    south_s = rims[0:1, :]
    north_s = rims[1:2, :]
    row = lax.broadcasted_iota(jnp.int32, depth.shape, 0)

    def level(i, _):
        k = first + i
        flow_x = advection * velocity_x[i]
        flow_y = advection * velocity_y[i]
        is_wet = k < depth
        for t in range(2):
            x = solved[t, i]
            from_south = below[pl.ds(t * levels + k, 1), :]
            from_north = beyond[pl.ds(t * levels + k, 1), :]
            if t == 0:
                x = x + s * solved[2, i]
                from_south = from_south + south_s * below[pl.ds(2 * levels + k, 1), :]
                from_north = from_north + north_s * beyond[pl.ds(2 * levels + k, 1), :]
            spread = diffusion * x
            push_x = flow_x * x
            push_y = flow_y * x
            eastern = pltpu.roll(spread + push_x, width - 1, 1)
            western = pltpu.roll(spread - push_x, 1, 1)
            northern = jnp.where(
                row == SUBLANES - 1, from_north, pltpu.roll(spread + push_y, SUBLANES - 1, 0)
            )
            southern = jnp.where(row == 0, from_south, pltpu.roll(spread - push_y, 1, 0))
            value = (1.0 - 4.0 * diffusion) * x + ((eastern + western) + (northern + southern))
            result[t, i] = jnp.where(is_wet, value, 0.0)
        return 0

    lax.fori_loop(0, levels_here, level, 0, unroll=True)


def gathered_sums(sums, axis):
    count = lax.axis_size(axis)
    if count & (count - 1):
        return lax.psum(sums, axis)[None]
    stride = 1
    parts = [sums]
    while stride < count:
        total = parts[0] if len(parts) == 1 else (parts[0] + parts[2]) + (parts[1] + parts[3])
        reach = min(4, count // stride)
        parts = [total]
        for step in range(1, reach):
            pairs = []
            for i in range(count):
                place = i // stride % reach
                pairs.append((i, i + ((place + step) % reach - place) * stride))
            parts.append(lax.ppermute(total, axis, pairs))
        stride *= reach
    return jnp.stack(parts)


def shards(
    tracer_adjoint,
    eta_adjoint,
    velocity_x,
    velocity_y,
    mixing,
    thickness,
    surface_damping,
    wet_levels,
    seam_codes,
):
    tracers, levels, rows, width = tracer_adjoint.shape
    f32 = jnp.float32
    count = lax.axis_size("face")
    upward = [(i, (i + 1) % count) for i in range(count)]
    downward = [(j, i) for i, j in upward]
    tile = jax.ShapeDtypeStruct((rows, width), f32)
    ext = jax.ShapeDtypeStruct((ITERS, 2 * rows, width), f32)
    lines = -(-3 * levels // SUBLANES) * SUBLANES
    line = jax.ShapeDtypeStruct((lines, width), f32)

    up, down = pl.pallas_call(
        outer_kernel,
        out_shape=(tile, tile),
        in_specs=[SMEM, VMEM, VMEM],
        out_specs=(VMEM, VMEM),
        name="outer_rows",
    )(seam_codes, eta_adjoint, surface_damping)
    below = lax.ppermute(up, "face", upward)
    above = lax.ppermute(down, "face", downward)

    basis, sums = pl.pallas_call(
        basis_kernel,
        out_shape=(ext, jax.ShapeDtypeStruct((SUBLANES, LANES), f32)),
        in_specs=[SMEM] + [VMEM] * 4,
        out_specs=(VMEM, VMEM),
        compiler_params=PARAMS,
        name="surface_basis",
    )(seam_codes, eta_adjoint, surface_damping, below, above)
    parts = gathered_sums(sums, "face")

    solved, up, down = pl.pallas_call(
        column_kernel,
        out_shape=(jax.ShapeDtypeStruct((3, levels, rows, width), f32), line, line),
        in_specs=[SMEM, SMEM] + [VMEM] * 4,
        out_specs=(VMEM, VMEM, VMEM),
        scratch_shapes=[pltpu.VMEM((levels, rows, width), f32)],
        compiler_params=PARAMS,
        cost_estimate=pl.CostEstimate(flops=40000000, bytes_accessed=13000000, transcendentals=0),
        name="columns",
    )(seam_codes, thickness, tracer_adjoint, mixing, velocity_y, wet_levels)
    below = lax.ppermute(up, "face", upward)
    above = lax.ppermute(down, "face", downward)

    surface, rims, sound = pl.pallas_call(
        surface_kernel,
        out_shape=(tile, tile, jax.ShapeDtypeStruct((SUBLANES, LANES), jnp.int32)),
        in_specs=[VMEM, VMEM],
        out_specs=(VMEM, VMEM, VMEM),
        compiler_params=PARAMS,
        name="surface",
    )(parts, basis)

    def transport(surface, rims, solved, below, above):
        chunk = 5 if levels % 5 == 0 else 1
        whole = pl.BlockSpec((rows, width), lambda k: (0, 0))
        many = pl.BlockSpec((lines, width), lambda k: (0, 0))
        field = pl.BlockSpec((chunk, rows, width), lambda k: (k, 0, 0))
        return pl.pallas_call(
            transport_kernel,
            out_shape=jax.ShapeDtypeStruct((tracers, levels, rows, width), f32),
            grid=(levels // chunk,),
            in_specs=[
                SMEM,
                pl.BlockSpec((3, chunk, rows, width), lambda k: (0, k, 0, 0)),
                field,
                field,
                whole,
                whole,
                whole,
                many,
                many,
            ],
            out_specs=pl.BlockSpec((tracers, chunk, rows, width), lambda k: (0, k, 0, 0)),
            scratch_shapes=[pltpu.VMEM((lines, width), f32)],
            compiler_params=PARAMS,
            name="transport",
        )(seam_codes, solved, velocity_x, velocity_y, wet_levels, surface, rims, below, above)

    def by_moments(surface, rims, solved, below, above):
        return transport(surface, rims, solved, below, above), surface

    def by_steps(surface, rims, solved, below, above):
        surface = stepwise_surface(eta_adjoint, surface_damping, seam_codes[0] == 1)
        top, bottom = surface[-1:], surface[:1]
        top = jnp.where(seam_codes[0] == 1, jnp.flip(top, -1), top)
        south = lax.ppermute(top, "face", upward)
        north = lax.ppermute(bottom, "face", downward)
        north = jnp.where(seam_codes[0] == 1, jnp.flip(north, -1), north)
        rims = jnp.concatenate([south, north, surface[2:]], axis=0)
        return transport(surface, rims, solved, below, above), surface

    return lax.cond(
        sound[0, 0] == 1, by_moments, by_steps, surface, rims, solved, below, above
    )


def solution(mesh):
    placed = (
        P(None, None, "face", "ens"),
        P("face", "ens"),
        P(None, "face", "ens"),
        P(None, "face", "ens"),
        P(None, "face", "ens"),
        P(),
        P("face", None),
        P("face", None),
        P("face"),
    )
    return jax.shard_map(
        shards,
        mesh=mesh,
        in_specs=placed,
        out_specs=(P(None, None, "face", "ens"), P("face", "ens")),
        check_vma=False,
    )
```

time: 537 us -> 63.1 us (0.12); the launches traced: 530 us -> 63.3 us
  blocking collectives: 220 us -> 0 us
  other arithmetic: 216 us -> 1.29 us
  local copies, waits for them, and re-layouts: 58.6 us -> 4.2 us
  Pallas kernels: 0 us -> 24.8 us
  between operations: 12.8 us -> 2.07 us
  starting transfers between devices: 11.5 us -> 20.5 us
    psum x7 -> x0, blocking collectives: 220 us -> none  [the longest x4 125 us: squares(): return lax.psum(jnp.sum(residual * residual), 'face')]
    mul x35 -> x0, other arithmetic: 136 us -> none  [the longest x31 120 us: transposed_solve(): solved.insert(0, scaled[level] - ratios[level] * solved[0])]
    sub x1 -> x0, other arithmetic: 32.8 us -> none  [transposed_solve(): pivots = pivots - below_term * ratios[level - 1]]
    rev x10 -> x0, local copies, waits for them, and re-layouts: 30 us -> none  [the longest x5 16.9 us: settled(): upper_rim = jnp.where(turned, jnp.flip(upper_rim, -1), upper_rim)]
    pallas_call x0 -> x5, Pallas kernels: none -> 24.8 us  [the longest x1 10.3 us: shards(): pl.pallas_call(column_kernel, out_shape=(jax.ShapeDtypeStruct((3, levels,...]
    slice x21 -> x1, local copies, waits for them, and re-layouts: 25.3 us -> 1.25 us  [shards(): sound[0, 0] == 1]
    reduce_sum x7 -> x0, other arithmetic: 10.9 us -> none  [the longest x4 7.43 us: shards(): step_size = norm_now / lax.psum(jnp.sum(direction * applied), 'face')]
    ppermute x10, starting transfers between devices: 11.5 us -> 20.5 us  [the longest x6 10.6 us: gathered_sums(): parts.append(lax.ppermute(total, axis, pairs))]
  transfers between devices with their start and end apart: 10 -> 10, of which waited for: 6 -> 6; matrix products, arithmetic and copies ran while one was open for 34% -> 4% of each run, Pallas kernels for 0% -> 7%
where the time goes in v1:
time: 63.1 us; the launch traced here: 63.3 us
  Pallas kernels  24.8 us (39%)
  starting transfers between devices  20.5 us (32%)
  waiting for transfers between devices  10.4 us (16%)
  local copies, waits for them, and re-layouts  4.2 us (7%)
  between operations  2.07 us (3%)
  other arithmetic  1.29 us (2%)
    ppermute x6, starting transfers between devices, gathered_sums(): parts.append(lax.ppermute(total, axis, pairs))  10.6 us
    pallas_call x1, Pallas kernels, shards(): pl.pallas_call(column_kernel, out_shape=(jax.ShapeDtypeStruct((3, levels,...  10.3 us
    pallas_call x1, Pallas kernels, transport(): pl.pallas_call(transport_kernel, out_shape=jax.ShapeDtypeStruct((tracers,...  10.1 us
    ppermute x2, starting transfers between devices, shards(): above = lax.ppermute(down, 'face', downward)  9.43 us
    ppermute x6, waiting for transfers between devices, gathered_sums(): parts.append(lax.ppermute(total, axis, pairs))  7 us
    ppermute x2, waiting for transfers between devices, shards(): below = lax.ppermute(up, 'face', upward)  3.42 us
    unnamed x16, local copies, waits for them, and re-layouts  2.95 us
    pallas_call x1, Pallas kernels, shards(): pl.pallas_call(surface_kernel, out_shape=(tile, tile, jax.ShapeDtypeStruc...  1.87 us
  transfers between devices with their start and end apart: 10, of which 6 were waited for; matrix products, arithmetic and copies ran while one was open for 4% of the time, Pallas kernels for 7%

profile of v1, /device:TPU:0, one launch (start us, length us, event | category | flops | bytes accessed | tf_op | source)
XLA Modules:
  0.0 63.3 jit_solution(10541577350534201569)
XLA Ops:
  1.3 0.0 copy-start.2
  1.3 0.0 copy-start.4
  1.3 0.0 copy-start
  1.3 0.0 copy-start.1
  1.3 0.0 copy-start.5
  1.3 10.3 %columns.1 = (f32[3,50,8,1024]{3,2,1,0:T(8,128)}, f32[152,1024]{1,0:T(8,128)}, f32[152,1024]{1,0:T(8,128)}) custom-call(s32[1]{0:T(128)S(6)} %copy.17.seam, f32[50]{0:T(128)} %thickness.1, f32[2,50,8,1024]{3,2,1,0:T(8,128)} %tracer.1, f32[49,8,1024]{2,1,0:T(8,128)} %mixing.1, f32[50,8,1024]{2,1,0:T(8,128)} %velocity_y.1, s32[8,1024]{1,0:T(8,128)} %wet.1), custom_call_target="tpu_custom_call" | custom-call | flops 40000000 | bytes 13000000 | tf_op jit(solution)/shard_map/columns/pallas_call | solution.py:369
  11.6 0.5 collective-permute-start.18
  12.1 5.0 %collective-permute-start.19 = (f32[152,1024]{1,0:T(8,128)}, f32[152,1024]{1,0:T(8,128)}, u32[]{:S(2)}, u32[]{:S(2)}) collective-permute-start(f32[152,1024]{1,0:T(8,128)} %get-tuple-element.73), channel_id=1, source_target_pairs={{1,0},{2,1},{3,2},{4,3},{5,4},{6,5},{7,6},{8,7},{9,8},{10,9},{11,1... | collective-permute-start | bytes 1867784 | tf_op jit(solution)/shard_map/ppermute | solution.py:380
  17.1 0.0 copy-done.2
  17.1 0.0 copy-done.4
  17.1 0.7 %outer_rows.1 = (f32[8,1024]{1,0:T(8,128)}, f32[8,1024]{1,0:T(8,128)}) custom-call(s32[1]{0:T(128)S(6)} %copy.17.seam, f32[8,1024]{1,0:T(8,128)S(1)} %copy-done.2, f32[8,1024]{1,0:T(8,128)S(1)} %copy-done.4), custom_call_target="tpu_custom_call" | custom-call | tf_op jit(solution)/shard_map/outer_rows/pallas_call | solution.py:349
  17.8 0.0 collective-permute-start.10
  17.8 4.4 %collective-permute-start.11 = (f32[8,1024]{1,0:T(8,128)}, f32[8,1024]{1,0:T(8,128)S(1)}, u32[]{:S(2)}, u32[]{:S(2)}) collective-permute-start(f32[8,1024]{1,0:T(8,128)} %get-tuple-element.67), channel_id=1, source_target_pairs={{1,0},{2,1},{3,2},{4,3},{5,4},{6,5},{7,6},{8,7},{9,8},{10,9},{11,1... | collective-permute-start | bytes 98312 | tf_op jit(solution)/shard_map/ppermute | solution.py:357
  22.2 3.4 %collective-permute-done.10.below = f32[8,1024]{1,0:T(8,128)S(1)} collective-permute-done((f32[8,1024]{1,0:T(8,128)}, f32[8,1024]{1,0:T(8,128)S(1)}, u32[]{:S(2)}, u32[]{:S(2)}) %collective-permute-start.10) | collective-permute-done | bytes 32800 | tf_op jit(solution)/shard_map/ppermute | solution.py:356
  25.7 0.0 copy-start.6
  25.7 0.0 collective-permute-done.11.above
  25.7 0.6 copy-done.6
  26.3 0.0 copy-start.7
  26.3 0.6 copy-done.7
  26.9 1.8 %surface_basis.1 = (f32[4,16,1024]{2,1,0:T(8,128)}, f32[8,128]{1,0:T(8,128)}) custom-call(s32[1]{0:T(128)S(6)} %copy.17.seam, f32[8,1024]{1,0:T(8,128)S(1)} %copy-done.2, f32[8,1024]{1,0:T(8,128)S(1)} %copy-done.4, f32[8,1024]{1,0:T(8,128)} %copy-done.6, f32[8,1024]{1,0:T(8,128)} %copy-done.7), custom_call_target="tpu_custom_call" | custom-call | tf_op jit(solution)/shard_map/surface_basis/pallas_call | solution.py:359
  28.7 0.0 collective-permute-start.14
  28.7 4.2 %collective-permute-start.13 = (f32[8,128]{1,0:T(8,128)}, f32[8,128]{1,0:T(8,128)S(1)}, u32[]{:S(2)}, u32[]{:S(2)}) collective-permute-start(f32[8,128]{1,0:T(8,128)} %get-tuple-element.68), channel_id=1, source_target_pairs={{0,1},{1,2},{2,3},{3,0},{4,5},{5,6},{6,7},{7,4},{8,9},{9,10},{10,1... | collective-permute-start | bytes 12296 | tf_op jit(solution)/shard_map/ppermute | solution.py:323
  32.9 1.7 %collective-permute-start.12 = (f32[8,128]{1,0:T(8,128)}, f32[8,128]{1,0:T(8,128)S(1)}, u32[]{:S(2)}, u32[]{:S(2)}) collective-permute-start(f32[8,128]{1,0:T(8,128)} %get-tuple-element.68), channel_id=1, source_target_pairs={{0,2},{1,3},{2,0},{3,1},{4,6},{5,7},{6,4},{7,5},{8,10},{9,11},{10,... | collective-permute-start | bytes 12296 | tf_op jit(solution)/shard_map/ppermute | solution.py:323
  34.6 0.0 collective-permute-done.14
  34.6 0.4 collective-permute-done.13
  35.0 1.7 %collective-permute-done.12 = f32[8,128]{1,0:T(8,128)S(1)} collective-permute-done((f32[8,128]{1,0:T(8,128)}, f32[8,128]{1,0:T(8,128)S(1)}, u32[]{:S(2)}, u32[]{:S(2)}) %collective-permute-start.12) | collective-permute-done | bytes 4128 | tf_op jit(solution)/shard_map/ppermute | solution.py:323
  36.7 0.7 %add_add_fusion = f32[8,128]{1,0:T(8,128)S(1)} fusion(f32[8,128]{1,0:T(8,128)S(1)} %collective-permute-done.13, f32[8,128]{1,0:T(8,128)S(1)} %collective-permute-done.14, f32[8,128]{1,0:T(8,128)} %get-tuple-element.68, f32[8,128]{1,0:T(8,128)S(1)} %collective-permute-done.12), kind=kLoop, calls=%fused_computation.44 | loop fusion | flops 3072 | bytes 20480 | tf_op jit(solution)/shard_map/add | solution.py:315
  37.4 4.2 %collective-permute-start.17 = (f32[8,128]{1,0:T(8,128)S(1)}, f32[8,128]{1,0:T(8,128)S(1)}, u32[]{:S(2)}, u32[]{:S(2)}) collective-permute-start(f32[8,128]{1,0:T(8,128)S(1)} %add_add_fusion), channel_id=1, source_target_pairs={{0,12},{1,13},{2,14},{3,15},{4,0},{5,1},{6,2},{7,3},{8,4},{9,5},{1... | collective-permute-start | bytes 12296 | tf_op jit(solution)/shard_map/ppermute | solution.py:323
  41.6 0.0 collective-permute-start.16
  41.6 0.6 collective-permute-start.15
  42.2 0.8 %collective-permute-done.17 = f32[8,128]{1,0:T(8,128)S(1)} collective-permute-done((f32[8,128]{1,0:T(8,128)S(1)}, f32[8,128]{1,0:T(8,128)S(1)}, u32[]{:S(2)}, u32[]{:S(2)}) %collective-permute-start.17) | collective-permute-done | bytes 4128 | tf_op jit(solution)/shard_map/ppermute | solution.py:323
  42.9 3.2 %collective-permute-done.16 = f32[8,128]{1,0:T(8,128)S(1)} collective-permute-done((f32[8,128]{1,0:T(8,128)S(1)}, f32[8,128]{1,0:T(8,128)S(1)}, u32[]{:S(2)}, u32[]{:S(2)}) %collective-permute-start.16) | collective-permute-done | bytes 4128 | tf_op jit(solution)/shard_map/ppermute | solution.py:323
  46.1 0.9 %collective-permute-done.15 = f32[8,128]{1,0:T(8,128)S(1)} collective-permute-done((f32[8,128]{1,0:T(8,128)S(1)}, f32[8,128]{1,0:T(8,128)S(1)}, u32[]{:S(2)}, u32[]{:S(2)}) %collective-permute-start.15) | collective-permute-done | bytes 4128 | tf_op jit(solution)/shard_map/ppermute | solution.py:323
  47.0 0.6 pad_maximum_fusion.1.sums
  47.6 1.9 %surface.1 = (f32[8,1024]{1,0:T(8,128)}, f32[8,1024]{1,0:T(8,128)}, s32[8,128]{1,0:T(8,128)}) custom-call(f32[4,8,128]{2,1,0:T(8,128)} %pad_maximum_fusion.1.sums, f32[4,16,1024]{2,1,0:T(8,128)} %get-tuple-element.69.basis), custom_call_target="tpu_custom_call" | custom-call | tf_op jit(solution)/shard_map/surface/pallas_call | solution.py:382
  49.5 1.3 %slice.120 = s32[1,1]{1,0:T(1,128)} slice(s32[8,128]{1,0:T(8,128)} %get-tuple-element.70), slice={[0:1], [0:1]} | slice | bytes 8 | tf_op jit(solution)/shard_map/slice | solution.py:431
  51.4 0.0 collective-permute-done.18
  51.4 0.0 collective-permute-done.19
  51.4 0.0 copy-done
  51.5 0.0 copy-done.1
  51.5 0.0 copy-done.5
  51.5 10.1 %conditional.1 = (f32[8,1024]{1,0:T(8,128)}, f32[2,50,8,1024]{3,2,1,0:T(8,128)S(1)}) conditional(s32[]{:T(128)} %bitcast.5, (f32[8,1024]{1,0:T(8,128)S(1)}, f32[8,1024]{1,0:T(8,128)S(1)}, s32[1]{0:T(128)}, f32[3,50,8,1024]{3,2,1,0:T(8,128)}, f32[50,8,1024]{2,1,0:T(8,128)S(1)}, /*index=5*/f32[50,8,1024]{2,1,0:T(8,128)S(1)}, ...), branch_computations={%region_0.17_spmd, %region_17.18_spmd} | conditional | flops 690184 | bytes 3187355 | solution.py:430
  51.5 10.1 %transport.3 = f32[2,50,8,1024]{3,2,1,0:T(8,128)S(1)} custom-call(s32[1]{0:T(128)} %get-tuple-element.45.seam, f32[3,50,8,1024]{3,2,1,0:T(8,128)} %get-tuple-element.46.solved, f32[50,8,1024]{2,1,0:T(8,128)S(1)} %get-tuple-element.47.velocity_x, f32[50,8,1024]{2,1,0:T(8,128)S(1)} %get-tuple-element.48.velocity_y, s32[8,1024]{1,0:T(8,128)S(1)} %get-tuple-element.49.wet, ...), custom_call_target="tpu_custom_call" | custom-call | tf_op jit(solution)/shard_map/cond/branch_1_fun/transport/pallas_call | solution.py:396
  61.6 0.0 copy-start.3
  61.6 1.7 %copy-done.3 = f32[2,50,8,1024]{3,2,1,0:T(8,128)} copy-done((f32[2,50,8,1024]{3,2,1,0:T(8,128)}, f32[2,50,8,1024]{3,2,1,0:T(8,128)S(1)}, u32[]{:S(2)}) %copy-start.3) | copy-done | bytes 3276824
Async XLA Ops:
  1.3 15.8 %copy-start.2 = (f32[8,1024]{1,0:T(8,128)S(1)}, f32[8,1024]{1,0:T(8,128)}, u32[]{:S(2)}) copy-start(f32[8,1024]{1,0:T(8,128)} %eta.3) | copy-start | bytes 98308
  1.3 15.8 %copy-start.4 = (f32[8,1024]{1,0:T(8,128)S(1)}, f32[8,1024]{1,0:T(8,128)}, u32[]{:S(2)}) copy-start(f32[8,1024]{1,0:T(8,128)} %damping.3) | copy-start | bytes 98308
  1.3 50.1 %copy-start = (f32[50,8,1024]{2,1,0:T(8,128)S(1)}, f32[50,8,1024]{2,1,0:T(8,128)}, u32[]{:S(2)}) copy-start(f32[50,8,1024]{2,1,0:T(8,128)} %velocity_y.1) | copy-start | bytes 4915204
  1.3 50.1 %copy-start.1 = (f32[50,8,1024]{2,1,0:T(8,128)S(1)}, f32[50,8,1024]{2,1,0:T(8,128)}, u32[]{:S(2)}) copy-start(f32[50,8,1024]{2,1,0:T(8,128)} %param.13) | copy-start | bytes 4915204
  1.3 50.1 %copy-start.5 = (s32[8,1024]{1,0:T(8,128)S(1)}, s32[8,1024]{1,0:T(8,128)}, u32[]{:S(2)}) copy-start(s32[8,1024]{1,0:T(8,128)} %wet.1) | copy-start | bytes 98308
  11.6 39.8 %collective-permute-start.18 = (f32[152,1024]{1,0:T(8,128)}, f32[152,1024]{1,0:T(8,128)}, u32[]{:S(2)}, u32[]{:S(2)}) collective-permute-start(f32[152,1024]{1,0:T(8,128)} %get-tuple-element.72), channel_id=1, source_target_pairs={{0,1},{1,2},{2,3},{3,4},{4,5},{5,6},{6,7},{7,8},{8,9},{9,10},{10,1... | collective-permute-start | bytes 1867784 | tf_op jit(solution)/shard_map/ppermute | solution.py:379
  12.1 39.4 %collective-permute-start.19 = (f32[152,1024]{1,0:T(8,128)}, f32[152,1024]{1,0:T(8,128)}, u32[]{:S(2)}, u32[]{:S(2)}) collective-permute-start(f32[152,1024]{1,0:T(8,128)} %get-tuple-element.73), channel_id=1, source_target_pairs={{1,0},{2,1},{3,2},{4,3},{5,4},{6,5},{7,6},{8,7},{9,8},{10,9},{11,1... | collective-permute-start | bytes 1867784 | tf_op jit(solution)/shard_map/ppermute | solution.py:380
  17.8 7.9 %collective-permute-start.10 = (f32[8,1024]{1,0:T(8,128)}, f32[8,1024]{1,0:T(8,128)S(1)}, u32[]{:S(2)}, u32[]{:S(2)}) collective-permute-start(f32[8,1024]{1,0:T(8,128)} %get-tuple-element.66), channel_id=1, source_target_pairs={{0,1},{1,2},{2,3},{3,4},{4,5},{5,6},{6,7},{7,8},{8,9},{9,10},{10,1... | collective-permute-start | bytes 98312 | tf_op jit(solution)/shard_map/ppermute | solution.py:356
  17.8 7.9 %collective-permute-start.11 = (f32[8,1024]{1,0:T(8,128)}, f32[8,1024]{1,0:T(8,128)S(1)}, u32[]{:S(2)}, u32[]{:S(2)}) collective-permute-start(f32[8,1024]{1,0:T(8,128)} %get-tuple-element.67), channel_id=1, source_target_pairs={{1,0},{2,1},{3,2},{4,3},{5,4},{6,5},{7,6},{8,7},{9,8},{10,9},{11,1... | collective-permute-start | bytes 98312 | tf_op jit(solution)/shard_map/ppermute | solution.py:357
  25.7 0.6 copy-start.6
  26.3 0.6 copy-start.7
  28.7 5.8 %collective-permute-start.14 = (f32[8,128]{1,0:T(8,128)}, f32[8,128]{1,0:T(8,128)S(1)}, u32[]{:S(2)}, u32[]{:S(2)}) collective-permute-start(f32[8,128]{1,0:T(8,128)} %get-tuple-element.68), channel_id=1, source_target_pairs={{0,3},{1,0},{2,1},{3,2},{4,7},{5,4},{6,5},{7,6},{8,11},{9,8},{10,9... | collective-permute-start | bytes 12296 | tf_op jit(solution)/shard_map/ppermute | solution.py:323
  28.7 6.3 %collective-permute-start.13 = (f32[8,128]{1,0:T(8,128)}, f32[8,128]{1,0:T(8,128)S(1)}, u32[]{:S(2)}, u32[]{:S(2)}) collective-permute-start(f32[8,128]{1,0:T(8,128)} %get-tuple-element.68), channel_id=1, source_target_pairs={{0,1},{1,2},{2,3},{3,0},{4,5},{5,6},{6,7},{7,4},{8,9},{9,10},{10,1... | collective-permute-start | bytes 12296 | tf_op jit(solution)/shard_map/ppermute | solution.py:323
  32.9 3.8 %collective-permute-start.12 = (f32[8,128]{1,0:T(8,128)}, f32[8,128]{1,0:T(8,128)S(1)}, u32[]{:S(2)}, u32[]{:S(2)}) collective-permute-start(f32[8,128]{1,0:T(8,128)} %get-tuple-element.68), channel_id=1, source_target_pairs={{0,2},{1,3},{2,0},{3,1},{4,6},{5,7},{6,4},{7,5},{8,10},{9,11},{10,... | collective-permute-start | bytes 12296 | tf_op jit(solution)/shard_map/ppermute | solution.py:323
  37.4 5.5 %collective-permute-start.17 = (f32[8,128]{1,0:T(8,128)S(1)}, f32[8,128]{1,0:T(8,128)S(1)}, u32[]{:S(2)}, u32[]{:S(2)}) collective-permute-start(f32[8,128]{1,0:T(8,128)S(1)} %add_add_fusion), channel_id=1, source_target_pairs={{0,12},{1,13},{2,14},{3,15},{4,0},{5,1},{6,2},{7,3},{8,4},{9,5},{1... | collective-permute-start | bytes 12296 | tf_op jit(solution)/shard_map/ppermute | solution.py:323
  41.6 4.5 %collective-permute-start.16 = (f32[8,128]{1,0:T(8,128)S(1)}, f32[8,128]{1,0:T(8,128)S(1)}, u32[]{:S(2)}, u32[]{:S(2)}) collective-permute-start(f32[8,128]{1,0:T(8,128)S(1)} %add_add_fusion), channel_id=1, source_target_pairs={{0,8},{1,9},{2,10},{3,11},{4,12},{5,13},{6,14},{7,15},{8,0},{9,1},... | collective-permute-start | bytes 12296 | tf_op jit(solution)/shard_map/ppermute | solution.py:323
  41.6 5.4 %collective-permute-start.15 = (f32[8,128]{1,0:T(8,128)S(1)}, f32[8,128]{1,0:T(8,128)S(1)}, u32[]{:S(2)}, u32[]{:S(2)}) collective-permute-start(f32[8,128]{1,0:T(8,128)S(1)} %add_add_fusion), channel_id=1, source_target_pairs={{0,4},{1,5},{2,6},{3,7},{4,8},{5,9},{6,10},{7,11},{8,12},{9,13},{1... | collective-permute-start | bytes 12296 | tf_op jit(solution)/shard_map/ppermute | solution.py:323
  61.6 1.7 %copy-start.3 = (f32[2,50,8,1024]{3,2,1,0:T(8,128)}, f32[2,50,8,1024]{3,2,1,0:T(8,128)S(1)}, u32[]{:S(2)}) copy-start(f32[2,50,8,1024]{3,2,1,0:T(8,128)S(1)} %get-tuple-element.76) | copy-start | bytes 9830404

commit v2 on v1

v2 whole, which is shorter than its diff:
```python
import jax
import jax.numpy as jnp
from jax import lax
from jax.experimental import pallas as pl
from jax.experimental.pallas import tpu as pltpu
from jax.sharding import PartitionSpec as P

ITERS = 4
LANES = 128
SUBLANES = 8
diffusion = 0.1
advection = 0.5

SMEM = pl.BlockSpec(memory_space=pltpu.SMEM)
VMEM = pl.BlockSpec(memory_space=pltpu.VMEM)
PARAMS = pltpu.CompilerParams(vmem_limit_bytes=56 * 2**20)


def flip_lanes(rows):
    height, width = rows.shape
    if height > SUBLANES:
        parts = [flip_lanes(rows[i : i + SUBLANES]) for i in range(0, height, SUBLANES)]
        return jnp.concatenate(parts, axis=0)
    back = LANES - 1 - lax.broadcasted_iota(jnp.int32, (SUBLANES, LANES), 1)
    tiles = []
    for start in range(width - LANES, -1, -LANES):
        tiles.append(
            jnp.take_along_axis(
                rows[:, start : start + LANES], back, axis=1, mode="promise_in_bounds"
            )
        )
    return jnp.concatenate(tiles, axis=1)


def flip_rows_in_place(ref):
    def body(i, _):
        at = pl.ds(pl.multiple_of(i * SUBLANES, SUBLANES), SUBLANES)
        ref[at, :] = flip_lanes(ref[at, :])
        return 0

    lax.fori_loop(0, ref.shape[0] // SUBLANES, body, 0)


def pack_kernel(seam, eta, damping, packed):
    rows, width = eta.shape
    packed[:rows, :width] = eta[...]
    packed[rows:, :width] = damping[...]
    code = seam[0].astype(jnp.float32)
    packed[:, width:] = jnp.full((2 * rows, LANES), code, jnp.float32)


def surface_kernel(place, packed, surface, rims, p_at, r_at, q_at, north_at, south_at):
    blocks, double, wide = packed.shape
    rows, width = double // 2, wide - LANES
    me = place[0]
    row = lax.broadcasted_iota(jnp.int32, (rows, width), 0)
    zero = jnp.zeros((rows, width), jnp.float32)
    turned = packed[:, 0, width : width + 1] > 0.5

    def whole(value):
        return jnp.sum(value, axis=(0, 1), keepdims=True)

    def start(b, total):
        value = packed[b, :rows, :width]
        r_at[b] = value
        return total + value * value

    norm_now = whole(lax.fori_loop(0, blocks, start, zero, unroll=2))
    ratio = None
    surface[...] = zero
    rims[...] = zero
    for step in range(ITERS):
        first = r_at[:, 0, :]
        last = r_at[:, rows - 1, :]
        if step:
            first = first + ratio * p_at[:, 0, :]
            last = last + ratio * p_at[:, rows - 1, :]
        after = pltpu.roll(first, blocks - 1, 0)
        north_at[...] = jnp.where(turned, flip_lanes(after), after)
        south_at[...] = pltpu.roll(jnp.where(turned, flip_lanes(last), last), 1, 0)

        def apply(b, total):
            p = r_at[b]
            if step:
                p = p + ratio * p_at[b]
            p_at[b] = p
            northern = jnp.where(
                row == rows - 1, north_at[pl.ds(b, 1), :], pltpu.roll(p, rows - 1, 0)
            )
            southern = jnp.where(row == 0, south_at[pl.ds(b, 1), :], pltpu.roll(p, 1, 0))
            near = (southern + northern) + (pltpu.roll(p, 1, 1) + pltpu.roll(p, width - 1, 1))
            q = (4.0 + packed[b, rows:, :width]) * p - near
            q_at[b] = q
            return total + p * q

        rate = norm_now / whole(lax.fori_loop(0, blocks, apply, zero, unroll=2))
        surface[...] += rate * p_at[me]
        rims[0:1, :] += rate * south_at[pl.ds(me, 1), :]
        rims[1:2, :] += rate * north_at[pl.ds(me, 1), :]
        if step < ITERS - 1:

            def reduce(b, total):
                r = r_at[b] - rate * q_at[b]
                r_at[b] = r
                return total + r * r

            norm_next = whole(lax.fori_loop(0, blocks, reduce, zero, unroll=2))
            ratio = norm_next / norm_now
            norm_now = norm_next


def column_kernel(
    seam, thickness, tracer, mixing, velocity_y, wet, solved, up, down, ratio_at
):
    levels = tracer.shape[1]
    depth = wet[...]
    zero = jnp.zeros(depth.shape, jnp.float32)

    def forward(k, carry):
        c_before, g_before, y0, y1, y2 = carry
        th = thickness[k]
        c = jnp.where(k + 1 < depth, mixing[jnp.minimum(k, levels - 2)], 0.0)
        inverse = 1.0 / (th + c + c_before * (1.0 - g_before))
        g = c * inverse
        y0 = (tracer[0, k] + c_before * y0) * inverse
        y1 = (tracer[1, k] + c_before * y1) * inverse
        y2 = (jnp.where(k < depth, th, 0.0) + c_before * y2) * inverse
        ratio_at[k] = g
        solved[0, k] = y0
        solved[1, k] = y1
        solved[2, k] = y2
        return c, g, y0, y1, y2

    lax.fori_loop(0, levels, forward, (zero,) * 5, unroll=2)

    def backward(i, carry):
        k = levels - 1 - i
        th = thickness[k]
        g = ratio_at[k]
        flow = advection * velocity_y[k]
        upward = diffusion - flow
        downward = diffusion + flow
        after = []
        for t in range(3):
            u = solved[t, k] + g * carry[t]
            x = th * u
            solved[t, k] = x
            up[pl.ds(t * levels + k, 1), :] = (x * upward)[SUBLANES - 1 :, :]
            down[pl.ds(t * levels + k, 1), :] = (x * downward)[:1, :]
            after.append(u)
        return tuple(after)

    lax.fori_loop(0, levels, backward, (zero,) * 3, unroll=2)

    @pl.when(seam[0] == 1)
    def _():
        flip_rows_in_place(up)


def transport_kernel(
    seam, solved, velocity_x, velocity_y, wet, surface, rims, below, above, result, beyond
):
    levels_here = velocity_x.shape[0]
    levels = levels_here * pl.num_programs(0)
    first = pl.program_id(0) * levels_here
    width = wet.shape[1]

    @pl.when(pl.program_id(0) == 0)
    def _():
        beyond[...] = above[...]

        @pl.when(seam[0] == 1)
        def _():
            flip_rows_in_place(beyond)

    depth = wet[...]
    s = surface[...]
    south_s = rims[0:1, :]
    north_s = rims[1:2, :]
    row = lax.broadcasted_iota(jnp.int32, depth.shape, 0)

    def level(i, _):
        k = first + i
        flow_x = advection * velocity_x[i]
        flow_y = advection * velocity_y[i]
        is_wet = k < depth
        for t in range(2):
            x = solved[t, i]
            from_south = below[pl.ds(t * levels + k, 1), :]
            from_north = beyond[pl.ds(t * levels + k, 1), :]
            if t == 0:
                x = x + s * solved[2, i]
                from_south = from_south + south_s * below[pl.ds(2 * levels + k, 1), :]
                from_north = from_north + north_s * beyond[pl.ds(2 * levels + k, 1), :]
            spread = diffusion * x
            push_x = flow_x * x
            push_y = flow_y * x
            eastern = pltpu.roll(spread + push_x, width - 1, 1)
            western = pltpu.roll(spread - push_x, 1, 1)
            northern = jnp.where(
                row == SUBLANES - 1, from_north, pltpu.roll(spread + push_y, SUBLANES - 1, 0)
            )
            southern = jnp.where(row == 0, from_south, pltpu.roll(spread - push_y, 1, 0))
            value = (1.0 - 4.0 * diffusion) * x + ((eastern + western) + (northern + southern))
            result[t, i] = jnp.where(is_wet, value, 0.0)
        return 0

    lax.fori_loop(0, levels_here, level, 0, unroll=True)


def shards(
    tracer_adjoint,
    eta_adjoint,
    velocity_x,
    velocity_y,
    mixing,
    thickness,
    surface_damping,
    wet_levels,
    seam_codes,
):
    tracers, levels, rows, width = tracer_adjoint.shape
    f32 = jnp.float32
    count = lax.axis_size("face")
    upward = [(i, (i + 1) % count) for i in range(count)]
    downward = [(j, i) for i, j in upward]
    tile = jax.ShapeDtypeStruct((rows, width), f32)
    lines = -(-3 * levels // SUBLANES) * SUBLANES
    line = jax.ShapeDtypeStruct((lines, width), f32)

    packed = pl.pallas_call(
        pack_kernel,
        out_shape=jax.ShapeDtypeStruct((2 * rows, width + LANES), f32),
        in_specs=[SMEM, VMEM, VMEM],
        out_specs=VMEM,
        name="pack",
    )(seam_codes, eta_adjoint, surface_damping)
    packed = lax.all_gather(packed, "face")

    solved, up, down = pl.pallas_call(
        column_kernel,
        out_shape=(jax.ShapeDtypeStruct((3, levels, rows, width), f32), line, line),
        in_specs=[SMEM, SMEM] + [VMEM] * 4,
        out_specs=(VMEM, VMEM, VMEM),
        scratch_shapes=[pltpu.VMEM((levels, rows, width), f32)],
        compiler_params=PARAMS,
        cost_estimate=pl.CostEstimate(flops=40000000, bytes_accessed=13000000, transcendentals=0),
        name="columns",
    )(seam_codes, thickness, tracer_adjoint, mixing, velocity_y, wet_levels)
    below = lax.ppermute(up, "face", upward)
    above = lax.ppermute(down, "face", downward)

    fields = pltpu.VMEM((count, rows, width), f32)
    edges = pltpu.VMEM((count, width), f32)
    surface, rims = pl.pallas_call(
        surface_kernel,
        out_shape=(tile, tile),
        in_specs=[SMEM, VMEM],
        out_specs=(VMEM, VMEM),
        scratch_shapes=[fields, fields, fields, edges, edges],
        compiler_params=PARAMS,
        name="surface",
    )(lax.axis_index("face")[None], packed)

    def transport(surface, rims, solved, below, above):
        chunk = 5 if levels % 5 == 0 else 1
        whole = pl.BlockSpec((rows, width), lambda k: (0, 0))
        many = pl.BlockSpec((lines, width), lambda k: (0, 0))
        field = pl.BlockSpec((chunk, rows, width), lambda k: (k, 0, 0))
        return pl.pallas_call(
            transport_kernel,
            out_shape=jax.ShapeDtypeStruct((tracers, levels, rows, width), f32),
            grid=(levels // chunk,),
            in_specs=[
                SMEM,
                pl.BlockSpec((3, chunk, rows, width), lambda k: (0, k, 0, 0)),
                field,
                field,
                whole,
                whole,
                whole,
                many,
                many,
            ],
            out_specs=pl.BlockSpec((tracers, chunk, rows, width), lambda k: (0, k, 0, 0)),
            scratch_shapes=[pltpu.VMEM((lines, width), f32)],
            compiler_params=PARAMS,
            name="transport",
        )(seam_codes, solved, velocity_x, velocity_y, wet_levels, surface, rims, below, above)

    return transport(surface, rims, solved, below, above), surface


def solution(mesh):
    placed = (
        P(None, None, "face", "ens"),
        P("face", "ens"),
        P(None, "face", "ens"),
        P(None, "face", "ens"),
        P(None, "face", "ens"),
        P(),
        P("face", None),
        P("face", None),
        P("face"),
    )
    return jax.shard_map(
        shards,
        mesh=mesh,
        in_specs=placed,
        out_specs=(P(None, None, "face", "ens"), P("face", "ens")),
        check_vma=False,
    )
```

time: 63.1 us -> 82 us (1.30)
  the two profiles are of different devices: /device:TPU:0 before, /device:TPU:1 now
where the time goes in v2:
time: 82 us; the launch traced here: 81.4 us
  waiting for transfers between devices  34.3 us (42%)
  Pallas kernels  30.2 us (37%)
  between operations  14.7 us (18%)
  starting transfers between devices  1.16 us (1%)
  local copies, waits for them, and re-layouts  1.06 us (1%)
    all_gather x1, waiting for transfers between devices, shards(): packed = lax.all_gather(packed, 'face')  34.3 us
    pallas_call x1, Pallas kernels, transport(): pl.pallas_call(transport_kernel, out_shape=jax.ShapeDtypeStruct((tracers,...  11.3 us
    pallas_call x1, Pallas kernels, shards(): pl.pallas_call(column_kernel, out_shape=(jax.ShapeDtypeStruct((3, levels,...  10.1 us
    pallas_call x1, Pallas kernels, shards(): pl.pallas_call(surface_kernel, out_shape=(tile, tile), in_specs=[SMEM, VM...  7.29 us
  transfers between devices with their start and end apart: 3, of which 1 were waited for; matrix products, arithmetic and copies ran while one was open for 0% of the time, Pallas kernels for 21%

profile of v2, /device:TPU:1, one launch (start us, length us, event | category | flops | bytes accessed | tf_op | source)
XLA Modules:
  0.0 81.4 jit_solution(800319284513360219)
XLA Ops:
  7.2 0.0 all-gather.3.cloned.1.call-start
  7.9 1.4 %pack.1 = f32[16,1152]{1,0:T(8,128)} custom-call(s32[1]{0:T(128)S(6)} %copy.11.seam, f32[8,1024]{1,0:T(8,128)} %eta.1, f32[8,1024]{1,0:T(8,128)} %damping.1), custom_call_target="tpu_custom_call" | custom-call | tf_op jit(solution)/shard_map/pack/pallas_call | solution.py:231
  9.3 0.0 all-gather.3.cloned.1.call-update
  9.3 10.1 %columns.1 = (f32[3,50,8,1024]{3,2,1,0:T(8,128)}, f32[152,1024]{1,0:T(8,128)}, f32[152,1024]{1,0:T(8,128)}) custom-call(s32[1]{0:T(128)S(6)} %copy.11.seam, f32[50]{0:T(128)} %thickness.1, f32[2,50,8,1024]{3,2,1,0:T(8,128)} %tracer.1, f32[49,8,1024]{2,1,0:T(8,128)} %mixing.1, f32[50,8,1024]{2,1,0:T(8,128)} %velocity_y.3, s32[8,1024]{1,0:T(8,128)} %wet.3), custom_call_target="tpu_custom_call" | custom-call | flops 40000000 | bytes 13000000 | tf_op jit(solution)/shard_map/columns/pallas_call | solution.py:240
  19.4 1.1 %collective-permute-start = (f32[152,1024]{1,0:T(8,128)}, f32[152,1024]{1,0:T(8,128)S(1)}, u32[]{:S(2)}, u32[]{:S(2)}) collective-permute-start(f32[152,1024]{1,0:T(8,128)} %get-tuple-element.10), channel_id=1, source_target_pairs={{0,1},{1,2},{2,3},{3,4},{4,5},{5,6},{6,7},{7,8},{8,9},{9,10},{10,1... | collective-permute-start | bytes 1867784 | tf_op jit(solution)/shard_map/ppermute | solution.py:250
  20.6 0.0 collective-permute-start.1
  20.6 34.3 %all-gather.3.cloned.1.call-done = f32[256,1152]{1,0:T(8,128)} async-done(((f32[16,1152]{1,0:T(8,128)}), f32[256,1152]{1,0:T(8,128)}) %all-gather.3.cloned.1.call-update) | async-done | bytes 1179664 | tf_op jit(solution)/shard_map/all_gather | solution.py:238
  54.9 7.3 %surface.1 = (f32[8,1024]{1,0:T(8,128)}, f32[8,1024]{1,0:T(8,128)}) custom-call(s32[1]{0:T(128)} %bitcast.place, f32[16,16,1152]{2,1,0:T(8,128)} %bitcast.2), custom_call_target="tpu_custom_call" | custom-call | tf_op jit(solution)/shard_map/surface/pallas_call | solution.py:255
  62.2 0.0 collective-permute-done.below
  62.2 0.0 copy-start
  62.2 0.0 collective-permute-done.1.above
  62.2 0.0 copy-start.1
  62.2 0.8 %copy-done = f32[152,1024]{1,0:T(8,128)} copy-done((f32[152,1024]{1,0:T(8,128)}, f32[152,1024]{1,0:T(8,128)S(1)}, u32[]{:S(2)}) %copy-start) | copy-done | bytes 622616
  63.0 0.2 copy-done.1
  63.2 11.3 %transport.1 = f32[2,50,8,1024]{3,2,1,0:T(8,128)} custom-call(s32[1]{0:T(128)S(6)} %copy.11.seam, f32[3,50,8,1024]{3,2,1,0:T(8,128)} %get-tuple-element.7.solved, f32[50,8,1024]{2,1,0:T(8,128)} %velocity_x.1, f32[50,8,1024]{2,1,0:T(8,128)} %velocity_y.3, s32[8,1024]{1,0:T(8,128)} %wet.3, f32[8,1024]{1,0:T(8,128)} %get-tuple-element.6.surface, ...), custom_call_target="tpu_custom_call" | custom-call | tf_op jit(solution)/shard_map/transport/pallas_call | solution.py:270
Async XLA Ops:
  7.2 47.7 %all-gather.3.cloned.1.call-start = ((), (), s32[]{:S(2)}) async-start(), calls=%async_computation | async-start | bytes 1253376 | tf_op jit(solution)/shard_map/all_gather | solution.py:238
  19.4 42.7 %collective-permute-start = (f32[152,1024]{1,0:T(8,128)}, f32[152,1024]{1,0:T(8,128)S(1)}, u32[]{:S(2)}, u32[]{:S(2)}) collective-permute-start(f32[152,1024]{1,0:T(8,128)} %get-tuple-element.10), channel_id=1, source_target_pairs={{0,1},{1,2},{2,3},{3,4},{4,5},{5,6},{6,7},{7,8},{8,9},{9,10},{10,1... | collective-permute-start | bytes 1867784 | tf_op jit(solution)/shard_map/ppermute | solution.py:250
  20.6 41.6 %collective-permute-start.1 = (f32[152,1024]{1,0:T(8,128)}, f32[152,1024]{1,0:T(8,128)S(1)}, u32[]{:S(2)}, u32[]{:S(2)}) collective-permute-start(f32[152,1024]{1,0:T(8,128)} %get-tuple-element.11), channel_id=1, source_target_pairs={{1,0},{2,1},{3,2},{4,3},{5,4},{6,5},{7,6},{8,7},{9,8},{10,9},{11,1... | collective-permute-start | bytes 1867784 | tf_op jit(solution)/shard_map/ppermute | solution.py:251
  62.2 0.9 %copy-start = (f32[152,1024]{1,0:T(8,128)}, f32[152,1024]{1,0:T(8,128)S(1)}, u32[]{:S(2)}) copy-start(f32[152,1024]{1,0:T(8,128)S(1)} %collective-permute-done.below) | copy-start | bytes 1867780
  62.2 1.1 %copy-start.1 = (f32[152,1024]{1,0:T(8,128)}, f32[152,1024]{1,0:T(8,128)S(1)}, u32[]{:S(2)}) copy-start(f32[152,1024]{1,0:T(8,128)S(1)} %collective-permute-done.1.above) | copy-start | bytes 1867780
Sparse Core Ops, SparseCore 0:
  10.3 44.5 all-gather.2

commit v3 on v1

v3 whole, which is shorter than its diff:
```python
import functools
import jax
import jax.numpy as jnp
from jax import lax
from jax.experimental import pallas as pl
from jax.experimental.pallas import tpu as pltpu
from jax.sharding import PartitionSpec as P

ITERS = 4
LANES = 128
SUBLANES = 8
diffusion = 0.1
advection = 0.5

MIDDLE = 4.1
LOSS = 1000.0

SMEM = pl.BlockSpec(memory_space=pltpu.SMEM)
VMEM = pl.BlockSpec(memory_space=pltpu.VMEM)
HBM = pl.BlockSpec(memory_space=pltpu.HBM)
PARAMS = pltpu.CompilerParams(vmem_limit_bytes=32 * 2**20)


def with_halo(x, sides, width):
    for axis, dim in sides:
        count, length = (lax.axis_size(axis), x.shape[dim])
        up = [(i, (i + 1) % count) for i in range(count)]
        down = [(j, i) for i, j in up]
        last = lax.slice_in_dim(x, length - width, length, axis=dim)
        initial = lax.slice_in_dim(x, 0, width, axis=dim)
        before = lax.ppermute(last, axis, up)
        after = lax.ppermute(initial, axis, down)
        x = jnp.concatenate([before, x, after], axis=dim)
    return x


def raised(block_rows, turned):
    upper_row = block_rows[..., -1:, :]
    upper_row = jnp.where(turned, jnp.flip(upper_row, -1), upper_row)
    return jnp.concatenate([block_rows[..., :-1, :], upper_row], axis=-2)


def settled(block_rows, padded, turned):
    lower_rim = padded[..., :1, :]
    upper_rim = padded[..., -1:, :]
    upper_rim = jnp.where(turned, jnp.flip(upper_rim, -1), upper_rim)
    southern = jnp.concatenate([lower_rim, block_rows[..., :-1, :]], axis=-2)
    northern = jnp.concatenate([block_rows[..., 1:, :], upper_rim], axis=-2)
    return (southern, northern)


def surface_apply(values_in, damping, turned):
    padded = with_halo(raised(values_in, turned), (("face", 0),), 1)
    southern, northern = settled(values_in, padded, turned)
    return (4.0 + damping) * values_in - (
        southern + northern + jnp.roll(values_in, 1, -1) + jnp.roll(values_in, -1, -1)
    )


def stepwise_surface(eta_adjoint, surface_damping, turned):
    surface = jnp.zeros_like(eta_adjoint)
    residual = eta_adjoint
    direction = eta_adjoint
    norm_now = lax.psum(jnp.sum(residual * residual), "face")
    for step in range(ITERS):
        applied = surface_apply(direction, surface_damping, turned)
        step_size = norm_now / lax.psum(jnp.sum(direction * applied), "face")
        surface = surface + step_size * direction
        residual = residual - step_size * applied
        norm_next = lax.psum(jnp.sum(residual * residual), "face")
        direction = residual + norm_next / norm_now * direction
        norm_now = norm_next
    return surface


def flip_lanes(rows):
    width = rows.shape[1]
    back = LANES - 1 - lax.broadcasted_iota(jnp.int32, (SUBLANES, LANES), 1)
    tiles = []
    for start in range(width - LANES, -1, -LANES):
        tiles.append(
            jnp.take_along_axis(
                rows[:, start : start + LANES], back, axis=1, mode="promise_in_bounds"
            )
        )
    return jnp.concatenate(tiles, axis=1)


def chunks_of(levels, size):
    return [(k, min(size, levels - k)) for k in range(0, levels, size)]


def line_of(tracer, level, levels):
    full = levels // SUBLANES
    if level < full * SUBLANES:
        return tracer * full * SUBLANES + level
    return 3 * full * SUBLANES + tracer * (levels % SUBLANES) + level - full * SUBLANES


def flip_some(rows):
    height, width = rows.shape
    if height < SUBLANES:
        rows = jnp.concatenate([rows, jnp.zeros((SUBLANES - height, width), rows.dtype)], axis=0)
    return flip_lanes(rows)[:height]


def outer_kernel(seam, eta, damping, up, down):
    half = SUBLANES // 2
    down[:half, :] = eta[:half, :]
    down[half:, :] = damping[:half, :]
    up[:half, :] = eta[half:, :]
    up[half:, :] = damping[half:, :]

    @pl.when(seam[0] == 1)
    def _():
        up[...] = flip_lanes(up[...])


def basis_kernel(seam, eta, damping, below, above, basis, sums):
    half = SUBLANES // 2
    rows = 2 * SUBLANES
    beyond = above[...]
    beyond = jnp.where(seam[0] == 1, flip_lanes(beyond), beyond)
    width = beyond.shape[1]
    v = jnp.concatenate([below[:half, :], eta[...], beyond[:half, :]], axis=0)
    d = jnp.concatenate([below[half:, :], damping[...], beyond[half:, :]], axis=0)
    d = (d + (4.0 - MIDDLE)) * (1.0 / MIDDLE)
    vectors = [v]
    for j in range(ITERS):
        now = vectors[-1]
        near = (
            pltpu.roll(now, 1, 0)
            + pltpu.roll(now, rows - 1, 0)
            + pltpu.roll(now, 1, 1)
            + pltpu.roll(now, width - 1, 1)
        )
        image = d * now - near * (1.0 / MIDDLE)
        vectors.append(image if j == 0 else 2.0 * image - vectors[-2])
    for j in range(ITERS):
        basis[j] = vectors[j]
    row = lax.broadcasted_iota(jnp.int32, (rows, LANES), 0)
    own = (row >= half) & (row < half + SUBLANES)
    parts = []
    for j in range(2 * ITERS):
        product = vectors[j // 2] * vectors[j // 2 + j % 2]
        total = product[:, :LANES]
        for start in range(LANES, width, LANES):
            total = total + product[:, start : start + LANES]
        parts.append(jnp.sum(jnp.where(own, total, 0.0), axis=0, keepdims=True))
    tile = jnp.concatenate(parts, axis=0)
    for i in range(sums.shape[0]):
        sums[i] = tile


def coefficients(moments):
    def dot(a, b):
        total = None
        for i, x in enumerate(a):
            for j, y in enumerate(b):
                term = x * y * (moments[i + j] + moments[abs(i - j)])
                total = term if total is None else total + term
        return 0.5 * total

    def image(p):
        q = [MIDDLE * x for x in p] + [jnp.zeros_like(p[0])]
        for i, x in enumerate(p):
            if i == 0:
                q[1] = q[1] + MIDDLE * x
            else:
                q[i + 1] = q[i + 1] + (0.5 * MIDDLE) * x
                q[i - 1] = q[i - 1] + (0.5 * MIDDLE) * x
        return q

    def size(p):
        return functools.reduce(lambda a, b: a + b, [jnp.abs(x) for x in p])

    def plus(a, b):
        return [x + y for x, y in zip(a, b)] + list(a[len(b) :]) + list(b[len(a) :])

    norm_first = moments[0]
    p = [jnp.ones_like(norm_first)]
    r = p
    norm_now = norm_first
    s = []
    sound = norm_first > 0.0
    for step in range(ITERS):
        q = image(p)
        curve = dot(p, q)
        sound = sound & (curve * LOSS >= size(p) * size(q) * norm_first)
        rate = norm_now / curve
        s = plus(s, [rate * x for x in p])
        if step < ITERS - 1:
            r = plus(r, [-rate * x for x in q])
            norm_next = dot(r, r)
            sound = sound & (norm_next * LOSS >= size(r) * size(r) * norm_first)
            ratio = norm_next / norm_now
            p = plus(r, [ratio * x for x in p])
            norm_now = norm_next
    return s, sound


def surface_kernel(sums, basis, surface, sound):
    half = SUBLANES // 2
    parts = [sums[i] for i in range(sums.shape[0])]
    while len(parts) > 1:
        pairs = [a + b for a, b in zip(parts[::2], parts[1::2])]
        parts = pairs + parts[len(parts) - len(parts) % 2 :]
    total = jnp.sum(parts[0], axis=1, keepdims=True)
    raw = [total[j : j + 1, :] for j in range(2 * ITERS)]
    moments = raw[:2]
    for j in range(2, 2 * ITERS):
        moments.append(2.0 * raw[j] - raw[j % 2])
    s, good = coefficients(moments)
    value = s[0] * basis[0]
    for j in range(1, ITERS):
        value = value + s[j] * basis[j]
    surface[:SUBLANES, :] = value[half : half + SUBLANES, :]
    surface[SUBLANES : SUBLANES + 1, :] = value[half - 1 : half, :]
    surface[SUBLANES + 1 : SUBLANES + 2, :] = value[half + SUBLANES : half + SUBLANES + 1, :]
    surface[SUBLANES + 2 :, :] = jnp.zeros((SUBLANES - 2, value.shape[1]), value.dtype)
    sound[0] = jnp.where(good, 1, 0)[0, 0]


CHUNK = 10


def column_kernel(
    seam, thickness, tracer, mixing, velocity_y, wet, after, solved, up, down,
    tracer_at, mixing_at, velocity_at, solved_at, ratio_at, sems, out_sems,
):
    levels = tracer.shape[1]
    chunks = chunks_of(levels, CHUNK)
    loads = []
    for i, (k, n) in enumerate(chunks):
        m = min(n, levels - 1 - k)
        loads.append((
            pltpu.make_async_copy(
                tracer.at[:, pl.ds(k, n)], tracer_at.at[:, pl.ds(k, n)], sems.at[0, i]
            ),
            pltpu.make_async_copy(
                mixing.at[pl.ds(k, m)], mixing_at.at[pl.ds(k, m)], sems.at[1, i]
            ),
        ))
    velocity_load = pltpu.make_async_copy(velocity_y, velocity_at, sems.at[2, 0])
    for pair in loads:
        pair[0].start()
        pair[1].start()
    velocity_load.start()

    depth = wet[...]
    zero = jnp.zeros(depth.shape, jnp.float32)

    def forward(k, carry):
        c_before, g_before, y0, y1, y2 = carry
        th = thickness[k]
        c = jnp.where(k + 1 < depth, mixing_at[jnp.minimum(k, levels - 2)], 0.0)
        inverse = 1.0 / (th + c + c_before * (1.0 - g_before))
        g = c * inverse
        y0 = (tracer_at[0, k] + c_before * y0) * inverse
        y1 = (tracer_at[1, k] + c_before * y1) * inverse
        y2 = (jnp.where(k < depth, th, 0.0) + c_before * y2) * inverse
        ratio_at[k] = g
        solved_at[0, k] = y0
        solved_at[1, k] = y1
        solved_at[2, k] = y2
        return c, g, y0, y1, y2

    carry = (zero,) * 5
    for i, (k, n) in enumerate(chunks):
        loads[i][0].wait()
        loads[i][1].wait()
        carry = lax.fori_loop(k, k + n, forward, carry, unroll=2)

    stores = []
    carry = (zero,) * 3
    for i, (k, n) in reversed(list(enumerate(chunks))):

        def backward(j, carry, last=k + n - 1):
            level = last - j
            th = thickness[level]
            g = ratio_at[level]
            after = []
            for t in range(3):
                u = solved_at[t, level] + g * carry[t]
                solved_at[t, level] = th * u
                after.append(u)
            return tuple(after)

        carry = lax.fori_loop(0, n, backward, carry, unroll=2)
        stores.append(
            pltpu.make_async_copy(
                solved_at.at[:, pl.ds(k, n)], solved.at[:, pl.ds(k, n)], out_sems.at[i]
            )
        )
        stores[-1].start()

    velocity_load.wait()
    turned = seam[0] == 1
    for k, n in chunks_of(levels, SUBLANES):
        flow_top = advection * velocity_at[pl.ds(k, n), SUBLANES - 1, :]
        flow_bottom = advection * velocity_at[pl.ds(k, n), 0, :]
        for t in range(3):
            line = line_of(t, k, levels)
            top = solved_at[t, pl.ds(k, n), SUBLANES - 1, :] * (diffusion - flow_top)
            up[line : line + n, :] = jnp.where(turned, flip_some(top), top)
            bottom = solved_at[t, pl.ds(k, n), 0, :] * (diffusion + flow_bottom)
            down[line : line + n, :] = bottom
    for store in stores:
        store.wait()


def transport_kernel(
    seam, solved, velocity_x, velocity_y, wet, fields, below, above, result, surface,
    solved_at, x_at, y_at, result_at, sems, out_sems,
):
    levels = velocity_x.shape[0]
    width = wet.shape[1]
    chunks = chunks_of(levels, SUBLANES)
    loads = []
    for i, (k, n) in enumerate(chunks):
        at = pl.ds(k, n)
        loads.append((
            pltpu.make_async_copy(solved.at[:, at], solved_at.at[:, at], sems.at[0, i]),
            pltpu.make_async_copy(velocity_x.at[at], x_at.at[at], sems.at[1, i]),
            pltpu.make_async_copy(velocity_y.at[at], y_at.at[at], sems.at[2, i]),
        ))
    for group in loads:
        for load in group:
            load.start()

    turned = seam[0] == 1
    depth = wet[...]
    s = fields[:SUBLANES, :]
    surface[...] = s
    south_s = fields[SUBLANES : SUBLANES + 1, :]
    north_s = fields[SUBLANES + 1 : SUBLANES + 2, :]
    depth_south = depth[:1, :]
    depth_north = depth[SUBLANES - 1 :, :]
    row = lax.broadcasted_iota(jnp.int32, depth.shape, 0)
    is_south = row == 0
    is_north = row == SUBLANES - 1

    def level(k, _):
        flow_x = advection * x_at[k]
        flow_y = advection * y_at[k]
        to_west = diffusion + flow_x
        to_east = diffusion - flow_x
        to_south = jnp.where(is_south, 0.0, diffusion + flow_y)
        to_north = jnp.where(is_north, 0.0, diffusion - flow_y)
        is_wet = k < depth
        for t in range(2):
            x = solved_at[t, k]
            if t == 0:
                x = x + s * solved_at[2, k]
            eastern = pltpu.roll(x * to_west, width - 1, 1)
            western = pltpu.roll(x * to_east, 1, 1)
            northern = pltpu.roll(x * to_south, SUBLANES - 1, 0)
            southern = pltpu.roll(x * to_north, 1, 0)
            value = (1.0 - 4.0 * diffusion) * x + ((eastern + western) + (northern + southern))
            result_at[t, k] = jnp.where(is_wet, value, 0.0)
        return 0

    stores = []
    for i, (k, n) in enumerate(chunks):
        for load in loads[i]:
            load.wait()
        lax.fori_loop(k, k + n, level, 0, unroll=2)
        index = k + lax.broadcasted_iota(jnp.int32, (n, width), 0)
        for t in range(2):
            line = line_of(t, k, levels)
            south = below[line : line + n, :]
            north = above[line : line + n, :]
            if t == 0:
                line = line_of(2, k, levels)
                south = south + south_s * below[line : line + n, :]
                beyond = above[line : line + n, :]
                north = jnp.where(turned, flip_some(north), north)
                north = north + north_s * jnp.where(turned, flip_some(beyond), beyond)
            else:
                north = jnp.where(turned, flip_some(north), north)
            at = pl.ds(k, n)
            result_at[t, at, 0, :] += jnp.where(index < depth_south, south, 0.0)
            result_at[t, at, SUBLANES - 1, :] += jnp.where(index < depth_north, north, 0.0)
        stores.append(
            pltpu.make_async_copy(
                result_at.at[:, pl.ds(k, n)], result.at[:, pl.ds(k, n)], out_sems.at[i]
            )
        )
        stores[-1].start()
    for store in stores:
        store.wait()


def shards(
    tracer_adjoint,
    eta_adjoint,
    velocity_x,
    velocity_y,
    mixing,
    thickness,
    surface_damping,
    wet_levels,
    seam_codes,
):
    tracers, levels, rows, width = tracer_adjoint.shape
    f32 = jnp.float32
    count = lax.axis_size("face")
    upward = [(i, (i + 1) % count) for i in range(count)]
    downward = [(j, i) for i, j in upward]
    tile = jax.ShapeDtypeStruct((rows, width), f32)
    ext = jax.ShapeDtypeStruct((ITERS, 2 * rows, width), f32)
    lines = -(-3 * levels // SUBLANES) * SUBLANES
    line = jax.ShapeDtypeStruct((lines, width), f32)

    up, down = pl.pallas_call(
        outer_kernel,
        out_shape=(tile, tile),
        in_specs=[SMEM, VMEM, VMEM],
        out_specs=(VMEM, VMEM),
        name="outer_rows",
    )(seam_codes, eta_adjoint, surface_damping)
    below = lax.ppermute(up, "face", upward)
    above = lax.ppermute(down, "face", downward)

    cube = pltpu.VMEM((levels, rows, width), f32)
    parts = len(chunks_of(levels, CHUNK))
    solved, up, down = pl.pallas_call(
        column_kernel,
        out_shape=(jax.ShapeDtypeStruct((3, levels, rows, width), f32), line, line),
        in_specs=[SMEM, SMEM, HBM, HBM, HBM, VMEM, HBM],
        out_specs=(HBM, VMEM, VMEM),
        scratch_shapes=[
            pltpu.VMEM((tracers, levels, rows, width), f32),
            cube,
            cube,
            pltpu.VMEM((3, levels, rows, width), f32),
            cube,
            pltpu.SemaphoreType.DMA((3, parts)),
            pltpu.SemaphoreType.DMA((parts,)),
        ],
        compiler_params=PARAMS,
        cost_estimate=pl.CostEstimate(flops=40000000, bytes_accessed=13000000, transcendentals=0),
        name="columns",
    )(
        seam_codes,
        thickness,
        *(pltpu.with_memory_space_constraint(x, pltpu.HBM) for x in (tracer_adjoint, mixing, velocity_y)),
        wet_levels,
        up,
    )

    basis, sums = pl.pallas_call(
        basis_kernel,
        out_shape=(ext, jax.ShapeDtypeStruct((count, SUBLANES, LANES), f32)),
        in_specs=[SMEM] + [VMEM] * 4,
        out_specs=(VMEM, VMEM),
        compiler_params=PARAMS,
        name="surface_basis",
    )(seam_codes, eta_adjoint, surface_damping, below, above)
    sums, up, down = lax.optimization_barrier((sums, up, down))
    sums = lax.all_to_all(sums, "face", 0, 0)
    below = lax.ppermute(up, "face", upward)
    above = lax.ppermute(down, "face", downward)

    fields, sound = pl.pallas_call(
        surface_kernel,
        out_shape=(
            jax.ShapeDtypeStruct((2 * rows, width), f32),
            jax.ShapeDtypeStruct((1,), jnp.int32),
        ),
        in_specs=[VMEM, VMEM],
        out_specs=(VMEM, SMEM),
        compiler_params=PARAMS,
        name="surface",
    )(sums, basis)

    def by_moments(fields):
        return fields

    def by_steps(fields):
        turned = seam_codes[0] == 1
        surface = stepwise_surface(eta_adjoint, surface_damping, turned)
        top, bottom = surface[-1:], surface[:1]
        top = jnp.where(turned, jnp.flip(top, -1), top)
        south = lax.ppermute(top, "face", upward)
        north = lax.ppermute(bottom, "face", downward)
        north = jnp.where(turned, jnp.flip(north, -1), north)
        return jnp.concatenate([surface, south, north, fields[rows + 2 :]], axis=0)

    fields = lax.cond(sound[0] == 1, by_moments, by_steps, fields)

    parts = len(chunks_of(levels, SUBLANES))
    return pl.pallas_call(
        transport_kernel,
        out_shape=(jax.ShapeDtypeStruct((tracers, levels, rows, width), f32), tile),
        in_specs=[SMEM, HBM, HBM, HBM] + [VMEM] * 4,
        out_specs=(HBM, VMEM),
        scratch_shapes=[
            pltpu.VMEM((3, levels, rows, width), f32),
            cube,
            cube,
            pltpu.VMEM((tracers, levels, rows, width), f32),
            pltpu.SemaphoreType.DMA((3, parts)),
            pltpu.SemaphoreType.DMA((parts,)),
        ],
        compiler_params=PARAMS,
        name="transport",
    )(seam_codes, solved, velocity_x, velocity_y, wet_levels, fields, below, above)


def solution(mesh):
    placed = (
        P(None, None, "face", "ens"),
        P("face", "ens"),
        P(None, "face", "ens"),
        P(None, "face", "ens"),
        P(None, "face", "ens"),
        P(),
        P("face", None),
        P("face", None),
        P("face"),
    )
    return jax.shard_map(
        shards,
        mesh=mesh,
        in_specs=placed,
        out_specs=(P(None, None, "face", "ens"), P("face", "ens")),
        check_vma=False,
    )
```

time: 63.1 us -> 47.9 us (0.76); the launches traced: 63.3 us -> 47.4 us
  blocking collectives: 0 us -> 11.2 us
  starting transfers between devices: 20.5 us -> 10.1 us
  waiting for transfers between devices: 10.4 us -> 0.01 us
  Pallas kernels: 24.8 us -> 17.4 us
  local copies, waits for them, and re-layouts: 4.2 us -> 6.75 us
  other arithmetic: 1.29 us -> 0 us
    all_to_all x0 -> x1, blocking collectives: none -> 11.2 us  [shards(): sums = lax.all_to_all(sums, 'face', 0, 0)]
    ppermute x6 -> x0, starting transfers between devices: 10.6 us -> none  [gathered_sums(): parts.append(lax.ppermute(total, axis, pairs))]
    ppermute x6 -> x0, waiting for transfers between devices: 7 us -> none  [gathered_sums(): parts.append(lax.ppermute(total, axis, pairs))]
    pallas_call x1, Pallas kernels: 10.3 us -> 6.2 us  [shards(): pl.pallas_call(column_kernel, out_shape=(jax.ShapeDtypeStruct((3, levels,...]
    pallas_call x3, Pallas kernels: 13.8 us -> 9.76 us  [the longest x1 8.37 us: shards(): pl.pallas_call(transport_kernel, out_shape=(jax.ShapeDtypeStruct((tracers...]
    unnamed x16 -> x20, local copies, waits for them, and re-layouts: 2.95 us -> 6.75 us
    ppermute x2, waiting for transfers between devices: 3.42 us -> 0.01 us  [shards(): below = lax.ppermute(up, 'face', upward)]
    slice x1 -> x0, local copies, waits for them, and re-layouts: 1.25 us -> none  [shards(): sound[0, 0] == 1]
  transfers between devices with their start and end apart: 10 -> 4, of which waited for: 6 -> 0; matrix products, arithmetic and copies ran while one was open for 4% -> 0% of each run, Pallas kernels for 7% -> 15%
where the time goes in v3:
time: 47.9 us; the launch traced here: 47.4 us
  Pallas kernels  17.4 us (36%)
  blocking collectives  11.2 us (23%)
  starting transfers between devices  10.1 us (21%)
  local copies, waits for them, and re-layouts  6.75 us (14%)
  between operations  2.05 us (4%)
    all_to_all x1, blocking collectives, shards(): sums = lax.all_to_all(sums, 'face', 0, 0)  11.2 us
    ppermute x2, starting transfers between devices, shards(): above = lax.ppermute(down, 'face', downward)  10 us
    pallas_call x1, Pallas kernels, shards(): pl.pallas_call(transport_kernel, out_shape=(jax.ShapeDtypeStruct((tracers...  8.37 us
    unnamed x20, local copies, waits for them, and re-layouts  6.75 us
    pallas_call x1, Pallas kernels, shards(): pl.pallas_call(column_kernel, out_shape=(jax.ShapeDtypeStruct((3, levels,...  6.2 us
    pallas_call x1, Pallas kernels, shards(): pl.pallas_call(outer_kernel, out_shape=(tile, tile), in_specs=[SMEM, VMEM...  1.41 us
  transfers between devices with their start and end apart: 4, of which 0 were waited for; matrix products, arithmetic and copies ran while one was open for 0% of the time, Pallas kernels for 15%

profile of v3, /device:TPU:0, one launch (start us, length us, event | category | flops | bytes accessed | tf_op | source)
XLA Modules:
  0.0 47.4 jit_solution(16511978500138441809)
XLA Ops:
  1.3 1.4 %outer_rows.1 = (f32[8,1024]{1,0:T(8,128)}, f32[8,1024]{1,0:T(8,128)}) custom-call(s32[1]{0:T(128)S(6)} %copy.13.seam, f32[8,1024]{1,0:T(8,128)} %eta.3, f32[8,1024]{1,0:T(8,128)} %damping.3), custom_call_target="tpu_custom_call" | custom-call | tf_op jit(solution)/shard_map/outer_rows/pallas_call | solution.py:415
  2.7 5.5 %collective-permute-start.11 = (f32[8,1024]{1,0:T(8,128)}, f32[8,1024]{1,0:T(8,128)S(1)}, u32[]{:S(2)}, u32[]{:S(2)}) collective-permute-start(f32[8,1024]{1,0:T(8,128)} %get-tuple-element.32), channel_id=1, source_target_pairs={{1,0},{2,1},{3,2},{4,3},{5,4},{6,5},{7,6},{8,7},{9,8},{10,9},{11,1... | collective-permute-start | bytes 98312 | tf_op jit(solution)/shard_map/ppermute | solution.py:423
  8.2 0.0 collective-permute-start.10
  8.2 0.0 copy-start.4
  8.2 0.8 %copy-done.4 = s32[8,1024]{1,0:T(8,128)S(1)} copy-done((s32[8,1024]{1,0:T(8,128)S(1)}, s32[8,1024]{1,0:T(8,128)}, u32[]{:S(2)}) %copy-start.4) | copy-done | bytes 32792
  9.0 0.0 copy-start.6
  9.0 0.8 %copy-done.6 = f32[8,1024]{1,0:T(8,128)S(1)} copy-done((f32[8,1024]{1,0:T(8,128)S(1)}, f32[8,1024]{1,0:T(8,128)}, u32[]{:S(2)}) %copy-start.6) | copy-done | bytes 32792
  9.7 0.0 copy-start.7
  9.7 0.7 %copy-done.7 = f32[50]{0:T(128)S(1)} copy-done((f32[50]{0:T(128)S(1)}, f32[50]{0:T(128)}, u32[]{:S(2)}) %copy-start.7) | copy-done | bytes 224
  10.4 0.0 copy-start.8
  10.4 0.0 copy-start.9
  10.4 6.2 %columns.1 = (f32[3,50,8,1024]{3,2,1,0:T(8,128)S(1)}, f32[152,1024]{1,0:T(8,128)}, f32[152,1024]{1,0:T(8,128)}) custom-call(s32[1]{0:T(128)S(6)} %copy.13.seam, f32[50]{0:T(128)S(1)} %copy-done.7, f32[2,50,8,1024]{3,2,1,0:T(8,128)} %tracer.1, f32[49,8,1024]{2,1,0:T(8,128)} %mixing.1, f32[50,8,1024]{2,1,0:T(8,128)} %velocity_y.3, s32[8,1024]{1,0:T(8,128)S(1)} %copy-done.4, ...), custom_call_target="tpu_custom_call" | custom-call | flops 40000000 | bytes 13000000 | tf_op jit(solution)/shard_map/columns/pallas_call | solution.py:427
  16.6 0.0 copy-start.1
  16.6 2.2 %copy-done.1 = f32[3,50,8,1024]{3,2,1,0:T(8,128)} copy-done((f32[3,50,8,1024]{3,2,1,0:T(8,128)}, f32[3,50,8,1024]{3,2,1,0:T(8,128)S(1)}, u32[]{:S(2)}) %copy-start.1) | copy-done | bytes 4915224
  18.8 0.0 copy-start
  18.8 0.0 copy-start.3
  18.8 0.0 copy-start.5
  18.8 0.0 collective-permute-done.11.above
  18.8 0.0 collective-permute-done.10.below
  18.8 0.0 copy-done.8
  18.8 0.0 copy-done.9
  18.8 0.5 surface_basis.1
  19.3 0.1 collective-permute-start.12
  19.4 4.5 %collective-permute-start.13 = (f32[152,1024]{1,0:T(8,128)}, f32[152,1024]{1,0:T(8,128)}, u32[]{:S(2)}, u32[]{:S(2)}) collective-permute-start(f32[152,1024]{1,0:T(8,128)} %get-tuple-element.41), channel_id=1, source_target_pairs={{1,0},{2,1},{3,2},{4,3},{5,4},{6,5},{7,6},{8,7},{9,8},{10,9},{11,1... | collective-permute-start | bytes 1867784 | tf_op jit(solution)/shard_map/ppermute | solution.py:463
  23.9 11.2 %all_to_all.5.sums = f32[16,8,128]{2,1,0:T(8,128)S(1)} all-to-all(f32[16,8,128]{2,1,0:T(8,128)S(1)} %get-tuple-element.36), channel_id=1, replica_groups=mesh['ens'=2,'face'=16] {'face'}, dimensions={0} | all-to-all | bytes 131072 | tf_op jit(solution)/shard_map/all_to_all | solution.py:461
  35.0 0.9 %surface.1 = (f32[16,1024]{1,0:T(8,128)}, s32[1]{0:T(128)}) custom-call(f32[16,8,128]{2,1,0:T(8,128)S(1)} %all_to_all.5.sums, f32[4,16,1024]{2,1,0:T(8,128)S(1)} %get-tuple-element.37.basis), custom_call_target="tpu_custom_call" | custom-call | tf_op jit(solution)/shard_map/surface/pallas_call | solution.py:465
  36.6 0.0 collective-permute-done.12.below
  36.6 0.0 collective-permute-done.13.above
  36.6 0.0 copy-done
  36.6 0.0 copy-done.3
  36.7 0.0 copy-done.5
  36.7 0.0 copy-start.2
  36.7 2.4 %copy-done.2 = f32[3,50,8,1024]{3,2,1,0:T(8,128)S(1)} copy-done((f32[3,50,8,1024]{3,2,1,0:T(8,128)S(1)}, f32[3,50,8,1024]{3,2,1,0:T(8,128)}, u32[]{:S(2)}) %copy-start.2) | copy-done | bytes 4915224
  39.1 8.4 %transport.1 = (f32[2,50,8,1024]{3,2,1,0:T(8,128)}, f32[8,1024]{1,0:T(8,128)}) custom-call(s32[1]{0:T(128)S(6)} %copy.13.seam, f32[3,50,8,1024]{3,2,1,0:T(8,128)S(1)} %copy-done.2, f32[50,8,1024]{2,1,0:T(8,128)S(1)} %copy-done.3, f32[50,8,1024]{2,1,0:T(8,128)S(1)} %copy-done, s32[8,1024]{1,0:T(8,128)S(1)} %copy-done.5, f32[16,1024]{1,0:T(8,128)} %get-tuple-element.87.fields, ...), custom_call_target="tpu_custom_call" | custom-call | tf_op jit(solution)/shard_map/transport/pallas_call | solution.py:493
  (1 shorter events, 0.0 us)
Async XLA Ops:
  2.7 16.1 %collective-permute-start.11 = (f32[8,1024]{1,0:T(8,128)}, f32[8,1024]{1,0:T(8,128)S(1)}, u32[]{:S(2)}, u32[]{:S(2)}) collective-permute-start(f32[8,1024]{1,0:T(8,128)} %get-tuple-element.32), channel_id=1, source_target_pairs={{1,0},{2,1},{3,2},{4,3},{5,4},{6,5},{7,6},{8,7},{9,8},{10,9},{11,1... | collective-permute-start | bytes 98312 | tf_op jit(solution)/shard_map/ppermute | solution.py:423
  8.2 10.6 %collective-permute-start.10 = (f32[8,1024]{1,0:T(8,128)}, f32[8,1024]{1,0:T(8,128)S(1)}, u32[]{:S(2)}, u32[]{:S(2)}) collective-permute-start(f32[8,1024]{1,0:T(8,128)} %get-tuple-element.30.after), channel_id=1, source_target_pairs={{0,1},{1,2},{2,3},{3,4},{4,5},{5,6},{6,7},{7,8},{8,9},{9,10},{10,1... | collective-permute-start | bytes 98312 | tf_op jit(solution)/shard_map/ppermute | solution.py:422
  8.2 0.8 %copy-start.4 = (s32[8,1024]{1,0:T(8,128)S(1)}, s32[8,1024]{1,0:T(8,128)}, u32[]{:S(2)}) copy-start(s32[8,1024]{1,0:T(8,128)} %wet.3) | copy-start | bytes 98308
  9.0 0.8 %copy-start.6 = (f32[8,1024]{1,0:T(8,128)S(1)}, f32[8,1024]{1,0:T(8,128)}, u32[]{:S(2)}) copy-start(f32[8,1024]{1,0:T(8,128)} %get-tuple-element.30.after) | copy-start | bytes 98308
  9.7 0.7 %copy-start.7 = (f32[50]{0:T(128)S(1)}, f32[50]{0:T(128)}, u32[]{:S(2)}) copy-start(f32[50]{0:T(128)} %thickness.1) | copy-start | bytes 604
  10.4 8.4 %copy-start.8 = (f32[8,1024]{1,0:T(8,128)S(1)}, f32[8,1024]{1,0:T(8,128)}, u32[]{:S(2)}) copy-start(f32[8,1024]{1,0:T(8,128)} %eta.3) | copy-start | bytes 98308
  10.4 8.4 %copy-start.9 = (f32[8,1024]{1,0:T(8,128)S(1)}, f32[8,1024]{1,0:T(8,128)}, u32[]{:S(2)}) copy-start(f32[8,1024]{1,0:T(8,128)} %damping.3) | copy-start | bytes 98308
  16.6 2.2 %copy-start.1 = (f32[3,50,8,1024]{3,2,1,0:T(8,128)}, f32[3,50,8,1024]{3,2,1,0:T(8,128)S(1)}, u32[]{:S(2)}) copy-start(f32[3,50,8,1024]{3,2,1,0:T(8,128)S(1)} %get-tuple-element.31.solved) | copy-start | bytes 14745604
  18.8 17.9 %copy-start = (f32[50,8,1024]{2,1,0:T(8,128)S(1)}, f32[50,8,1024]{2,1,0:T(8,128)}, u32[]{:S(2)}) copy-start(f32[50,8,1024]{2,1,0:T(8,128)} %velocity_y.3) | copy-start | bytes 4915204
  18.8 17.9 %copy-start.3 = (f32[50,8,1024]{2,1,0:T(8,128)S(1)}, f32[50,8,1024]{2,1,0:T(8,128)}, u32[]{:S(2)}) copy-start(f32[50,8,1024]{2,1,0:T(8,128)} %velocity_x.1) | copy-start | bytes 4915204
  18.8 17.9 %copy-start.5 = (s32[8,1024]{1,0:T(8,128)S(1)}, s32[8,1024]{1,0:T(8,128)}, u32[]{:S(2)}) copy-start(s32[8,1024]{1,0:T(8,128)} %wet.3) | copy-start | bytes 98308
  19.3 17.3 %collective-permute-start.12 = (f32[152,1024]{1,0:T(8,128)}, f32[152,1024]{1,0:T(8,128)}, u32[]{:S(2)}, u32[]{:S(2)}) collective-permute-start(f32[152,1024]{1,0:T(8,128)} %get-tuple-element.40), channel_id=1, source_target_pairs={{0,1},{1,2},{2,3},{3,4},{4,5},{5,6},{6,7},{7,8},{8,9},{9,10},{10,1... | collective-permute-start | bytes 1867784 | tf_op jit(solution)/shard_map/ppermute | solution.py:462
  19.4 17.3 %collective-permute-start.13 = (f32[152,1024]{1,0:T(8,128)}, f32[152,1024]{1,0:T(8,128)}, u32[]{:S(2)}, u32[]{:S(2)}) collective-permute-start(f32[152,1024]{1,0:T(8,128)} %get-tuple-element.41), channel_id=1, source_target_pairs={{1,0},{2,1},{3,2},{4,3},{5,4},{6,5},{7,6},{8,7},{9,8},{10,9},{11,1... | collective-permute-start | bytes 1867784 | tf_op jit(solution)/shard_map/ppermute | solution.py:463
  36.7 2.4 %copy-start.2 = (f32[3,50,8,1024]{3,2,1,0:T(8,128)S(1)}, f32[3,50,8,1024]{3,2,1,0:T(8,128)}, u32[]{:S(2)}) copy-start(f32[3,50,8,1024]{3,2,1,0:T(8,128)} %copy-done.1) | copy-start | bytes 14745604

commit v4 on v3

--- a/solution.py
+++ b/solution.py
@@ -19,6 +19,10 @@
 VMEM = pl.BlockSpec(memory_space=pltpu.VMEM)
 HBM = pl.BlockSpec(memory_space=pltpu.HBM)
 PARAMS = pltpu.CompilerParams(vmem_limit_bytes=32 * 2**20)
+
+
+def in_hbm(x):
+    return pltpu.with_memory_space_constraint(x, pltpu.HBM)
 
 
 def with_halo(x, sides, width):
@@ -90,13 +94,6 @@
     return [(k, min(size, levels - k)) for k in range(0, levels, size)]
 
 
-def line_of(tracer, level, levels):
-    full = levels // SUBLANES
-    if level < full * SUBLANES:
-        return tracer * full * SUBLANES + level
-    return 3 * full * SUBLANES + tracer * (levels % SUBLANES) + level - full * SUBLANES
-
-
 def flip_some(rows):
     height, width = rows.shape
     if height < SUBLANES:
@@ -104,7 +101,7 @@
     return flip_lanes(rows)[:height]
 
 
-def outer_kernel(seam, eta, damping, up, down):
+def outer_kernel(seam, eta, damping, up, down, mark):
     half = SUBLANES // 2
     down[:half, :] = eta[:half, :]
     down[half:, :] = damping[:half, :]
@@ -199,7 +196,16 @@
     return s, sound
 
 
-def surface_kernel(sums, basis, surface, sound):
+def outer_lines(seam, fields, edges, up, down):
+    turned = seam[0] == 1
+    for k in range(0, up.shape[0], SUBLANES):
+        at = slice(k, k + SUBLANES)
+        top = edges[0, at, :] + fields[SUBLANES - 1 : SUBLANES, :] * edges[1, at, :]
+        up[at, :] = jnp.where(turned, flip_lanes(top), top)
+        down[at, :] = edges[2, at, :] + fields[:1, :] * edges[3, at, :]
+
+
+def surface_kernel(seam, sums, basis, edges, surface, up, down, sound):
     half = SUBLANES // 2
     parts = [sums[i] for i in range(sums.shape[0])]
     while len(parts) > 1:
@@ -214,40 +220,45 @@
     value = s[0] * basis[0]
     for j in range(1, ITERS):
         value = value + s[j] * basis[j]
-    surface[:SUBLANES, :] = value[half : half + SUBLANES, :]
-    surface[SUBLANES : SUBLANES + 1, :] = value[half - 1 : half, :]
-    surface[SUBLANES + 1 : SUBLANES + 2, :] = value[half + SUBLANES : half + SUBLANES + 1, :]
-    surface[SUBLANES + 2 :, :] = jnp.zeros((SUBLANES - 2, value.shape[1]), value.dtype)
+    surface[...] = value[half : half + SUBLANES, :]
     sound[0] = jnp.where(good, 1, 0)[0, 0]
+    outer_lines(seam, surface, edges, up, down)
 
 
 CHUNK = 10
 
 
 def column_kernel(
-    seam, thickness, tracer, mixing, velocity_y, wet, after, solved, up, down,
-    tracer_at, mixing_at, velocity_at, solved_at, ratio_at, sems, out_sems,
+    seam, thickness_from, tracer, mixing, velocity_y, wet, after, solved, up, down, edges,
+    thickness, depth_at, tracer_at, mixing_at, velocity_at, solved_at, ratio_at,
+    sems, out_sems,
 ):
     levels = tracer.shape[1]
     chunks = chunks_of(levels, CHUNK)
+    few = [
+        pltpu.make_async_copy(thickness_from, thickness, sems.at[2, 1]),
+        pltpu.make_async_copy(wet, depth_at, sems.at[2, 2]),
+    ]
     loads = []
     for i, (k, n) in enumerate(chunks):
         m = min(n, levels - 1 - k)
         loads.append((
             pltpu.make_async_copy(
-                tracer.at[:, pl.ds(k, n)], tracer_at.at[:, pl.ds(k, n)], sems.at[0, i]
+                mixing.at[pl.ds(k, m)], mixing_at.at[pl.ds(k, m)], sems.at[1, i]
             ),
             pltpu.make_async_copy(
-                mixing.at[pl.ds(k, m)], mixing_at.at[pl.ds(k, m)], sems.at[1, i]
+                tracer.at[:, pl.ds(k, n)], tracer_at.at[:, pl.ds(k, n)], sems.at[0, i]
             ),
         ))
     velocity_load = pltpu.make_async_copy(velocity_y, velocity_at, sems.at[2, 0])
-    for pair in loads:
+    for pair in [few] + loads:
         pair[0].start()
         pair[1].start()
     velocity_load.start()
 
-    depth = wet[...]
+    few[0].wait()
+    few[1].wait()
+    depth = depth_at[...]
     zero = jnp.zeros(depth.shape, jnp.float32)
 
     def forward(k, carry):
@@ -269,7 +280,7 @@
     for i, (k, n) in enumerate(chunks):
         loads[i][0].wait()
         loads[i][1].wait()
-        carry = lax.fori_loop(k, k + n, forward, carry, unroll=2)
+        carry = lax.fori_loop(k, k + n, forward, carry, unroll=5)
 
     stores = []
     carry = (zero,) * 3
@@ -286,7 +297,7 @@
                 after.append(u)
             return tuple(after)
 
-        carry = lax.fori_loop(0, n, backward, carry, unroll=2)
+        carry = lax.fori_loop(0, n, backward, carry, unroll=5)
         stores.append(
             pltpu.make_async_copy(
                 solved_at.at[:, pl.ds(k, n)], solved.at[:, pl.ds(k, n)], out_sems.at[i]
@@ -297,95 +308,70 @@
     velocity_load.wait()
     turned = seam[0] == 1
     for k, n in chunks_of(levels, SUBLANES):
-        flow_top = advection * velocity_at[pl.ds(k, n), SUBLANES - 1, :]
-        flow_bottom = advection * velocity_at[pl.ds(k, n), 0, :]
-        for t in range(3):
-            line = line_of(t, k, levels)
-            top = solved_at[t, pl.ds(k, n), SUBLANES - 1, :] * (diffusion - flow_top)
-            up[line : line + n, :] = jnp.where(turned, flip_some(top), top)
-            bottom = solved_at[t, pl.ds(k, n), 0, :] * (diffusion + flow_bottom)
-            down[line : line + n, :] = bottom
+        at = slice(k, k + n)
+        to_up = diffusion - advection * velocity_at[pl.ds(k, n), SUBLANES - 1, :]
+        to_down = diffusion + advection * velocity_at[pl.ds(k, n), 0, :]
+        top = solved_at[1, pl.ds(k, n), SUBLANES - 1, :] * to_up
+        up[at, :] = jnp.where(turned, flip_some(top), top)
+        down[at, :] = solved_at[1, pl.ds(k, n), 0, :] * to_down
+        for t in range(2):
+            edges[t, at, :] = solved_at[2 * t, pl.ds(k, n), SUBLANES - 1, :] * to_up
+            edges[2 + t, at, :] = solved_at[2 * t, pl.ds(k, n), 0, :] * to_down
     for store in stores:
         store.wait()
 
 
-def transport_kernel(
-    seam, solved, velocity_x, velocity_y, wet, fields, below, above, result, surface,
-    solved_at, x_at, y_at, result_at, sems, out_sems,
-):
+def inside_kernel(solved, velocity_x, velocity_y, wet, fields, result, surface):
     levels = velocity_x.shape[0]
     width = wet.shape[1]
-    chunks = chunks_of(levels, SUBLANES)
-    loads = []
-    for i, (k, n) in enumerate(chunks):
-        at = pl.ds(k, n)
-        loads.append((
-            pltpu.make_async_copy(solved.at[:, at], solved_at.at[:, at], sems.at[0, i]),
-            pltpu.make_async_copy(velocity_x.at[at], x_at.at[at], sems.at[1, i]),
-            pltpu.make_async_copy(velocity_y.at[at], y_at.at[at], sems.at[2, i]),
-        ))
-    for group in loads:
-        for load in group:
-            load.start()
-
-    turned = seam[0] == 1
     depth = wet[...]
-    s = fields[:SUBLANES, :]
+    s = fields[...]
     surface[...] = s
-    south_s = fields[SUBLANES : SUBLANES + 1, :]
-    north_s = fields[SUBLANES + 1 : SUBLANES + 2, :]
-    depth_south = depth[:1, :]
-    depth_north = depth[SUBLANES - 1 :, :]
     row = lax.broadcasted_iota(jnp.int32, depth.shape, 0)
     is_south = row == 0
     is_north = row == SUBLANES - 1
 
     def level(k, _):
-        flow_x = advection * x_at[k]
-        flow_y = advection * y_at[k]
+        flow_x = advection * velocity_x[k]
+        flow_y = advection * velocity_y[k]
         to_west = diffusion + flow_x
         to_east = diffusion - flow_x
         to_south = jnp.where(is_south, 0.0, diffusion + flow_y)
         to_north = jnp.where(is_north, 0.0, diffusion - flow_y)
         is_wet = k < depth
         for t in range(2):
-            x = solved_at[t, k]
+            x = solved[t, k]
             if t == 0:
-                x = x + s * solved_at[2, k]
+                x = x + s * solved[2, k]
             eastern = pltpu.roll(x * to_west, width - 1, 1)
             western = pltpu.roll(x * to_east, 1, 1)
             northern = pltpu.roll(x * to_south, SUBLANES - 1, 0)
             southern = pltpu.roll(x * to_north, 1, 0)
             value = (1.0 - 4.0 * diffusion) * x + ((eastern + western) + (northern + southern))
-            result_at[t, k] = jnp.where(is_wet, value, 0.0)
+            result[t, k] = jnp.where(is_wet, value, 0.0)
         return 0
 
+    lax.fori_loop(0, levels, level, 0, unroll=5)
+
+
+def rim_kernel(seam, inside, wet, south0, north0, south1, north1, result, result_at, out_sems):
+    levels = inside.shape[1]
+    width = wet.shape[1]
+    turned = seam[0] == 1
+    depth_south = wet[:1, :]
+    depth_north = wet[SUBLANES - 1 :, :]
     stores = []
-    for i, (k, n) in enumerate(chunks):
-        for load in loads[i]:
-            load.wait()
-        lax.fori_loop(k, k + n, level, 0, unroll=2)
+    for i, (k, n) in enumerate(chunks_of(levels, SUBLANES)):
+        at = pl.ds(k, n)
         index = k + lax.broadcasted_iota(jnp.int32, (n, width), 0)
-        for t in range(2):
-            line = line_of(t, k, levels)
-            south = below[line : line + n, :]
-            north = above[line : line + n, :]
-            if t == 0:
-                line = line_of(2, k, levels)
-                south = south + south_s * below[line : line + n, :]
-                beyond = above[line : line + n, :]
-                north = jnp.where(turned, flip_some(north), north)
-                north = north + north_s * jnp.where(turned, flip_some(beyond), beyond)
-            else:
-                north = jnp.where(turned, flip_some(north), north)
-            at = pl.ds(k, n)
+        result_at[:, at] = inside[:, at]
+        for t, (south_from, north_from) in enumerate(((south0, north0), (south1, north1))):
+            south = south_from[k : k + n, :]
+            north = north_from[k : k + n, :]
+            north = jnp.where(turned, flip_some(north), north)
             result_at[t, at, 0, :] += jnp.where(index < depth_south, south, 0.0)
             result_at[t, at, SUBLANES - 1, :] += jnp.where(index < depth_north, north, 0.0)
-        stores.append(
-            pltpu.make_async_copy(
-                result_at.at[:, pl.ds(k, n)], result.at[:, pl.ds(k, n)], out_sems.at[i]
-            )
-        )
+        stores.append(pltpu.make_async_copy(result_at.at[:, at], result.at[:, at], out_sems.at[i]))
         stores[-1].start()
     for store in stores:
         store.wait()
@@ -409,14 +395,14 @@
     downward = [(j, i) for i, j in upward]
     tile = jax.ShapeDtypeStruct((rows, width), f32)
     ext = jax.ShapeDtypeStruct((ITERS, 2 * rows, width), f32)
-    lines = -(-3 * levels // SUBLANES) * SUBLANES
+    lines = -(-levels // SUBLANES) * SUBLANES
     line = jax.ShapeDtypeStruct((lines, width), f32)
 
-    up, down = pl.pallas_call(
+    up, down, mark = pl.pallas_call(
         outer_kernel,
-        out_shape=(tile, tile),
+        out_shape=(tile, tile, pltpu.HBM((rows, LANES), f32)),
         in_specs=[SMEM, VMEM, VMEM],
-        out_specs=(VMEM, VMEM),
+        out_specs=(VMEM, VMEM, HBM),
         name="outer_rows",
     )(seam_codes, eta_adjoint, surface_damping)
     below = lax.ppermute(up, "face", upward)
@@ -424,18 +410,25 @@
 
     cube = pltpu.VMEM((levels, rows, width), f32)
     parts = len(chunks_of(levels, CHUNK))
-    solved, up, down = pl.pallas_call(
+    solved, up1, down1, edges = pl.pallas_call(
         column_kernel,
-        out_shape=(jax.ShapeDtypeStruct((3, levels, rows, width), f32), line, line),
-        in_specs=[SMEM, SMEM, HBM, HBM, HBM, VMEM, HBM],
-        out_specs=(HBM, VMEM, VMEM),
+        out_shape=(
+            pltpu.HBM((3, levels, rows, width), f32),
+            line,
+            line,
+            jax.ShapeDtypeStruct((4, lines, width), f32),
+        ),
+        in_specs=[SMEM] + [HBM] * 6,
+        out_specs=(HBM, VMEM, VMEM, VMEM),
         scratch_shapes=[
+            pltpu.SMEM((levels,), f32),
+            pltpu.VMEM((rows, width), jnp.int32),
             pltpu.VMEM((tracers, levels, rows, width), f32),
             cube,
             cube,
             pltpu.VMEM((3, levels, rows, width), f32),
             cube,
-            pltpu.SemaphoreType.DMA((3, parts)),
+            pltpu.SemaphoreType.DMA((3, max(parts, 3))),
             pltpu.SemaphoreType.DMA((parts,)),
         ],
         compiler_params=PARAMS,
@@ -443,10 +436,7 @@
         name="columns",
     )(
         seam_codes,
-        thickness,
-        *(pltpu.with_memory_space_constraint(x, pltpu.HBM) for x in (tracer_adjoint, mixing, velocity_y)),
-        wet_levels,
-        up,
+        *map(in_hbm, (thickness, tracer_adjoint, mixing, velocity_y, wet_levels, mark)),
     )
 
     basis, sums = pl.pallas_call(
@@ -457,55 +447,65 @@
         compiler_params=PARAMS,
         name="surface_basis",
     )(seam_codes, eta_adjoint, surface_damping, below, above)
-    sums, up, down = lax.optimization_barrier((sums, up, down))
+    sums, up1, down1 = lax.optimization_barrier((sums, up1, down1))
     sums = lax.all_to_all(sums, "face", 0, 0)
-    below = lax.ppermute(up, "face", upward)
-    above = lax.ppermute(down, "face", downward)
-
-    fields, sound = pl.pallas_call(
+    south1 = lax.ppermute(up1, "face", upward)
+    north1 = lax.ppermute(down1, "face", downward)
+    sums, south1, north1 = lax.optimization_barrier((sums, south1, north1))
+
+    fields, up0, down0, sound = pl.pallas_call(
         surface_kernel,
-        out_shape=(
-            jax.ShapeDtypeStruct((2 * rows, width), f32),
-            jax.ShapeDtypeStruct((1,), jnp.int32),
-        ),
-        in_specs=[VMEM, VMEM],
-        out_specs=(VMEM, SMEM),
+        out_shape=(tile, line, line, jax.ShapeDtypeStruct((1,), jnp.int32)),
+        in_specs=[SMEM, VMEM, VMEM, VMEM],
+        out_specs=(VMEM, VMEM, VMEM, SMEM),
         compiler_params=PARAMS,
         name="surface",
-    )(sums, basis)
-
-    def by_moments(fields):
-        return fields
-
-    def by_steps(fields):
+    )(seam_codes, sums, basis, edges)
+
+    def by_moments(fields, up0, down0):
+        return fields, up0, down0
+
+    def by_steps(fields, up0, down0):
         turned = seam_codes[0] == 1
         surface = stepwise_surface(eta_adjoint, surface_damping, turned)
-        top, bottom = surface[-1:], surface[:1]
-        top = jnp.where(turned, jnp.flip(top, -1), top)
-        south = lax.ppermute(top, "face", upward)
-        north = lax.ppermute(bottom, "face", downward)
-        north = jnp.where(turned, jnp.flip(north, -1), north)
-        return jnp.concatenate([surface, south, north, fields[rows + 2 :]], axis=0)
-
-    fields = lax.cond(sound[0] == 1, by_moments, by_steps, fields)
+        up0, down0 = pl.pallas_call(
+            outer_lines,
+            out_shape=(line, line),
+            in_specs=[SMEM, VMEM, VMEM],
+            out_specs=(VMEM, VMEM),
+            compiler_params=PARAMS,
+            name="outer_lines",
+        )(seam_codes, surface, edges)
+        return surface, up0, down0
+
+    fields, up0, down0 = lax.cond(sound[0] == 1, by_moments, by_steps, fields, up0, down0)
+    south0 = lax.ppermute(up0, "face", upward)
+    north0 = lax.ppermute(down0, "face", downward)
 
     parts = len(chunks_of(levels, SUBLANES))
-    return pl.pallas_call(
-        transport_kernel,
+    inside, surface = pl.pallas_call(
+        inside_kernel,
         out_shape=(jax.ShapeDtypeStruct((tracers, levels, rows, width), f32), tile),
-        in_specs=[SMEM, HBM, HBM, HBM] + [VMEM] * 4,
-        out_specs=(HBM, VMEM),
+        in_specs=[VMEM] * 5,
+        out_specs=(VMEM, VMEM),
+        compiler_params=PARAMS,
+        cost_estimate=pl.CostEstimate(flops=20000000, bytes_accessed=13000000, transcendentals=0),
+        name="inside",
+    )(solved, velocity_x, velocity_y, wet_levels, fields)
+
+    result = pl.pallas_call(
+        rim_kernel,
+        out_shape=jax.ShapeDtypeStruct((tracers, levels, rows, width), f32),
+        in_specs=[SMEM] + [VMEM] * 6,
+        out_specs=HBM,
         scratch_shapes=[
-            pltpu.VMEM((3, levels, rows, width), f32),
-            cube,
-            cube,
             pltpu.VMEM((tracers, levels, rows, width), f32),
-            pltpu.SemaphoreType.DMA((3, parts)),
             pltpu.SemaphoreType.DMA((parts,)),
         ],
         compiler_params=PARAMS,
-        name="transport",
-    )(seam_codes, solved, velocity_x, velocity_y, wet_levels, fields, below, above)
+        name="rims",
+    )(seam_codes, inside, wet_levels, south0, north0, south1, north1)
+    return result, surface
 
 
 def solution(mesh):

time: 47.9 us -> 51.8 us (1.081)
  blocking collectives: 11.2 us -> 0 us
  starting transfers between devices: 10.1 us -> 17.2 us
  waiting for transfers between devices: 0.01 us -> 6.87 us
  local copies, waits for them, and re-layouts: 6.75 us -> 7.32 us
    all_to_all x1 -> x0, blocking collectives: 11.2 us -> none  [shards(): sums = lax.all_to_all(sums, 'face', 0, 0)]
    ppermute x0 -> x4, starting transfers between devices: none -> 8.2 us  [the longest x1 4.44 us: shards(): north1 = lax.ppermute(down1, 'face', downward)]
    all_to_all x0 -> x1, waiting for transfers between devices: none -> 6.86 us  [shards(): sums = lax.all_to_all(sums, 'face', 0, 0)]
    ppermute x2 -> x1, starting transfers between devices: 10 us -> 5.07 us  [shards(): above = lax.ppermute(down, 'face', downward)]
    all_to_all x0 -> x1, starting transfers between devices: none -> 3.48 us  [shards(): sums = lax.all_to_all(sums, 'face', 0, 0)]
    cond x0 -> x2, local copies, waits for them, and re-layouts: none -> 1.88 us
    unnamed x20, local copies, waits for them, and re-layouts: 6.75 us -> 5.44 us
    pallas_call x1, Pallas kernels: 0.46 us -> 1.08 us  [shards(): pl.pallas_call(basis_kernel, out_shape=(ext, jax.ShapeDtypeStruct((count,...]
  transfers between devices with their start and end apart: 4 -> 7, of which waited for: 0 -> 1; matrix products, arithmetic and copies ran while one was open for 0% -> 0% of each run, Pallas kernels for 15% -> 19%
where the time goes in v4:
time: 51.8 us; the launch traced here: 51.3 us
  Pallas kernels  17.8 us (34%)
  starting transfers between devices  17.2 us (33%)
  local copies, waits for them, and re-layouts  7.32 us (14%)
  waiting for transfers between devices  6.87 us (13%)
  between operations  2.03 us (4%)
    all_to_all x1, waiting for transfers between devices, shards(): sums = lax.all_to_all(sums, 'face', 0, 0)  6.86 us
    pallas_call x1, Pallas kernels, shards(): pl.pallas_call(column_kernel, out_shape=(pltpu.HBM((3, levels, rows, widt...  6.2 us
    unnamed x20, local copies, waits for them, and re-layouts  5.44 us
    ppermute x1, starting transfers between devices, shards(): above = lax.ppermute(down, 'face', downward)  5.07 us
    ppermute x1, starting transfers between devices, shards(): north1 = lax.ppermute(down1, 'face', downward)  4.44 us
    ppermute x1, starting transfers between devices, shards(): north0 = lax.ppermute(down0, 'face', downward)  3.75 us
    pallas_call x1, Pallas kernels, shards(): pl.pallas_call(inside_kernel, out_shape=(jax.ShapeDtypeStruct((tracers, l...  3.75 us
    all_to_all x1, starting transfers between devices, shards(): sums = lax.all_to_all(sums, 'face', 0, 0)  3.48 us
  transfers between devices with their start and end apart: 7, of which 1 were waited for; matrix products, arithmetic and copies ran while one was open for 0% of the time, Pallas kernels for 19%

profile of v4, /device:TPU:0, one launch (start us, length us, event | category | flops | bytes accessed | tf_op | source)
XLA Modules:
  0.0 51.3 jit_solution(9335966238362912475)
XLA Ops:
  1.3 1.4 %outer_rows.1 = (f32[8,1024]{1,0:T(8,128)}, f32[8,1024]{1,0:T(8,128)}, f32[8,128]{1,0:T(8,128)}) custom-call(s32[1]{0:T(128)S(6)} %copy.17.seam, f32[8,1024]{1,0:T(8,128)} %eta.3, f32[8,1024]{1,0:T(8,128)} %damping.3), custom_call_target="tpu_custom_call" | custom-call | tf_op jit(solution)/shard_map/outer_rows/pallas_call | solution.py:401
  2.7 0.5 collective-permute-start.8
  3.1 5.1 %collective-permute-start.9 = (f32[8,1024]{1,0:T(8,128)}, f32[8,1024]{1,0:T(8,128)S(1)}, u32[]{:S(2)}, u32[]{:S(2)}) collective-permute-start(f32[8,1024]{1,0:T(8,128)} %get-tuple-element.49), channel_id=1, source_target_pairs={{1,0},{2,1},{3,2},{4,3},{5,4},{6,5},{7,6},{8,7},{9,8},{10,9},{11,1... | collective-permute-start | bytes 98312 | tf_op jit(solution)/shard_map/ppermute | solution.py:409
  8.2 0.0 copy-start.6
  8.2 0.0 copy-start.7
  8.2 6.2 %columns.1 = (f32[3,50,8,1024]{3,2,1,0:T(8,128)}, f32[56,1024]{1,0:T(8,128)}, f32[56,1024]{1,0:T(8,128)}, f32[4,56,1024]{2,1,0:T(8,128)}) custom-call(s32[1]{0:T(128)S(6)} %copy.17.seam, f32[50]{0:T(128)} %thickness_from.1, f32[2,50,8,1024]{3,2,1,0:T(8,128)} %tracer.1, f32[49,8,1024]{2,1,0:T(8,128)} %mixing.1, f32[50,8,1024]{2,1,0:T(8,128)} %velocity_y.3, ...), custom_call_target="tpu_custom_call" | custom-call | flops 40000000 | bytes 13000000 | tf_op jit(solution)/shard_map/columns/pallas_call | solution.py:413
  14.4 0.0 copy-start
  14.4 0.0 copy-start.2
  14.5 0.0 copy-start.3
  14.5 0.0 collective-permute-done.8.below
  14.5 0.0 collective-permute-done.9.above
  14.5 0.0 copy-done.6
  14.5 0.0 copy-done.7
  14.5 1.1 %surface_basis.1 = (f32[4,16,1024]{2,1,0:T(8,128)S(1)}, f32[16,8,128]{2,1,0:T(8,128)}) custom-call(s32[1]{0:T(128)S(6)} %copy.17.seam, f32[8,1024]{1,0:T(8,128)S(1)} %copy-done.6, f32[8,1024]{1,0:T(8,128)S(1)} %copy-done.7, f32[8,1024]{1,0:T(8,128)S(1)} %collective-permute-done.8.below, f32[8,1024]{1,0:T(8,128)S(1)} %collective-permute-done.9.above), custom_call_target="tpu_custom_call" | custom-call | tf_op jit(solution)/shard_map/surface_basis/pallas_call | solution.py:442
  15.6 0.0 copy-start.4
  15.6 0.7 %copy-done.4 = f32[4,16,1024]{2,1,0:T(8,128)} copy-done((f32[4,16,1024]{2,1,0:T(8,128)}, f32[4,16,1024]{2,1,0:T(8,128)S(1)}, u32[]{:S(2)}) %copy-start.4) | copy-done | bytes 262168
  16.3 0.0 collective-permute-start.10
  16.3 4.4 %collective-permute-start.11 = (f32[56,1024]{1,0:T(8,128)}, f32[56,1024]{1,0:T(8,128)}, u32[]{:S(2)}, u32[]{:S(2)}) collective-permute-start(f32[56,1024]{1,0:T(8,128)} %get-tuple-element.55), channel_id=1, source_target_pairs={{1,0},{2,1},{3,2},{4,3},{5,4},{6,5},{7,6},{8,7},{9,8},{10,9},{11,1... | collective-permute-start | bytes 688136 | tf_op jit(solution)/shard_map/ppermute | solution.py:453
  20.7 3.5 %all-to-all-start = ((f32[16,8,128]{2,1,0:T(8,128)}), f32[16,8,128]{2,1,0:T(8,128)S(1)}, u32[]{:S(2)}, u32[]{:S(2)}) async-start(f32[16,8,128]{2,1,0:T(8,128)} %get-tuple-element.53), calls=%async_computation | async-start | bytes 131072 | tf_op jit(solution)/shard_map/all_to_all | solution.py:451
  24.2 6.9 %all-to-all-done.sums = f32[16,8,128]{2,1,0:T(8,128)S(1)} async-done(((f32[16,8,128]{2,1,0:T(8,128)}), f32[16,8,128]{2,1,0:T(8,128)S(1)}, u32[]{:S(2)}, u32[]{:S(2)}) %all-to-all-start) | async-done | bytes 65568 | tf_op jit(solution)/shard_map/all_to_all | solution.py:451
  31.1 0.0 collective-permute-done.10.south1
  31.1 0.0 collective-permute-done.11.north1
  31.1 0.0 copy-start.5
  31.1 0.9 %copy-done.5 = f32[4,16,1024]{2,1,0:T(8,128)S(1)} copy-done((f32[4,16,1024]{2,1,0:T(8,128)S(1)}, f32[4,16,1024]{2,1,0:T(8,128)}, u32[]{:S(2)}) %copy-start.5) | copy-done | bytes 262168
  32.0 2.4 %surface.1 = (f32[8,1024]{1,0:T(8,128)}, f32[56,1024]{1,0:T(8,128)}, f32[56,1024]{1,0:T(8,128)}, s32[1]{0:T(128)}) custom-call(s32[1]{0:T(128)S(6)} %copy.17.seam, f32[16,8,128]{2,1,0:T(8,128)S(1)} %all-to-all-done.sums, f32[4,16,1024]{2,1,0:T(8,128)S(1)} %copy-done.5, f32[4,56,1024]{2,1,0:T(8,128)} %get-tuple-element.58.edges), custom_call_target="tpu_custom_call" | custom-call | tf_op jit(solution)/shard_map/surface/pallas_call | solution.py:456
  35.1 1.9 %conditional.1 = (f32[8,1024]{1,0:T(8,128)}, f32[56,1024]{1,0:T(8,128)S(1)}, f32[56,1024]{1,0:T(8,128)S(1)}) conditional(s32[]{:T(128)} %bitcast.1, (f32[8,1024]{1,0:T(8,128)S(1)}, f32[8,1024]{1,0:T(8,128)S(1)}, s32[1]{0:T(128)}, f32[4,56,1024]{2,1,0:T(8,128)}) %tuple.46, (f32[8,1024]{1,0:T(8,128)}, f32[56,1024]{1,0:T(8,128)}, ...), branch_computations={%region_0.17_spmd, %region_17.18_spmd} | conditional | flops 671752 | bytes 3113581 | solution.py:481
  35.1 0.9 %copy.15 = f32[56,1024]{1,0:T(8,128)S(1)} copy(f32[56,1024]{1,0:T(8,128)} %get-tuple-element.117) | data formatting | bytes 458752 | tf_op jit(solution)/shard_map/cond
  36.1 0.9 %copy.16 = f32[56,1024]{1,0:T(8,128)S(1)} copy(f32[56,1024]{1,0:T(8,128)} %get-tuple-element.118) | data formatting | bytes 458752 | tf_op jit(solution)/shard_map/cond
  37.0 0.0 copy-start.9
  37.0 0.7 %copy-done.9 = f32[56,1024]{1,0:T(8,128)} copy-done((f32[56,1024]{1,0:T(8,128)}, f32[56,1024]{1,0:T(8,128)S(1)}, u32[]{:S(2)}) %copy-start.9) | copy-done | bytes 229400
  37.7 0.0 copy-start.10
  37.7 0.0 collective-permute-start.12
  37.7 0.7 %copy-done.10 = f32[56,1024]{1,0:T(8,128)} copy-done((f32[56,1024]{1,0:T(8,128)}, f32[56,1024]{1,0:T(8,128)S(1)}, u32[]{:S(2)}) %copy-start.10) | copy-done | bytes 229400
  38.4 3.8 %collective-permute-start.13 = (f32[56,1024]{1,0:T(8,128)}, f32[56,1024]{1,0:T(8,128)S(1)}, u32[]{:S(2)}, u32[]{:S(2)}) collective-permute-start(f32[56,1024]{1,0:T(8,128)} %copy-done.10), channel_id=1, source_target_pairs={{1,0},{2,1},{3,2},{4,3},{5,4},{6,5},{7,6},{8,7},{9,8},{10,9},{11,1... | collective-permute-start | bytes 688136 | tf_op jit(solution)/shard_map/ppermute | solution.py:483
  42.2 0.0 copy-done
  42.2 0.0 copy-done.2
  42.2 0.0 copy-done.3
  42.2 0.0 copy-start.1
  42.2 2.4 %copy-done.1 = f32[3,50,8,1024]{3,2,1,0:T(8,128)S(1)} copy-done((f32[3,50,8,1024]{3,2,1,0:T(8,128)S(1)}, f32[3,50,8,1024]{3,2,1,0:T(8,128)}, u32[]{:S(2)}) %copy-start.1) | copy-done | bytes 4915224
  44.6 3.7 %inside.1 = (f32[2,50,8,1024]{3,2,1,0:T(8,128)S(1)}, f32[8,1024]{1,0:T(8,128)}) custom-call(f32[3,50,8,1024]{3,2,1,0:T(8,128)S(1)} %copy-done.1, f32[50,8,1024]{2,1,0:T(8,128)S(1)} %copy-done.2, f32[50,8,1024]{2,1,0:T(8,128)S(1)} %copy-done, s32[8,1024]{1,0:T(8,128)S(1)} %copy-done.3, f32[8,1024]{1,0:T(8,128)} %get-tuple-element.63.fields), custom_call_target="tpu_custom_call" | custom-call | flops 20000000 | bytes 13000000 | tf_op jit(solution)/shard_map/inside/pallas_call | solution.py:486
  48.3 0.0 collective-permute-done.12.south0
  48.3 0.0 collective-permute-done.13.north0
  48.3 3.0 %rims.1 = f32[2,50,8,1024]{3,2,1,0:T(8,128)} custom-call(s32[1]{0:T(128)S(6)} %copy.17.seam, f32[2,50,8,1024]{3,2,1,0:T(8,128)S(1)} %get-tuple-element.64.inside, s32[8,1024]{1,0:T(8,128)S(1)} %copy-done.3, f32[56,1024]{1,0:T(8,128)S(1)} %collective-permute-done.12.south0, f32[56,1024]{1,0:T(8,128)S(1)} %collective-permute-done.13.north0, ...), custom_call_target="tpu_custom_call" | custom-call | tf_op jit(solution)/shard_map/rims/pallas_call | solution.py:496
Async XLA Ops:
  2.7 11.8 %collective-permute-start.8 = (f32[8,1024]{1,0:T(8,128)}, f32[8,1024]{1,0:T(8,128)S(1)}, u32[]{:S(2)}, u32[]{:S(2)}) collective-permute-start(f32[8,1024]{1,0:T(8,128)} %get-tuple-element.48), channel_id=1, source_target_pairs={{0,1},{1,2},{2,3},{3,4},{4,5},{5,6},{6,7},{7,8},{8,9},{9,10},{10,1... | collective-permute-start | bytes 98312 | tf_op jit(solution)/shard_map/ppermute | solution.py:408
  3.1 11.3 %collective-permute-start.9 = (f32[8,1024]{1,0:T(8,128)}, f32[8,1024]{1,0:T(8,128)S(1)}, u32[]{:S(2)}, u32[]{:S(2)}) collective-permute-start(f32[8,1024]{1,0:T(8,128)} %get-tuple-element.49), channel_id=1, source_target_pairs={{1,0},{2,1},{3,2},{4,3},{5,4},{6,5},{7,6},{8,7},{9,8},{10,9},{11,1... | collective-permute-start | bytes 98312 | tf_op jit(solution)/shard_map/ppermute | solution.py:409
  8.2 6.3 %copy-start.6 = (f32[8,1024]{1,0:T(8,128)S(1)}, f32[8,1024]{1,0:T(8,128)}, u32[]{:S(2)}) copy-start(f32[8,1024]{1,0:T(8,128)} %eta.3) | copy-start | bytes 98308
  8.2 6.3 %copy-start.7 = (f32[8,1024]{1,0:T(8,128)S(1)}, f32[8,1024]{1,0:T(8,128)}, u32[]{:S(2)}) copy-start(f32[8,1024]{1,0:T(8,128)} %damping.3) | copy-start | bytes 98308
  14.4 27.7 %copy-start = (f32[50,8,1024]{2,1,0:T(8,128)S(1)}, f32[50,8,1024]{2,1,0:T(8,128)}, u32[]{:S(2)}) copy-start(f32[50,8,1024]{2,1,0:T(8,128)} %velocity_y.3) | copy-start | bytes 4915204
  14.4 27.7 %copy-start.2 = (f32[50,8,1024]{2,1,0:T(8,128)S(1)}, f32[50,8,1024]{2,1,0:T(8,128)}, u32[]{:S(2)}) copy-start(f32[50,8,1024]{2,1,0:T(8,128)} %velocity_x.1) | copy-start | bytes 4915204
  14.5 27.7 %copy-start.3 = (s32[8,1024]{1,0:T(8,128)S(1)}, s32[8,1024]{1,0:T(8,128)}, u32[]{:S(2)}) copy-start(s32[8,1024]{1,0:T(8,128)} %wet.5) | copy-start | bytes 98308
  15.6 0.7 %copy-start.4 = (f32[4,16,1024]{2,1,0:T(8,128)}, f32[4,16,1024]{2,1,0:T(8,128)S(1)}, u32[]{:S(2)}) copy-start(f32[4,16,1024]{2,1,0:T(8,128)S(1)} %get-tuple-element.57.basis) | copy-start | bytes 786436
  16.3 14.8 %collective-permute-start.10 = (f32[56,1024]{1,0:T(8,128)}, f32[56,1024]{1,0:T(8,128)}, u32[]{:S(2)}, u32[]{:S(2)}) collective-permute-start(f32[56,1024]{1,0:T(8,128)} %get-tuple-element.54), channel_id=1, source_target_pairs={{0,1},{1,2},{2,3},{3,4},{4,5},{5,6},{6,7},{7,8},{8,9},{9,10},{10,1... | collective-permute-start | bytes 688136 | tf_op jit(solution)/shard_map/ppermute | solution.py:452
  16.3 14.8 %collective-permute-start.11 = (f32[56,1024]{1,0:T(8,128)}, f32[56,1024]{1,0:T(8,128)}, u32[]{:S(2)}, u32[]{:S(2)}) collective-permute-start(f32[56,1024]{1,0:T(8,128)} %get-tuple-element.55), channel_id=1, source_target_pairs={{1,0},{2,1},{3,2},{4,3},{5,4},{6,5},{7,6},{8,7},{9,8},{10,9},{11,1... | collective-permute-start | bytes 688136 | tf_op jit(solution)/shard_map/ppermute | solution.py:453
  20.7 10.4 %all-to-all-start = ((f32[16,8,128]{2,1,0:T(8,128)}), f32[16,8,128]{2,1,0:T(8,128)S(1)}, u32[]{:S(2)}, u32[]{:S(2)}) async-start(f32[16,8,128]{2,1,0:T(8,128)} %get-tuple-element.53), calls=%async_computation | async-start | bytes 131072 | tf_op jit(solution)/shard_map/all_to_all | solution.py:451
  31.1 1.0 %copy-start.5 = (f32[4,16,1024]{2,1,0:T(8,128)S(1)}, f32[4,16,1024]{2,1,0:T(8,128)}, u32[]{:S(2)}) copy-start(f32[4,16,1024]{2,1,0:T(8,128)} %copy-done.4) | copy-start | bytes 786436
  37.0 0.7 %copy-start.9 = (f32[56,1024]{1,0:T(8,128)}, f32[56,1024]{1,0:T(8,128)S(1)}, u32[]{:S(2)}) copy-start(f32[56,1024]{1,0:T(8,128)S(1)} %get-tuple-element.65) | copy-start | bytes 688132
  37.7 0.7 %copy-start.10 = (f32[56,1024]{1,0:T(8,128)}, f32[56,1024]{1,0:T(8,128)S(1)}, u32[]{:S(2)}) copy-start(f32[56,1024]{1,0:T(8,128)S(1)} %get-tuple-element.66) | copy-start | bytes 688132
  37.7 10.6 %collective-permute-start.12 = (f32[56,1024]{1,0:T(8,128)}, f32[56,1024]{1,0:T(8,128)S(1)}, u32[]{:S(2)}, u32[]{:S(2)}) collective-permute-start(f32[56,1024]{1,0:T(8,128)} %copy-done.9), channel_id=1, source_target_pairs={{0,1},{1,2},{2,3},{3,4},{4,5},{5,6},{6,7},{7,8},{8,9},{9,10},{10,1... | collective-permute-start | bytes 688136 | tf_op jit(solution)/shard_map/ppermute | solution.py:482
  38.4 9.9 %collective-permute-start.13 = (f32[56,1024]{1,0:T(8,128)}, f32[56,1024]{1,0:T(8,128)S(1)}, u32[]{:S(2)}, u32[]{:S(2)}) collective-permute-start(f32[56,1024]{1,0:T(8,128)} %copy-done.10), channel_id=1, source_target_pairs={{1,0},{2,1},{3,2},{4,3},{5,4},{6,5},{7,6},{8,7},{9,8},{10,9},{11,1... | collective-permute-start | bytes 688136 | tf_op jit(solution)/shard_map/ppermute | solution.py:483
  42.2 2.4 %copy-start.1 = (f32[3,50,8,1024]{3,2,1,0:T(8,128)S(1)}, f32[3,50,8,1024]{3,2,1,0:T(8,128)}, u32[]{:S(2)}) copy-start(f32[3,50,8,1024]{3,2,1,0:T(8,128)} %get-tuple-element.47.solved) | copy-start | bytes 14745604

commit v5 on v4

--- a/solution.py
+++ b/solution.py
@@ -230,8 +230,7 @@
 
 def column_kernel(
     seam, thickness_from, tracer, mixing, velocity_y, wet, after, solved, up, down, edges,
-    thickness, depth_at, tracer_at, mixing_at, velocity_at, solved_at, ratio_at,
-    sems, out_sems,
+    thickness, depth_at, tracer_at, mixing_at, velocity_at, ratio_at, sems,
 ):
     levels = tracer.shape[1]
     chunks = chunks_of(levels, CHUNK)
@@ -271,9 +270,9 @@
         y1 = (tracer_at[1, k] + c_before * y1) * inverse
         y2 = (jnp.where(k < depth, th, 0.0) + c_before * y2) * inverse
         ratio_at[k] = g
-        solved_at[0, k] = y0
-        solved_at[1, k] = y1
-        solved_at[2, k] = y2
+        solved[0, k] = y0
+        solved[1, k] = y1
+        solved[2, k] = y2
         return c, g, y0, y1, y2
 
     carry = (zero,) * 5
@@ -282,7 +281,6 @@
         loads[i][1].wait()
         carry = lax.fori_loop(k, k + n, forward, carry, unroll=5)
 
-    stores = []
     carry = (zero,) * 3
     for i, (k, n) in reversed(list(enumerate(chunks))):
 
@@ -292,18 +290,12 @@
             g = ratio_at[level]
             after = []
             for t in range(3):
-                u = solved_at[t, level] + g * carry[t]
-                solved_at[t, level] = th * u
+                u = solved[t, level] + g * carry[t]
+                solved[t, level] = th * u
                 after.append(u)
             return tuple(after)
 
         carry = lax.fori_loop(0, n, backward, carry, unroll=5)
-        stores.append(
-            pltpu.make_async_copy(
-                solved_at.at[:, pl.ds(k, n)], solved.at[:, pl.ds(k, n)], out_sems.at[i]
-            )
-        )
-        stores[-1].start()
 
     velocity_load.wait()
     turned = seam[0] == 1
@@ -311,22 +303,19 @@
         at = slice(k, k + n)
         to_up = diffusion - advection * velocity_at[pl.ds(k, n), SUBLANES - 1, :]
         to_down = diffusion + advection * velocity_at[pl.ds(k, n), 0, :]
-        top = solved_at[1, pl.ds(k, n), SUBLANES - 1, :] * to_up
+        top = solved[1, pl.ds(k, n), SUBLANES - 1, :] * to_up
         up[at, :] = jnp.where(turned, flip_some(top), top)
-        down[at, :] = solved_at[1, pl.ds(k, n), 0, :] * to_down
+        down[at, :] = solved[1, pl.ds(k, n), 0, :] * to_down
         for t in range(2):
-            edges[t, at, :] = solved_at[2 * t, pl.ds(k, n), SUBLANES - 1, :] * to_up
-            edges[2 + t, at, :] = solved_at[2 * t, pl.ds(k, n), 0, :] * to_down
-    for store in stores:
-        store.wait()
-
-
-def inside_kernel(solved, velocity_x, velocity_y, wet, fields, result, surface):
+            edges[t, at, :] = solved[2 * t, pl.ds(k, n), SUBLANES - 1, :] * to_up
+            edges[2 + t, at, :] = solved[2 * t, pl.ds(k, n), 0, :] * to_down
+
+
+def inside_kernel(solved, velocity_x, velocity_y, wet, surface, result):
     levels = velocity_x.shape[0]
     width = wet.shape[1]
     depth = wet[...]
-    s = fields[...]
-    surface[...] = s
+    s = surface[...]
     row = lax.broadcasted_iota(jnp.int32, depth.shape, 0)
     is_south = row == 0
     is_north = row == SUBLANES - 1
@@ -394,7 +383,7 @@
     upward = [(i, (i + 1) % count) for i in range(count)]
     downward = [(j, i) for i, j in upward]
     tile = jax.ShapeDtypeStruct((rows, width), f32)
-    ext = jax.ShapeDtypeStruct((ITERS, 2 * rows, width), f32)
+    ext = pltpu.HBM((ITERS, 2 * rows, width), f32)
     lines = -(-levels // SUBLANES) * SUBLANES
     line = jax.ShapeDtypeStruct((lines, width), f32)
 
@@ -413,23 +402,21 @@
     solved, up1, down1, edges = pl.pallas_call(
         column_kernel,
         out_shape=(
-            pltpu.HBM((3, levels, rows, width), f32),
+            jax.ShapeDtypeStruct((3, levels, rows, width), f32),
             line,
             line,
             jax.ShapeDtypeStruct((4, lines, width), f32),
         ),
         in_specs=[SMEM] + [HBM] * 6,
-        out_specs=(HBM, VMEM, VMEM, VMEM),
+        out_specs=(VMEM, VMEM, VMEM, VMEM),
         scratch_shapes=[
             pltpu.SMEM((levels,), f32),
             pltpu.VMEM((rows, width), jnp.int32),
             pltpu.VMEM((tracers, levels, rows, width), f32),
             cube,
             cube,
-            pltpu.VMEM((3, levels, rows, width), f32),
             cube,
             pltpu.SemaphoreType.DMA((3, max(parts, 3))),
-            pltpu.SemaphoreType.DMA((parts,)),
         ],
         compiler_params=PARAMS,
         cost_estimate=pl.CostEstimate(flops=40000000, bytes_accessed=13000000, transcendentals=0),
@@ -453,7 +440,7 @@
     north1 = lax.ppermute(down1, "face", downward)
     sums, south1, north1 = lax.optimization_barrier((sums, south1, north1))
 
-    fields, up0, down0, sound = pl.pallas_call(
+    surface, up0, down0, sound = pl.pallas_call(
         surface_kernel,
         out_shape=(tile, line, line, jax.ShapeDtypeStruct((1,), jnp.int32)),
         in_specs=[SMEM, VMEM, VMEM, VMEM],
@@ -462,12 +449,44 @@
         name="surface",
     )(seam_codes, sums, basis, edges)
 
-    def by_moments(fields, up0, down0):
-        return fields, up0, down0
-
-    def by_steps(fields, up0, down0):
-        turned = seam_codes[0] == 1
-        surface = stepwise_surface(eta_adjoint, surface_damping, turned)
+    parts = len(chunks_of(levels, SUBLANES))
+
+    def inside_of(surface):
+        return pl.pallas_call(
+            inside_kernel,
+            out_shape=jax.ShapeDtypeStruct((tracers, levels, rows, width), f32),
+            in_specs=[VMEM] * 5,
+            out_specs=VMEM,
+            compiler_params=PARAMS,
+            cost_estimate=pl.CostEstimate(
+                flops=20000000, bytes_accessed=13000000, transcendentals=0
+            ),
+            name="inside",
+        )(solved, velocity_x, velocity_y, wet_levels, surface)
+
+    def with_rims(inside, south0, north0, south1, north1):
+        return pl.pallas_call(
+            rim_kernel,
+            out_shape=pltpu.HBM((tracers, levels, rows, width), f32),
+            in_specs=[SMEM] + [VMEM] * 6,
+            out_specs=HBM,
+            scratch_shapes=[
+                pltpu.VMEM((tracers, levels, rows, width), f32),
+                pltpu.SemaphoreType.DMA((parts,)),
+            ],
+            compiler_params=PARAMS,
+            name="rims",
+        )(seam_codes, inside, wet_levels, south0, north0, south1, north1)
+
+    south0 = lax.ppermute(up0, "face", upward)
+    north0 = lax.ppermute(down0, "face", downward)
+    inside = inside_of(surface)
+
+    def by_moments(surface, inside, south0, north0):
+        return with_rims(inside, south0, north0, south1, north1), surface
+
+    def by_steps(surface, inside, south0, north0):
+        surface = stepwise_surface(eta_adjoint, surface_damping, seam_codes[0] == 1)
         up0, down0 = pl.pallas_call(
             outer_lines,
             out_shape=(line, line),
@@ -476,36 +495,11 @@
             compiler_params=PARAMS,
             name="outer_lines",
         )(seam_codes, surface, edges)
-        return surface, up0, down0
-
-    fields, up0, down0 = lax.cond(sound[0] == 1, by_moments, by_steps, fields, up0, down0)
-    south0 = lax.ppermute(up0, "face", upward)
-    north0 = lax.ppermute(down0, "face", downward)
-
-    parts = len(chunks_of(levels, SUBLANES))
-    inside, surface = pl.pallas_call(
-        inside_kernel,
-        out_shape=(jax.ShapeDtypeStruct((tracers, levels, rows, width), f32), tile),
-        in_specs=[VMEM] * 5,
-        out_specs=(VMEM, VMEM),
-        compiler_params=PARAMS,
-        cost_estimate=pl.CostEstimate(flops=20000000, bytes_accessed=13000000, transcendentals=0),
-        name="inside",
-    )(solved, velocity_x, velocity_y, wet_levels, fields)
-
-    result = pl.pallas_call(
-        rim_kernel,
-        out_shape=jax.ShapeDtypeStruct((tracers, levels, rows, width), f32),
-        in_specs=[SMEM] + [VMEM] * 6,
-        out_specs=HBM,
-        scratch_shapes=[
-            pltpu.VMEM((tracers, levels, rows, width), f32),
-            pltpu.SemaphoreType.DMA((parts,)),
-        ],
-        compiler_params=PARAMS,
-        name="rims",
-    )(seam_codes, inside, wet_levels, south0, north0, south1, north1)
-    return result, surface
+        south0 = lax.ppermute(up0, "face", upward)
+        north0 = lax.ppermute(down0, "face", downward)
+        return with_rims(inside_of(surface), south0, north0, south1, north1), surface
+
+    return lax.cond(sound[0] == 1, by_moments, by_steps, surface, inside, south0, north0)
 
 
 def solution(mesh):

time: 51.8 us -> 48.9 us (0.944)
  blocking collectives: 0 us -> 9.47 us
  waiting for transfers between devices: 6.87 us -> 0.02 us
  local copies, waits for them, and re-layouts: 7.32 us -> 1.78 us
  Pallas kernels: 17.8 us -> 20.8 us
  starting transfers between devices: 17.2 us -> 14.5 us
    all_to_all x0 -> x1, blocking collectives: none -> 9.47 us  [shards(): sums = lax.all_to_all(sums, 'face', 0, 0)]
    all_to_all x1 -> x0, waiting for transfers between devices: 6.86 us -> none  [shards(): sums = lax.all_to_all(sums, 'face', 0, 0)]
    pallas_call x3, Pallas kernels: 12.9 us -> 17.4 us  [the longest x1 6.66 us: inside_of(): pl.pallas_call(inside_kernel, out_shape=jax.ShapeDtypeStruct((tracers, le...]
    unnamed x20 -> x16, local copies, waits for them, and re-layouts: 5.44 us -> 1.78 us
    all_to_all x1 -> x0, starting transfers between devices: 3.48 us -> none  [shards(): sums = lax.all_to_all(sums, 'face', 0, 0)]
    cond x2 -> x0, local copies, waits for them, and re-layouts: 1.88 us -> none
    pallas_call x1, Pallas kernels: 2.42 us -> 0.9 us  [shards(): pl.pallas_call(surface_kernel, out_shape=(tile, line, line, jax.ShapeDtyp...]
    ppermute x1, starting transfers between devices: 3.75 us -> 4.43 us  [shards(): north0 = lax.ppermute(down0, 'face', downward)]
  transfers between devices with their start and end apart: 7 -> 6, of which waited for: 1 -> 0; matrix products, arithmetic and copies ran while one was open for 0% -> 0% of each run, Pallas kernels for 19% -> 26%
where the time goes in v5:
time: 48.9 us; the launch traced here: 48.6 us
  Pallas kernels  20.8 us (43%)
  starting transfers between devices  14.5 us (30%)
  blocking collectives  9.47 us (19%)
  between operations  2.04 us (4%)
  local copies, waits for them, and re-layouts  1.78 us (4%)
    all_to_all x1, blocking collectives, shards(): sums = lax.all_to_all(sums, 'face', 0, 0)  9.47 us
    pallas_call x1, Pallas kernels, inside_of(): pl.pallas_call(inside_kernel, out_shape=jax.ShapeDtypeStruct((tracers, le...  6.66 us
    pallas_call x1, Pallas kernels, shards(): pl.pallas_call(column_kernel, out_shape=(jax.ShapeDtypeStruct((3, levels,...  6.16 us
    ppermute x1, starting transfers between devices, shards(): above = lax.ppermute(down, 'face', downward)  4.99 us
    pallas_call x1, Pallas kernels, with_rims(): pl.pallas_call(rim_kernel, out_shape=pltpu.HBM((tracers, levels, rows, wi...  4.62 us
    ppermute x1, starting transfers between devices, shards(): north1 = lax.ppermute(down1, 'face', downward)  4.44 us
    ppermute x1, starting transfers between devices, shards(): north0 = lax.ppermute(down0, 'face', downward)  4.43 us
    unnamed x16, local copies, waits for them, and re-layouts  1.78 us
  transfers between devices with their start and end apart: 6, of which 0 were waited for; matrix products, arithmetic and copies ran while one was open for 0% of the time, Pallas kernels for 26%

profile of v5, /device:TPU:0, one launch (start us, length us, event | category | flops | bytes accessed | tf_op | source)
XLA Modules:
  0.0 48.6 jit_solution(13193833859896121074)
XLA Ops:
  1.3 1.4 %outer_rows.1 = (f32[8,1024]{1,0:T(8,128)}, f32[8,1024]{1,0:T(8,128)}, f32[8,128]{1,0:T(8,128)}) custom-call(s32[1]{0:T(128)S(6)} %copy.17.seam, f32[8,1024]{1,0:T(8,128)} %eta.3, f32[8,1024]{1,0:T(8,128)} %damping.3), custom_call_target="tpu_custom_call" | custom-call | tf_op jit(solution)/shard_map/outer_rows/pallas_call | solution.py:390
  2.7 0.5 %collective-permute-start.10 = (f32[8,1024]{1,0:T(8,128)}, f32[8,1024]{1,0:T(8,128)S(1)}, u32[]{:S(2)}, u32[]{:S(2)}) collective-permute-start(f32[8,1024]{1,0:T(8,128)} %get-tuple-element.77), channel_id=1, source_target_pairs={{0,1},{1,2},{2,3},{3,4},{4,5},{5,6},{6,7},{7,8},{8,9},{9,10},{10,1... | collective-permute-start | bytes 98312 | tf_op jit(solution)/shard_map/ppermute | solution.py:397
  3.2 5.0 %collective-permute-start.11 = (f32[8,1024]{1,0:T(8,128)}, f32[8,1024]{1,0:T(8,128)S(1)}, u32[]{:S(2)}, u32[]{:S(2)}) collective-permute-start(f32[8,1024]{1,0:T(8,128)} %get-tuple-element.78), channel_id=1, source_target_pairs={{1,0},{2,1},{3,2},{4,3},{5,4},{6,5},{7,6},{8,7},{9,8},{10,9},{11,1... | collective-permute-start | bytes 98312 | tf_op jit(solution)/shard_map/ppermute | solution.py:398
  8.2 0.0 copy-start.3
  8.2 0.0 copy-start.5
  8.2 0.0 copy-start.1
  8.2 0.0 copy-start.2
  8.2 0.0 copy-start.10
  8.2 6.2 %columns.1 = (f32[3,50,8,1024]{3,2,1,0:T(8,128)}, f32[56,1024]{1,0:T(8,128)S(1)}, f32[56,1024]{1,0:T(8,128)S(1)}, f32[4,56,1024]{2,1,0:T(8,128)S(1)}) custom-call(s32[1]{0:T(128)S(6)} %copy.17.seam, f32[50]{0:T(128)} %thickness_from.1, f32[2,50,8,1024]{3,2,1,0:T(8,128)} %tracer.1, f32[49,8,1024]{2,1,0:T(8,128)} %mixing.1, f32[50,8,1024]{2,1,0:T(8,128)} %velocity_y.3, ...), custom_call_target="tpu_custom_call" | custom-call | flops 40000000 | bytes 13000000 | tf_op jit(solution)/shard_map/columns/pallas_call | solution.py:402
  14.4 0.0 collective-permute-done.10.below
  14.4 0.0 collective-permute-done.11.above
  14.4 0.0 copy-done.3
  14.4 0.0 copy-done.5
  14.5 1.1 %surface_basis.1 = (f32[4,16,1024]{2,1,0:T(8,128)}, f32[16,8,128]{2,1,0:T(8,128)S(1)}) custom-call(s32[1]{0:T(128)S(6)} %copy.17.seam, f32[8,1024]{1,0:T(8,128)S(1)} %copy-done.3, f32[8,1024]{1,0:T(8,128)S(1)} %copy-done.5, f32[8,1024]{1,0:T(8,128)S(1)} %collective-permute-done.10.below, f32[8,1024]{1,0:T(8,128)S(1)} %collective-permute-done.11.above), custom_call_target="tpu_custom_call" | custom-call | tf_op jit(solution)/shard_map/surface_basis/pallas_call | solution.py:429
  15.5 0.0 collective-permute-start.12
  15.5 4.4 %collective-permute-start.13 = (f32[56,1024]{1,0:T(8,128)S(1)}, f32[56,1024]{1,0:T(8,128)S(1)}, u32[]{:S(2)}, u32[]{:S(2)}) collective-permute-start(f32[56,1024]{1,0:T(8,128)S(1)} %get-tuple-element.85), channel_id=1, source_target_pairs={{1,0},{2,1},{3,2},{4,3},{5,4},{6,5},{7,6},{8,7},{9,8},{10,9},{11,1... | collective-permute-start | bytes 688136 | tf_op jit(solution)/shard_map/ppermute | solution.py:440
  20.0 9.5 %all_to_all.5.sums = f32[16,8,128]{2,1,0:T(8,128)S(1)} all-to-all(f32[16,8,128]{2,1,0:T(8,128)S(1)} %get-tuple-element.83), channel_id=1, replica_groups=mesh['ens'=2,'face'=16] {'face'}, dimensions={0} | all-to-all | bytes 131072 | tf_op jit(solution)/shard_map/all_to_all | solution.py:438
  29.4 0.0 collective-permute-done.12
  29.4 0.0 copy-start.6
  29.4 0.0 collective-permute-done.13
  29.5 0.0 copy-start.8
  29.5 0.7 %copy-done.6 = f32[56,1024]{1,0:T(8,128)} copy-done((f32[56,1024]{1,0:T(8,128)}, f32[56,1024]{1,0:T(8,128)S(1)}, u32[]{:S(2)}) %copy-start.6) | copy-done | bytes 229400
  30.1 0.1 copy-done.8
  30.3 0.0 copy-start
  30.3 0.9 %copy-done = f32[4,16,1024]{2,1,0:T(8,128)S(1)} copy-done((f32[4,16,1024]{2,1,0:T(8,128)S(1)}, f32[4,16,1024]{2,1,0:T(8,128)}, u32[]{:S(2)}) %copy-start) | copy-done | bytes 262168
  31.2 0.9 %surface.1 = (f32[8,1024]{1,0:T(8,128)}, f32[56,1024]{1,0:T(8,128)S(1)}, f32[56,1024]{1,0:T(8,128)S(1)}, s32[1]{0:T(128)}) custom-call(s32[1]{0:T(128)S(6)} %copy.17.seam, f32[16,8,128]{2,1,0:T(8,128)S(1)} %all_to_all.5.sums, f32[4,16,1024]{2,1,0:T(8,128)S(1)} %copy-done, f32[4,56,1024]{2,1,0:T(8,128)S(1)} %get-tuple-element.88.edges), custom_call_target="tpu_custom_call" | custom-call | tf_op jit(solution)/shard_map/surface/pallas_call | solution.py:443
  32.1 0.1 collective-permute-start.14
  32.2 4.4 %collective-permute-start.15 = (f32[56,1024]{1,0:T(8,128)S(1)}, f32[56,1024]{1,0:T(8,128)S(1)}, u32[]{:S(2)}, u32[]{:S(2)}) collective-permute-start(f32[56,1024]{1,0:T(8,128)S(1)} %get-tuple-element.95), channel_id=1, source_target_pairs={{1,0},{2,1},{3,2},{4,3},{5,4},{6,5},{7,6},{8,7},{9,8},{10,9},{11,1... | collective-permute-start | bytes 688136 | tf_op jit(solution)/shard_map/ppermute | solution.py:482
  37.3 0.0 copy-done.1
  37.3 0.0 copy-done.2
  37.3 0.0 copy-done.10
  37.3 6.7 %inside.3 = f32[2,50,8,1024]{3,2,1,0:T(8,128)} custom-call(f32[3,50,8,1024]{3,2,1,0:T(8,128)} %get-tuple-element.90.solved, f32[50,8,1024]{2,1,0:T(8,128)S(1)} %copy-done.2, f32[50,8,1024]{2,1,0:T(8,128)S(1)} %copy-done.1, s32[8,1024]{1,0:T(8,128)S(1)} %copy-done.10, f32[8,1024]{1,0:T(8,128)} %get-tuple-element.93.surface), custom_call_target="tpu_custom_call" | custom-call | flops 20000000 | bytes 13000000 | tf_op jit(solution)/shard_map/inside/pallas_call | solution.py:455
  44.0 0.0 collective-permute-done.14
  44.0 0.0 collective-permute-done.15
  44.0 4.6 %conditional.1 = (f32[8,1024]{1,0:T(8,128)}, f32[2,50,8,1024]{3,2,1,0:T(8,128)}) conditional(s32[]{:T(128)} %bitcast.1, (f32[8,1024]{1,0:T(8,128)S(1)}, f32[8,1024]{1,0:T(8,128)S(1)}, s32[1]{0:T(128)}, f32[3,50,8,1024]{3,2,1,0:T(8,128)}, f32[50,8,1024]{2,1,0:T(8,128)S(1)}, /*index=5*/f32[50,8,1024]{2,1,0:T(8,128)S(1)}, s32[8,1024]{1,0:T(8,128)S(1)}, ...), branch_computations={%region_0.17_spmd, %region_17.18_spmd} | conditional | flops 20671752 | bytes 23322668 | solution.py:502
  44.0 4.6 %rims.3 = f32[2,50,8,1024]{3,2,1,0:T(8,128)} custom-call(s32[1]{0:T(128)} %get-tuple-element.48.seam, f32[2,50,8,1024]{3,2,1,0:T(8,128)} %get-tuple-element.49.inside, s32[8,1024]{1,0:T(8,128)S(1)} %get-tuple-element.50.wet, f32[56,1024]{1,0:T(8,128)S(1)} %get-tuple-element.51.south0, f32[56,1024]{1,0:T(8,128)S(1)} %get-tuple-element.52.north0, ...), custom_call_target="tpu_custom_call" | custom-call | tf_op jit(solution)/shard_map/cond/branch_1_fun/rims/pallas_call | solution.py:468
Async XLA Ops:
  2.7 11.7 %collective-permute-start.10 = (f32[8,1024]{1,0:T(8,128)}, f32[8,1024]{1,0:T(8,128)S(1)}, u32[]{:S(2)}, u32[]{:S(2)}) collective-permute-start(f32[8,1024]{1,0:T(8,128)} %get-tuple-element.77), channel_id=1, source_target_pairs={{0,1},{1,2},{2,3},{3,4},{4,5},{5,6},{6,7},{7,8},{8,9},{9,10},{10,1... | collective-permute-start | bytes 98312 | tf_op jit(solution)/shard_map/ppermute | solution.py:397
  3.2 11.2 %collective-permute-start.11 = (f32[8,1024]{1,0:T(8,128)}, f32[8,1024]{1,0:T(8,128)S(1)}, u32[]{:S(2)}, u32[]{:S(2)}) collective-permute-start(f32[8,1024]{1,0:T(8,128)} %get-tuple-element.78), channel_id=1, source_target_pairs={{1,0},{2,1},{3,2},{4,3},{5,4},{6,5},{7,6},{8,7},{9,8},{10,9},{11,1... | collective-permute-start | bytes 98312 | tf_op jit(solution)/shard_map/ppermute | solution.py:398
  8.2 6.2 %copy-start.3 = (f32[8,1024]{1,0:T(8,128)S(1)}, f32[8,1024]{1,0:T(8,128)}, u32[]{:S(2)}) copy-start(f32[8,1024]{1,0:T(8,128)} %eta.3) | copy-start | bytes 98308
  8.2 6.2 %copy-start.5 = (f32[8,1024]{1,0:T(8,128)S(1)}, f32[8,1024]{1,0:T(8,128)}, u32[]{:S(2)}) copy-start(f32[8,1024]{1,0:T(8,128)} %damping.3) | copy-start | bytes 98308
  8.2 29.1 %copy-start.1 = (f32[50,8,1024]{2,1,0:T(8,128)S(1)}, f32[50,8,1024]{2,1,0:T(8,128)}, u32[]{:S(2)}) copy-start(f32[50,8,1024]{2,1,0:T(8,128)} %velocity_y.3) | copy-start | bytes 4915204
  8.2 29.1 %copy-start.2 = (f32[50,8,1024]{2,1,0:T(8,128)S(1)}, f32[50,8,1024]{2,1,0:T(8,128)}, u32[]{:S(2)}) copy-start(f32[50,8,1024]{2,1,0:T(8,128)} %velocity_x.1) | copy-start | bytes 4915204
  8.2 29.1 %copy-start.10 = (s32[8,1024]{1,0:T(8,128)S(1)}, s32[8,1024]{1,0:T(8,128)}, u32[]{:S(2)}) copy-start(s32[8,1024]{1,0:T(8,128)} %wet.3) | copy-start | bytes 98308
  15.5 13.9 %collective-permute-start.12 = (f32[56,1024]{1,0:T(8,128)S(1)}, f32[56,1024]{1,0:T(8,128)S(1)}, u32[]{:S(2)}, u32[]{:S(2)}) collective-permute-start(f32[56,1024]{1,0:T(8,128)S(1)} %get-tuple-element.84), channel_id=1, source_target_pairs={{0,1},{1,2},{2,3},{3,4},{4,5},{5,6},{6,7},{7,8},{8,9},{9,10},{10,1... | collective-permute-start | bytes 688136 | tf_op jit(solution)/shard_map/ppermute | solution.py:439
  15.5 13.9 %collective-permute-start.13 = (f32[56,1024]{1,0:T(8,128)S(1)}, f32[56,1024]{1,0:T(8,128)S(1)}, u32[]{:S(2)}, u32[]{:S(2)}) collective-permute-start(f32[56,1024]{1,0:T(8,128)S(1)} %get-tuple-element.85), channel_id=1, source_target_pairs={{1,0},{2,1},{3,2},{4,3},{5,4},{6,5},{7,6},{8,7},{9,8},{10,9},{11,1... | collective-permute-start | bytes 688136 | tf_op jit(solution)/shard_map/ppermute | solution.py:440
  29.4 0.7 %copy-start.6 = (f32[56,1024]{1,0:T(8,128)}, f32[56,1024]{1,0:T(8,128)S(1)}, u32[]{:S(2)}) copy-start(f32[56,1024]{1,0:T(8,128)S(1)} %collective-permute-done.12) | copy-start | bytes 688132
  29.5 0.8 %copy-start.8 = (f32[56,1024]{1,0:T(8,128)}, f32[56,1024]{1,0:T(8,128)S(1)}, u32[]{:S(2)}) copy-start(f32[56,1024]{1,0:T(8,128)S(1)} %collective-permute-done.13) | copy-start | bytes 688132
  30.3 0.9 %copy-start = (f32[4,16,1024]{2,1,0:T(8,128)S(1)}, f32[4,16,1024]{2,1,0:T(8,128)}, u32[]{:S(2)}) copy-start(f32[4,16,1024]{2,1,0:T(8,128)} %get-tuple-element.87.basis) | copy-start | bytes 786436
  32.1 11.8 %collective-permute-start.14 = (f32[56,1024]{1,0:T(8,128)S(1)}, f32[56,1024]{1,0:T(8,128)S(1)}, u32[]{:S(2)}, u32[]{:S(2)}) collective-permute-start(f32[56,1024]{1,0:T(8,128)S(1)} %get-tuple-element.94), channel_id=1, source_target_pairs={{0,1},{1,2},{2,3},{3,4},{4,5},{5,6},{6,7},{7,8},{8,9},{9,10},{10,1... | collective-permute-start | bytes 688136 | tf_op jit(solution)/shard_map/ppermute | solution.py:481
  32.2 11.8 %collective-permute-start.15 = (f32[56,1024]{1,0:T(8,128)S(1)}, f32[56,1024]{1,0:T(8,128)S(1)}, u32[]{:S(2)}, u32[]{:S(2)}) collective-permute-start(f32[56,1024]{1,0:T(8,128)S(1)} %get-tuple-element.95), channel_id=1, source_target_pairs={{1,0},{2,1},{3,2},{4,3},{5,4},{6,5},{7,6},{8,7},{9,8},{10,9},{11,1... | collective-permute-start | bytes 688136 | tf_op jit(solution)/shard_map/ppermute | solution.py:482

commit v6 on v5

--- a/solution.py
+++ b/solution.py
@@ -18,7 +18,7 @@
 SMEM = pl.BlockSpec(memory_space=pltpu.SMEM)
 VMEM = pl.BlockSpec(memory_space=pltpu.VMEM)
 HBM = pl.BlockSpec(memory_space=pltpu.HBM)
-PARAMS = pltpu.CompilerParams(vmem_limit_bytes=32 * 2**20)
+PARAMS = pltpu.CompilerParams(vmem_limit_bytes=24 * 2**20)
 
 
 def in_hbm(x):
@@ -101,7 +101,7 @@
     return flip_lanes(rows)[:height]
 
 
-def outer_kernel(seam, eta, damping, up, down, mark):
+def outer_kernel(seam, eta, damping, up, down):
     half = SUBLANES // 2
     down[:half, :] = eta[:half, :]
     down[half:, :] = damping[:half, :]
@@ -113,7 +113,7 @@
         up[...] = flip_lanes(up[...])
 
 
-def basis_kernel(seam, eta, damping, below, above, basis, sums):
+def basis_kernel(seam, eta, damping, below, above, basis, sums, mark):
     half = SUBLANES // 2
     rows = 2 * SUBLANES
     beyond = above[...]
@@ -205,8 +205,16 @@
         down[at, :] = edges[2, at, :] + fields[:1, :] * edges[3, at, :]
 
 
-def surface_kernel(seam, sums, basis, edges, surface, up, down, sound):
+def surface_kernel(
+    seam, sums, basis_from, edges_from, surface, up, down, sound, basis, edges, sems
+):
     half = SUBLANES // 2
+    loads = (
+        pltpu.make_async_copy(basis_from, basis, sems.at[0]),
+        pltpu.make_async_copy(edges_from, edges, sems.at[1]),
+    )
+    for load in loads:
+        load.start()
     parts = [sums[i] for i in range(sums.shape[0])]
     while len(parts) > 1:
         pairs = [a + b for a, b in zip(parts[::2], parts[1::2])]
@@ -217,6 +225,8 @@
     for j in range(2, 2 * ITERS):
         moments.append(2.0 * raw[j] - raw[j % 2])
     s, good = coefficients(moments)
+    for load in loads:
+        load.wait()
     value = s[0] * basis[0]
     for j in range(1, ITERS):
         value = value + s[j] * basis[j]
@@ -343,7 +353,15 @@
     lax.fori_loop(0, levels, level, 0, unroll=5)
 
 
-def rim_kernel(seam, inside, wet, south0, north0, south1, north1, result, result_at, out_sems):
+def rim_kernel(
+    seam, inside, wet, south0, north0, south1, north1, result, result_at, lines_at, sems, out_sems
+):
+    loads = []
+    for i, line in enumerate((south1, north1, south0, north0)):
+        loads.append(pltpu.make_async_copy(line, lines_at.at[i], sems.at[i]))
+        loads[-1].start()
+    for load in loads:
+        load.wait()
     levels = inside.shape[1]
     width = wet.shape[1]
     turned = seam[0] == 1
@@ -354,9 +372,9 @@
         at = pl.ds(k, n)
         index = k + lax.broadcasted_iota(jnp.int32, (n, width), 0)
         result_at[:, at] = inside[:, at]
-        for t, (south_from, north_from) in enumerate(((south0, north0), (south1, north1))):
-            south = south_from[k : k + n, :]
-            north = north_from[k : k + n, :]
+        for t in range(2):
+            south = lines_at[2 - 2 * t, k : k + n, :]
+            north = lines_at[3 - 2 * t, k : k + n, :]
             north = jnp.where(turned, flip_some(north), north)
             result_at[t, at, 0, :] += jnp.where(index < depth_south, south, 0.0)
             result_at[t, at, SUBLANES - 1, :] += jnp.where(index < depth_north, north, 0.0)
@@ -387,106 +405,118 @@
     lines = -(-levels // SUBLANES) * SUBLANES
     line = jax.ShapeDtypeStruct((lines, width), f32)
 
-    up, down, mark = pl.pallas_call(
+    up, down = pl.pallas_call(
         outer_kernel,
-        out_shape=(tile, tile, pltpu.HBM((rows, LANES), f32)),
+        out_shape=(tile, tile),
         in_specs=[SMEM, VMEM, VMEM],
-        out_specs=(VMEM, VMEM, HBM),
+        out_specs=(VMEM, VMEM),
         name="outer_rows",
     )(seam_codes, eta_adjoint, surface_damping)
     below = lax.ppermute(up, "face", upward)
     above = lax.ppermute(down, "face", downward)
 
     cube = pltpu.VMEM((levels, rows, width), f32)
-    parts = len(chunks_of(levels, CHUNK))
-    solved, up1, down1, edges = pl.pallas_call(
-        column_kernel,
-        out_shape=(
-            jax.ShapeDtypeStruct((3, levels, rows, width), f32),
-            line,
-            line,
-            jax.ShapeDtypeStruct((4, lines, width), f32),
-        ),
-        in_specs=[SMEM] + [HBM] * 6,
-        out_specs=(VMEM, VMEM, VMEM, VMEM),
-        scratch_shapes=[
-            pltpu.SMEM((levels,), f32),
-            pltpu.VMEM((rows, width), jnp.int32),
-            pltpu.VMEM((tracers, levels, rows, width), f32),
-            cube,
-            cube,
-            cube,
-            pltpu.SemaphoreType.DMA((3, max(parts, 3))),
-        ],
-        compiler_params=PARAMS,
-        cost_estimate=pl.CostEstimate(flops=40000000, bytes_accessed=13000000, transcendentals=0),
-        name="columns",
-    )(
-        seam_codes,
-        *map(in_hbm, (thickness, tracer_adjoint, mixing, velocity_y, wet_levels, mark)),
-    )
-
-    basis, sums = pl.pallas_call(
-        basis_kernel,
-        out_shape=(ext, jax.ShapeDtypeStruct((count, SUBLANES, LANES), f32)),
-        in_specs=[SMEM] + [VMEM] * 4,
-        out_specs=(VMEM, VMEM),
-        compiler_params=PARAMS,
-        name="surface_basis",
-    )(seam_codes, eta_adjoint, surface_damping, below, above)
-    sums, up1, down1 = lax.optimization_barrier((sums, up1, down1))
-    sums = lax.all_to_all(sums, "face", 0, 0)
-    south1 = lax.ppermute(up1, "face", upward)
-    north1 = lax.ppermute(down1, "face", downward)
-    sums, south1, north1 = lax.optimization_barrier((sums, south1, north1))
-
-    surface, up0, down0, sound = pl.pallas_call(
-        surface_kernel,
-        out_shape=(tile, line, line, jax.ShapeDtypeStruct((1,), jnp.int32)),
-        in_specs=[SMEM, VMEM, VMEM, VMEM],
-        out_specs=(VMEM, VMEM, VMEM, SMEM),
-        compiler_params=PARAMS,
-        name="surface",
-    )(seam_codes, sums, basis, edges)
-
+    chunks = len(chunks_of(levels, CHUNK))
     parts = len(chunks_of(levels, SUBLANES))
-
-    def inside_of(surface):
+    inputs = [in_hbm(x) for x in (thickness, tracer_adjoint, mixing, velocity_y, wet_levels)]
+
+    def columns_after(mark, place):
+        return pl.pallas_call(
+            column_kernel,
+            out_shape=(
+                place((3, levels, rows, width), f32),
+                line,
+                line,
+                pltpu.HBM((4, lines, width), f32),
+            ),
+            in_specs=[SMEM] + [HBM] * 6,
+            out_specs=(VMEM, VMEM, VMEM, VMEM),
+            scratch_shapes=[
+                pltpu.SMEM((levels,), f32),
+                pltpu.VMEM((rows, width), jnp.int32),
+                pltpu.VMEM((tracers, levels, rows, width), f32),
+                cube,
+                cube,
+                cube,
+                pltpu.SemaphoreType.DMA((3, max(chunks, 3))),
+            ],
+            compiler_params=PARAMS,
+            cost_estimate=pl.CostEstimate(
+                flops=40000000, bytes_accessed=13000000, transcendentals=0
+            ),
+            name="columns",
+        )(seam_codes, *inputs, mark)
+
+    def inside_of(solved, surface, place):
         return pl.pallas_call(
             inside_kernel,
-            out_shape=jax.ShapeDtypeStruct((tracers, levels, rows, width), f32),
+            out_shape=place((tracers, levels, rows, width), f32),
             in_specs=[VMEM] * 5,
             out_specs=VMEM,
             compiler_params=PARAMS,
-            cost_estimate=pl.CostEstimate(
-                flops=20000000, bytes_accessed=13000000, transcendentals=0
-            ),
+            cost_estimate=pl.CostEstimate(flops=1000, bytes_accessed=1000, transcendentals=0),
             name="inside",
         )(solved, velocity_x, velocity_y, wet_levels, surface)
 
-    def with_rims(inside, south0, north0, south1, north1):
+    def with_rims(inside, *beyond):
         return pl.pallas_call(
             rim_kernel,
             out_shape=pltpu.HBM((tracers, levels, rows, width), f32),
-            in_specs=[SMEM] + [VMEM] * 6,
+            in_specs=[SMEM, VMEM, VMEM] + [HBM] * 4,
             out_specs=HBM,
             scratch_shapes=[
                 pltpu.VMEM((tracers, levels, rows, width), f32),
+                pltpu.VMEM((4, lines, width), f32),
+                pltpu.SemaphoreType.DMA((4,)),
                 pltpu.SemaphoreType.DMA((parts,)),
             ],
             compiler_params=PARAMS,
             name="rims",
-        )(seam_codes, inside, wet_levels, south0, north0, south1, north1)
-
-    south0 = lax.ppermute(up0, "face", upward)
-    north0 = lax.ppermute(down0, "face", downward)
-    inside = inside_of(surface)
-
-    def by_moments(surface, inside, south0, north0):
+        )(seam_codes, inside, wet_levels, *map(in_hbm, beyond))
+
+    def across(up, down):
+        return lax.ppermute(up, "face", upward), lax.ppermute(down, "face", downward)
+
+    basis, sums, mark = pl.pallas_call(
+        basis_kernel,
+        out_shape=(
+            ext,
+            pltpu.HBM((count, SUBLANES, LANES), f32),
+            pltpu.HBM((SUBLANES, LANES), f32),
+        ),
+        in_specs=[SMEM] + [VMEM] * 4,
+        out_specs=(VMEM, VMEM, HBM),
+        compiler_params=PARAMS,
+        name="surface_basis",
+    )(seam_codes, eta_adjoint, surface_damping, below, above)
+    sums = lax.all_to_all(sums, "face", 0, 0)
+
+    solved, up1, down1, edges = columns_after(in_hbm(mark), pltpu.VMEM)
+    south1, north1 = across(up1, down1)
+    sums, south1, north1 = lax.optimization_barrier((sums, south1, north1))
+
+    surface, up0, down0, sound = pl.pallas_call(
+        surface_kernel,
+        out_shape=(tile, line, line, jax.ShapeDtypeStruct((1,), jnp.int32)),
+        in_specs=[SMEM, VMEM, HBM, HBM],
+        out_specs=(VMEM, VMEM, VMEM, SMEM),
+        scratch_shapes=[
+            pltpu.VMEM((ITERS, 2 * rows, width), f32),
+            pltpu.VMEM((4, lines, width), f32),
+            pltpu.SemaphoreType.DMA((2,)),
+        ],
+        compiler_params=PARAMS,
+        name="surface",
+    )(seam_codes, sums, in_hbm(basis), in_hbm(edges))
+    south0, north0 = across(up0, down0)
+    inside = inside_of(solved, surface, pltpu.VMEM)
+
+    def by_moments(surface, inside, south0, north0, south1, north1):
         return with_rims(inside, south0, north0, south1, north1), surface
 
-    def by_steps(surface, inside, south0, north0):
+    def by_steps(surface, inside, south0, north0, south1, north1):
         surface = stepwise_surface(eta_adjoint, surface_damping, seam_codes[0] == 1)
+        solved, up1, down1, edges = columns_after(in_hbm(mark), jax.ShapeDtypeStruct)
         up0, down0 = pl.pallas_call(
             outer_lines,
             out_shape=(line, line),
@@ -495,11 +525,12 @@
             compiler_params=PARAMS,
             name="outer_lines",
         )(seam_codes, surface, edges)
-        south0 = lax.ppermute(up0, "face", upward)
-        north0 = lax.ppermute(down0, "face", downward)
-        return with_rims(inside_of(surface), south0, north0, south1, north1), surface
-
-    return lax.cond(sound[0] == 1, by_moments, by_steps, surface, inside, south0, north0)
+        inside = inside_of(solved, surface, jax.ShapeDtypeStruct)
+        return with_rims(inside, *across(up0, down0), *across(up1, down1)), surface
+
+    return lax.cond(
+        sound[0] == 1, by_moments, by_steps, surface, inside, south0, north0, south1, north1
+    )
 
 
 def solution(mesh):

time: 48.9 us -> 46.7 us (0.955)
  Pallas kernels: 20.8 us -> 17.5 us
  waiting for transfers between devices: 0.02 us -> 1.92 us
  local copies, waits for them, and re-layouts: 1.78 us -> 0.79 us
    pallas_call x4, Pallas kernels: 15.3 us -> 11.5 us  [the longest x1 4.92 us: columns_after(): pl.pallas_call(column_kernel, out_shape=(place((3, levels, rows, width),...]
    ppermute x1, waiting for transfers between devices: 0.01 us -> 1.8 us  [shards(): below = lax.ppermute(up, 'face', upward)]
    unnamed x16, local copies, waits for them, and re-layouts: 1.78 us -> 0.04 us
    pallas_call x1, Pallas kernels: 0.9 us -> 2.12 us  [shards(): pl.pallas_call(surface_kernel, out_shape=(tile, line, line, jax.ShapeDtyp...]
    cond x0 -> x4, local copies, waits for them, and re-layouts: none -> 0.76 us
    pallas_call x1, Pallas kernels: 4.62 us -> 3.87 us  [with_rims(): pl.pallas_call(rim_kernel, out_shape=pltpu.HBM((tracers, levels, rows, wi...]
  transfers between devices with their start and end apart: 6 -> 6, of which waited for: 0 -> 2; matrix products, arithmetic and copies ran while one was open for 0% -> 0% of each run, Pallas kernels for 26% -> 7%
where the time goes in v6:
time: 46.7 us; the launch traced here: 46.2 us
  Pallas kernels  17.5 us (37%)
  starting transfers between devices  14.4 us (31%)
  blocking collectives  9.47 us (20%)
  between operations  2.08 us (4%)
  waiting for transfers between devices  1.92 us (4%)
  local copies, waits for them, and re-layouts  0.79 us (2%)
    all_to_all x1, blocking collectives, shards(): sums = lax.all_to_all(sums, 'face', 0, 0)  9.47 us
    ppermute x2, starting transfers between devices, across(): lax.ppermute(down, 'face', downward)  8.86 us
    pallas_call x1, Pallas kernels, columns_after(): pl.pallas_call(column_kernel, out_shape=(place((3, levels, rows, width),...  4.92 us
    ppermute x1, starting transfers between devices, shards(): above = lax.ppermute(down, 'face', downward)  4.91 us
    pallas_call x1, Pallas kernels, with_rims(): pl.pallas_call(rim_kernel, out_shape=pltpu.HBM((tracers, levels, rows, wi...  3.87 us
    pallas_call x1, Pallas kernels, inside_of(): pl.pallas_call(inside_kernel, out_shape=place((tracers, levels, rows, wid...  3.33 us
    pallas_call x1, Pallas kernels, shards(): pl.pallas_call(surface_kernel, out_shape=(tile, line, line, jax.ShapeDtyp...  2.12 us
    pallas_call x1, Pallas kernels, shards(): pl.pallas_call(basis_kernel, out_shape=(ext, pltpu.HBM((count, SUBLANES,...  1.86 us
  transfers between devices with their start and end apart: 6, of which 2 were waited for; matrix products, arithmetic and copies ran while one was open for 0% of the time, Pallas kernels for 7%

profile of v6, /device:TPU:0, one launch (start us, length us, event | category | flops | bytes accessed | tf_op | source)
XLA Modules:
  0.0 46.2 jit_solution(9592686521874735373)
XLA Ops:
  1.3 1.4 %outer_rows.1 = (f32[8,1024]{1,0:T(8,128)}, f32[8,1024]{1,0:T(8,128)}) custom-call(s32[1]{0:T(128)S(6)} %copy.17.seam, f32[8,1024]{1,0:T(8,128)} %eta.3, f32[8,1024]{1,0:T(8,128)} %damping.3), custom_call_target="tpu_custom_call" | custom-call | tf_op jit(solution)/shard_map/outer_rows/pallas_call | solution.py:408
  2.7 0.5 %collective-permute-start.12 = (f32[8,1024]{1,0:T(8,128)}, f32[8,1024]{1,0:T(8,128)S(1)}, u32[]{:S(2)}, u32[]{:S(2)}) collective-permute-start(f32[8,1024]{1,0:T(8,128)} %get-tuple-element.78), channel_id=1, source_target_pairs={{0,1},{1,2},{2,3},{3,4},{4,5},{5,6},{6,7},{7,8},{8,9},{9,10},{10,1... | collective-permute-start | bytes 98312 | tf_op jit(solution)/shard_map/ppermute | solution.py:415
  3.2 4.9 %collective-permute-start.13 = (f32[8,1024]{1,0:T(8,128)}, f32[8,1024]{1,0:T(8,128)S(1)}, u32[]{:S(2)}, u32[]{:S(2)}) collective-permute-start(f32[8,1024]{1,0:T(8,128)} %get-tuple-element.79), channel_id=1, source_target_pairs={{1,0},{2,1},{3,2},{4,3},{5,4},{6,5},{7,6},{8,7},{9,8},{10,9},{11,1... | collective-permute-start | bytes 98312 | tf_op jit(solution)/shard_map/ppermute | solution.py:416
  8.1 1.8 %collective-permute-done.12.below = f32[8,1024]{1,0:T(8,128)S(1)} collective-permute-done((f32[8,1024]{1,0:T(8,128)}, f32[8,1024]{1,0:T(8,128)S(1)}, u32[]{:S(2)}, u32[]{:S(2)}) %collective-permute-start.12) | collective-permute-done | bytes 32800 | tf_op jit(solution)/shard_map/ppermute | solution.py:415
  9.9 0.1 collective-permute-done.13.above
  10.1 1.9 %surface_basis.1 = (f32[4,16,1024]{2,1,0:T(8,128)}, f32[16,8,128]{2,1,0:T(8,128)}, f32[8,128]{1,0:T(8,128)}) custom-call(s32[1]{0:T(128)S(6)} %copy.17.seam, f32[8,1024]{1,0:T(8,128)} %eta.3, f32[8,1024]{1,0:T(8,128)} %damping.3, f32[8,1024]{1,0:T(8,128)S(1)} %collective-permute-done.12.below, f32[8,1024]{1,0:T(8,128)S(1)} %collective-permute-done.13.above), custom_call_target="tpu_custom_call" | custom-call | tf_op jit(solution)/shard_map/surface_basis/pallas_call | solution.py:480
  11.9 0.0 copy-start.21
  11.9 0.0 copy-start.3
  11.9 0.0 copy-start.6
  11.9 0.0 copy-start.9
  11.9 4.9 %columns.3 = (f32[3,50,8,1024]{3,2,1,0:T(8,128)S(1)}, f32[56,1024]{1,0:T(8,128)S(1)}, f32[56,1024]{1,0:T(8,128)S(1)}, f32[4,56,1024]{2,1,0:T(8,128)}) custom-call(s32[1]{0:T(128)S(6)} %copy.17.seam, f32[50]{0:T(128)} %thickness_from.1, f32[2,50,8,1024]{3,2,1,0:T(8,128)} %tracer.1, f32[49,8,1024]{2,1,0:T(8,128)} %mixing.1, f32[50,8,1024]{2,1,0:T(8,128)} %velocity_y.3, ...), custom_call_target="tpu_custom_call" | custom-call | flops 40000000 | bytes 13000000 | tf_op jit(solution)/shard_map/columns/pallas_call | solution.py:424
  16.9 0.1 collective-permute-start.14
  16.9 4.4 %collective-permute-start.15 = (f32[56,1024]{1,0:T(8,128)S(1)}, f32[56,1024]{1,0:T(8,128)S(1)}, u32[]{:S(2)}, u32[]{:S(2)}) collective-permute-start(f32[56,1024]{1,0:T(8,128)S(1)} %get-tuple-element.83), channel_id=1, source_target_pairs={{1,0},{2,1},{3,2},{4,3},{5,4},{6,5},{7,6},{8,7},{9,8},{10,9},{11,1... | collective-permute-start | bytes 688136 | tf_op jit(solution)/shard_map/ppermute | solution.py:478
  21.4 0.0 copy-done.21
  21.4 9.5 %all_to_all.5.sums = f32[16,8,128]{2,1,0:T(8,128)S(1)} all-to-all(f32[16,8,128]{2,1,0:T(8,128)S(1)} %copy-done.21), channel_id=1, replica_groups=mesh['ens'=2,'face'=16] {'face'}, dimensions={0} | all-to-all | bytes 131072 | tf_op jit(solution)/shard_map/all_to_all | solution.py:492
  30.8 0.0 collective-permute-done.14
  30.8 0.0 copy-start.13
  30.8 0.0 collective-permute-done.15
  30.8 0.0 copy-start.14
  30.8 2.1 %surface.1 = (f32[8,1024]{1,0:T(8,128)}, f32[56,1024]{1,0:T(8,128)S(1)}, f32[56,1024]{1,0:T(8,128)S(1)}, s32[1]{0:T(128)}) custom-call(s32[1]{0:T(128)S(6)} %copy.17.seam, f32[16,8,128]{2,1,0:T(8,128)S(1)} %all_to_all.5.sums, f32[4,16,1024]{2,1,0:T(8,128)} %get-tuple-element.85.basis_from, f32[4,56,1024]{2,1,0:T(8,128)} %get-tuple-element.86.edges_from), custom_call_target="tpu_custom_call" | custom-call | tf_op jit(solution)/shard_map/surface/pallas_call | solution.py:498
  33.0 0.1 collective-permute-start.16
  33.0 4.4 %collective-permute-start.17 = (f32[56,1024]{1,0:T(8,128)S(1)}, f32[56,1024]{1,0:T(8,128)S(1)}, u32[]{:S(2)}, u32[]{:S(2)}) collective-permute-start(f32[56,1024]{1,0:T(8,128)S(1)} %get-tuple-element.91), channel_id=1, source_target_pairs={{1,0},{2,1},{3,2},{4,3},{5,4},{6,5},{7,6},{8,7},{9,8},{10,9},{11,1... | collective-permute-start | bytes 688136 | tf_op jit(solution)/shard_map/ppermute | solution.py:478
  37.5 0.0 copy-done.13
  37.5 0.0 copy-done.14
  37.5 0.0 copy-done.3
  37.5 0.0 copy-done.6
  37.5 0.0 copy-done.9
  37.5 0.0 copy-start.8
  37.5 0.0 copy-start.12
  37.5 3.3 %inside.3 = f32[2,50,8,1024]{3,2,1,0:T(8,128)S(1)} custom-call(f32[3,50,8,1024]{3,2,1,0:T(8,128)S(1)} %get-tuple-element.88.solved, f32[50,8,1024]{2,1,0:T(8,128)S(1)} %copy-done.6, f32[50,8,1024]{2,1,0:T(8,128)S(1)} %copy-done.3, s32[8,1024]{1,0:T(8,128)S(1)} %copy-done.9, f32[8,1024]{1,0:T(8,128)} %get-tuple-element.89.surface), custom_call_target="tpu_custom_call" | custom-call | flops 1000 | bytes 1000 | tf_op jit(solution)/shard_map/inside/pallas_call | solution.py:451
  41.5 0.0 collective-permute-done.16
  41.5 0.0 collective-permute-done.17
  41.6 0.0 copy-done.8
  41.6 0.0 copy-done.12
  41.6 4.7 %conditional.1 = (f32[8,1024]{1,0:T(8,128)}, f32[2,50,8,1024]{3,2,1,0:T(8,128)}) conditional(s32[]{:T(128)} %bitcast.1, (s32[1]{0:T(128)}, f32[50]{0:T(128)}, f32[2,50,8,1024]{3,2,1,0:T(8,128)}, f32[49,8,1024]{2,1,0:T(8,128)}, f32[50,8,1024]{2,1,0:T(8,128)S(1)}, /*index=5*/s32[8,1024]{1,0:T(8,128)S(1)}, f32[8,128]{1,0:T(8,128)}, ...), branch_computations={%region_0.17_spmd, %region_17.18_spmd} | conditional | flops 40672752 | bytes 86238536 | solution.py:531
  41.6 0.0 copy-start.15
  41.6 0.0 copy-start.16
  41.6 0.7 %copy-done.15 = f32[56,1024]{1,0:T(8,128)} copy-done((f32[56,1024]{1,0:T(8,128)}, f32[56,1024]{1,0:T(8,128)S(1)}, u32[]{:S(2)}) %copy-start.15) | copy-done | bytes 229400 | tf_op jit(solution)/shard_map/cond
  42.3 0.1 copy-done.16
  42.4 3.9 %rims.3 = f32[2,50,8,1024]{3,2,1,0:T(8,128)} custom-call(s32[1]{0:T(128)} %get-tuple-element.52.seam, f32[2,50,8,1024]{3,2,1,0:T(8,128)S(1)} %get-tuple-element.53.inside, s32[8,1024]{1,0:T(8,128)S(1)} %get-tuple-element.54.wet, f32[56,1024]{1,0:T(8,128)} %copy-done.15, f32[56,1024]{1,0:T(8,128)} %copy-done.16, f32[56,1024]{1,0:T(8,128)} %get-tuple-element.57.south1, ...), custom_call_target="tpu_custom_call" | custom-call | tf_op jit(solution)/shard_map/cond/branch_1_fun/rims/pallas_call | solution.py:462
Async XLA Ops:
  2.7 7.3 %collective-permute-start.12 = (f32[8,1024]{1,0:T(8,128)}, f32[8,1024]{1,0:T(8,128)S(1)}, u32[]{:S(2)}, u32[]{:S(2)}) collective-permute-start(f32[8,1024]{1,0:T(8,128)} %get-tuple-element.78), channel_id=1, source_target_pairs={{0,1},{1,2},{2,3},{3,4},{4,5},{5,6},{6,7},{7,8},{8,9},{9,10},{10,1... | collective-permute-start | bytes 98312 | tf_op jit(solution)/shard_map/ppermute | solution.py:415
  3.2 6.8 %collective-permute-start.13 = (f32[8,1024]{1,0:T(8,128)}, f32[8,1024]{1,0:T(8,128)S(1)}, u32[]{:S(2)}, u32[]{:S(2)}) collective-permute-start(f32[8,1024]{1,0:T(8,128)} %get-tuple-element.79), channel_id=1, source_target_pairs={{1,0},{2,1},{3,2},{4,3},{5,4},{6,5},{7,6},{8,7},{9,8},{10,9},{11,1... | collective-permute-start | bytes 98312 | tf_op jit(solution)/shard_map/ppermute | solution.py:416
  11.9 9.4 %copy-start.21 = (f32[16,8,128]{2,1,0:T(8,128)S(1)}, f32[16,8,128]{2,1,0:T(8,128)}, u32[]{:S(2)}) copy-start(f32[16,8,128]{2,1,0:T(8,128)} %get-tuple-element.80) | copy-start | bytes 196612
  11.9 25.6 %copy-start.3 = (f32[50,8,1024]{2,1,0:T(8,128)S(1)}, f32[50,8,1024]{2,1,0:T(8,128)}, u32[]{:S(2)}) copy-start(f32[50,8,1024]{2,1,0:T(8,128)} %velocity_y.3) | copy-start | bytes 4915204
  11.9 25.6 %copy-start.6 = (f32[50,8,1024]{2,1,0:T(8,128)S(1)}, f32[50,8,1024]{2,1,0:T(8,128)}, u32[]{:S(2)}) copy-start(f32[50,8,1024]{2,1,0:T(8,128)} %velocity_x.1) | copy-start | bytes 4915204
  11.9 25.6 %copy-start.9 = (s32[8,1024]{1,0:T(8,128)S(1)}, s32[8,1024]{1,0:T(8,128)}, u32[]{:S(2)}) copy-start(s32[8,1024]{1,0:T(8,128)} %wet.3) | copy-start | bytes 98308
  16.9 14.0 %collective-permute-start.14 = (f32[56,1024]{1,0:T(8,128)S(1)}, f32[56,1024]{1,0:T(8,128)S(1)}, u32[]{:S(2)}, u32[]{:S(2)}) collective-permute-start(f32[56,1024]{1,0:T(8,128)S(1)} %get-tuple-element.82), channel_id=1, source_target_pairs={{0,1},{1,2},{2,3},{3,4},{4,5},{5,6},{6,7},{7,8},{8,9},{9,10},{10,1... | collective-permute-start | bytes 688136 | tf_op jit(solution)/shard_map/ppermute | solution.py:478
  16.9 13.9 %collective-permute-start.15 = (f32[56,1024]{1,0:T(8,128)S(1)}, f32[56,1024]{1,0:T(8,128)S(1)}, u32[]{:S(2)}, u32[]{:S(2)}) collective-permute-start(f32[56,1024]{1,0:T(8,128)S(1)} %get-tuple-element.83), channel_id=1, source_target_pairs={{1,0},{2,1},{3,2},{4,3},{5,4},{6,5},{7,6},{8,7},{9,8},{10,9},{11,1... | collective-permute-start | bytes 688136 | tf_op jit(solution)/shard_map/ppermute | solution.py:478
  30.8 6.6 %copy-start.13 = (f32[56,1024]{1,0:T(8,128)}, f32[56,1024]{1,0:T(8,128)S(1)}, u32[]{:S(2)}) copy-start(f32[56,1024]{1,0:T(8,128)S(1)} %collective-permute-done.14) | copy-start | bytes 688132
  30.8 6.6 %copy-start.14 = (f32[56,1024]{1,0:T(8,128)}, f32[56,1024]{1,0:T(8,128)S(1)}, u32[]{:S(2)}) copy-start(f32[56,1024]{1,0:T(8,128)S(1)} %collective-permute-done.15) | copy-start | bytes 688132
  33.0 8.6 %collective-permute-start.16 = (f32[56,1024]{1,0:T(8,128)S(1)}, f32[56,1024]{1,0:T(8,128)S(1)}, u32[]{:S(2)}, u32[]{:S(2)}) collective-permute-start(f32[56,1024]{1,0:T(8,128)S(1)} %get-tuple-element.90), channel_id=1, source_target_pairs={{0,1},{1,2},{2,3},{3,4},{4,5},{5,6},{6,7},{7,8},{8,9},{9,10},{10,1... | collective-permute-start | bytes 688136 | tf_op jit(solution)/shard_map/ppermute | solution.py:478
  33.0 8.5 %collective-permute-start.17 = (f32[56,1024]{1,0:T(8,128)S(1)}, f32[56,1024]{1,0:T(8,128)S(1)}, u32[]{:S(2)}, u32[]{:S(2)}) collective-permute-start(f32[56,1024]{1,0:T(8,128)S(1)} %get-tuple-element.91), channel_id=1, source_target_pairs={{1,0},{2,1},{3,2},{4,3},{5,4},{6,5},{7,6},{8,7},{9,8},{10,9},{11,1... | collective-permute-start | bytes 688136 | tf_op jit(solution)/shard_map/ppermute | solution.py:478
  37.5 4.1 %copy-start.8 = (f32[8,1024]{1,0:T(8,128)S(1)}, f32[8,1024]{1,0:T(8,128)}, u32[]{:S(2)}) copy-start(f32[8,1024]{1,0:T(8,128)} %eta.3) | copy-start | bytes 98308
  37.5 4.1 %copy-start.12 = (f32[8,1024]{1,0:T(8,128)S(1)}, f32[8,1024]{1,0:T(8,128)}, u32[]{:S(2)}) copy-start(f32[8,1024]{1,0:T(8,128)} %damping.3) | copy-start | bytes 98308
  41.6 0.7 %copy-start.15 = (f32[56,1024]{1,0:T(8,128)}, f32[56,1024]{1,0:T(8,128)S(1)}, u32[]{:S(2)}) copy-start(f32[56,1024]{1,0:T(8,128)S(1)} %get-tuple-element.55.south0) | copy-start | bytes 688132 | tf_op jit(solution)/shard_map/cond
  41.6 0.8 %copy-start.16 = (f32[56,1024]{1,0:T(8,128)}, f32[56,1024]{1,0:T(8,128)S(1)}, u32[]{:S(2)}) copy-start(f32[56,1024]{1,0:T(8,128)S(1)} %get-tuple-element.56.north0) | copy-start | bytes 688132 | tf_op jit(solution)/shard_map/cond

commit v7 on v6

--- a/solution.py
+++ b/solution.py
@@ -101,8 +101,10 @@
     return flip_lanes(rows)[:height]
 
 
-def outer_kernel(seam, eta, damping, up, down):
+def outer_kernel(seam, eta, damping, up, down, own, mark):
     half = SUBLANES // 2
+    own[:SUBLANES, :] = eta[...]
+    own[SUBLANES:, :] = damping[...]
     down[:half, :] = eta[:half, :]
     down[half:, :] = damping[:half, :]
     up[:half, :] = eta[half:, :]
@@ -113,14 +115,14 @@
         up[...] = flip_lanes(up[...])
 
 
-def basis_kernel(seam, eta, damping, below, above, basis, sums, mark):
+def basis_kernel(seam, own_rows, below, above, basis, sums):
     half = SUBLANES // 2
     rows = 2 * SUBLANES
     beyond = above[...]
     beyond = jnp.where(seam[0] == 1, flip_lanes(beyond), beyond)
     width = beyond.shape[1]
-    v = jnp.concatenate([below[:half, :], eta[...], beyond[:half, :]], axis=0)
-    d = jnp.concatenate([below[half:, :], damping[...], beyond[half:, :]], axis=0)
+    v = jnp.concatenate([below[:half, :], own_rows[:SUBLANES, :], beyond[:half, :]], axis=0)
+    d = jnp.concatenate([below[half:, :], own_rows[SUBLANES:, :], beyond[half:, :]], axis=0)
     d = (d + (4.0 - MIDDLE)) * (1.0 / MIDDLE)
     vectors = [v]
     for j in range(ITERS):
@@ -205,16 +207,8 @@
         down[at, :] = edges[2, at, :] + fields[:1, :] * edges[3, at, :]
 
 
-def surface_kernel(
-    seam, sums, basis_from, edges_from, surface, up, down, sound, basis, edges, sems
-):
+def surface_kernel(seam, sums, basis, edges, surface, up, down, sound):
     half = SUBLANES // 2
-    loads = (
-        pltpu.make_async_copy(basis_from, basis, sems.at[0]),
-        pltpu.make_async_copy(edges_from, edges, sems.at[1]),
-    )
-    for load in loads:
-        load.start()
     parts = [sums[i] for i in range(sums.shape[0])]
     while len(parts) > 1:
         pairs = [a + b for a, b in zip(parts[::2], parts[1::2])]
@@ -225,8 +219,6 @@
     for j in range(2, 2 * ITERS):
         moments.append(2.0 * raw[j] - raw[j % 2])
     s, good = coefficients(moments)
-    for load in loads:
-        load.wait()
     value = s[0] * basis[0]
     for j in range(1, ITERS):
         value = value + s[j] * basis[j]
@@ -353,15 +345,7 @@
     lax.fori_loop(0, levels, level, 0, unroll=5)
 
 
-def rim_kernel(
-    seam, inside, wet, south0, north0, south1, north1, result, result_at, lines_at, sems, out_sems
-):
-    loads = []
-    for i, line in enumerate((south1, north1, south0, north0)):
-        loads.append(pltpu.make_async_copy(line, lines_at.at[i], sems.at[i]))
-        loads[-1].start()
-    for load in loads:
-        load.wait()
+def rim_kernel(seam, inside, wet, south0, north0, south1, north1, result, result_at, out_sems):
     levels = inside.shape[1]
     width = wet.shape[1]
     turned = seam[0] == 1
@@ -372,9 +356,9 @@
         at = pl.ds(k, n)
         index = k + lax.broadcasted_iota(jnp.int32, (n, width), 0)
         result_at[:, at] = inside[:, at]
-        for t in range(2):
-            south = lines_at[2 - 2 * t, k : k + n, :]
-            north = lines_at[3 - 2 * t, k : k + n, :]
+        for t, (south_from, north_from) in enumerate(((south0, north0), (south1, north1))):
+            south = south_from[k : k + n, :]
+            north = north_from[k : k + n, :]
             north = jnp.where(turned, flip_some(north), north)
             result_at[t, at, 0, :] += jnp.where(index < depth_south, south, 0.0)
             result_at[t, at, SUBLANES - 1, :] += jnp.where(index < depth_north, north, 0.0)
@@ -401,15 +385,20 @@
     upward = [(i, (i + 1) % count) for i in range(count)]
     downward = [(j, i) for i, j in upward]
     tile = jax.ShapeDtypeStruct((rows, width), f32)
-    ext = pltpu.HBM((ITERS, 2 * rows, width), f32)
+    ext = pltpu.VMEM((ITERS, 2 * rows, width), f32)
     lines = -(-levels // SUBLANES) * SUBLANES
     line = jax.ShapeDtypeStruct((lines, width), f32)
 
-    up, down = pl.pallas_call(
+    up, down, own, mark = pl.pallas_call(
         outer_kernel,
-        out_shape=(tile, tile),
+        out_shape=(
+            tile,
+            tile,
+            pltpu.VMEM((2 * rows, width), f32),
+            pltpu.HBM((SUBLANES, LANES), f32),
+        ),
         in_specs=[SMEM, VMEM, VMEM],
-        out_specs=(VMEM, VMEM),
+        out_specs=(VMEM, VMEM, VMEM, HBM),
         name="outer_rows",
     )(seam_codes, eta_adjoint, surface_damping)
     below = lax.ppermute(up, "face", upward)
@@ -427,7 +416,7 @@
                 place((3, levels, rows, width), f32),
                 line,
                 line,
-                pltpu.HBM((4, lines, width), f32),
+                place((4, lines, width), f32),
             ),
             in_specs=[SMEM] + [HBM] * 6,
             out_specs=(VMEM, VMEM, VMEM, VMEM),
@@ -462,33 +451,30 @@
         return pl.pallas_call(
             rim_kernel,
             out_shape=pltpu.HBM((tracers, levels, rows, width), f32),
-            in_specs=[SMEM, VMEM, VMEM] + [HBM] * 4,
+            in_specs=[SMEM] + [VMEM] * 6,
             out_specs=HBM,
             scratch_shapes=[
                 pltpu.VMEM((tracers, levels, rows, width), f32),
-                pltpu.VMEM((4, lines, width), f32),
-                pltpu.SemaphoreType.DMA((4,)),
                 pltpu.SemaphoreType.DMA((parts,)),
             ],
             compiler_params=PARAMS,
             name="rims",
-        )(seam_codes, inside, wet_levels, *map(in_hbm, beyond))
+        )(seam_codes, inside, wet_levels, *beyond)
 
     def across(up, down):
         return lax.ppermute(up, "face", upward), lax.ppermute(down, "face", downward)
 
-    basis, sums, mark = pl.pallas_call(
+    basis, sums = pl.pallas_call(
         basis_kernel,
         out_shape=(
             ext,
-            pltpu.HBM((count, SUBLANES, LANES), f32),
-            pltpu.HBM((SUBLANES, LANES), f32),
+            jax.ShapeDtypeStruct((count, SUBLANES, LANES), f32),
         ),
-        in_specs=[SMEM] + [VMEM] * 4,
-        out_specs=(VMEM, VMEM, HBM),
+        in_specs=[SMEM] + [VMEM] * 3,
+        out_specs=(VMEM, VMEM),
         compiler_params=PARAMS,
         name="surface_basis",
-    )(seam_codes, eta_adjoint, surface_damping, below, above)
+    )(seam_codes, own, below, above)
     sums = lax.all_to_all(sums, "face", 0, 0)
 
     solved, up1, down1, edges = columns_after(in_hbm(mark), pltpu.VMEM)
@@ -498,16 +484,11 @@
     surface, up0, down0, sound = pl.pallas_call(
         surface_kernel,
         out_shape=(tile, line, line, jax.ShapeDtypeStruct((1,), jnp.int32)),
-        in_specs=[SMEM, VMEM, HBM, HBM],
+        in_specs=[SMEM, VMEM, VMEM, VMEM],
         out_specs=(VMEM, VMEM, VMEM, SMEM),
-        scratch_shapes=[
-            pltpu.VMEM((ITERS, 2 * rows, width), f32),
-            pltpu.VMEM((4, lines, width), f32),
-            pltpu.SemaphoreType.DMA((2,)),
-        ],
         compiler_params=PARAMS,
         name="surface",
-    )(seam_codes, sums, in_hbm(basis), in_hbm(edges))
+    )(seam_codes, sums, basis, edges)
     south0, north0 = across(up0, down0)
     inside = inside_of(solved, surface, pltpu.VMEM)
 

time: 46.7 us -> 44.9 us (0.961)
  Pallas kernels: 17.5 us -> 13.8 us
  blocking collectives: 9.47 us -> 12.4 us
  local copies, waits for them, and re-layouts: 0.79 us -> 0.04 us
    all_to_all x1, blocking collectives: 9.47 us -> 12.4 us  [shards(): sums = lax.all_to_all(sums, 'face', 0, 0)]
    pallas_call x2, Pallas kernels: 3.28 us -> 1.88 us  [the longest x1 1.42 us: shards(): pl.pallas_call(outer_kernel, out_shape=(tile, tile, pltpu.VMEM((2 * rows,...]
    pallas_call x1, Pallas kernels: 2.12 us -> 0.91 us  [shards(): pl.pallas_call(surface_kernel, out_shape=(tile, line, line, jax.ShapeDtyp...]
    pallas_call x1, Pallas kernels: 4.92 us -> 4.06 us  [columns_after(): pl.pallas_call(column_kernel, out_shape=(place((3, levels, rows, width),...]
    cond x4 -> x0, local copies, waits for them, and re-layouts: 0.76 us -> none
    ppermute x2, starting transfers between devices: 8.86 us -> 9.41 us  [across(): lax.ppermute(down, 'face', downward)]
    ppermute x1, starting transfers between devices: 0.53 us -> 0.01 us  [shards(): below = lax.ppermute(up, 'face', upward)]
    ppermute x2, starting transfers between devices: 0.12 us -> 0.64 us  [across(): lax.ppermute(up, 'face', upward)]
  transfers between devices with their start and end apart: 6 -> 6, of which waited for: 2 -> 1; matrix products, arithmetic and copies ran while one was open for 0% -> 0% of each run, Pallas kernels for 7% -> 9%
where the time goes in v7:
time: 44.9 us; the launch traced here: 44.5 us
  starting transfers between devices  14.5 us (32%)
  Pallas kernels  13.8 us (31%)
  blocking collectives  12.4 us (28%)
  between operations  2.06 us (5%)
  waiting for transfers between devices  1.71 us (4%)
    all_to_all x1, blocking collectives, shards(): sums = lax.all_to_all(sums, 'face', 0, 0)  12.4 us
    ppermute x2, starting transfers between devices, across(): lax.ppermute(down, 'face', downward)  9.41 us
    ppermute x1, starting transfers between devices, shards(): above = lax.ppermute(down, 'face', downward)  4.44 us
    pallas_call x1, Pallas kernels, columns_after(): pl.pallas_call(column_kernel, out_shape=(place((3, levels, rows, width),...  4.06 us
    pallas_call x1, Pallas kernels, with_rims(): pl.pallas_call(rim_kernel, out_shape=pltpu.HBM((tracers, levels, rows, wi...  3.61 us
    pallas_call x1, Pallas kernels, inside_of(): pl.pallas_call(inside_kernel, out_shape=place((tracers, levels, rows, wid...  3.33 us
    ppermute x1, waiting for transfers between devices, shards(): below = lax.ppermute(up, 'face', upward)  1.7 us
    pallas_call x1, Pallas kernels, shards(): pl.pallas_call(outer_kernel, out_shape=(tile, tile, pltpu.VMEM((2 * rows,...  1.42 us
  transfers between devices with their start and end apart: 6, of which 1 were waited for; matrix products, arithmetic and copies ran while one was open for 0% of the time, Pallas kernels for 9%

profile of v7, /device:TPU:0, one launch (start us, length us, event | category | flops | bytes accessed | tf_op | source)
XLA Modules:
  0.0 44.5 jit_solution(6963393441784701986)
XLA Ops:
  1.3 1.4 %outer_rows.1 = (f32[8,1024]{1,0:T(8,128)}, f32[8,1024]{1,0:T(8,128)}, f32[16,1024]{1,0:T(8,128)S(1)}, f32[8,128]{1,0:T(8,128)}) custom-call(s32[1]{0:T(128)S(6)} %copy.17.seam, f32[8,1024]{1,0:T(8,128)} %eta.1, f32[8,1024]{1,0:T(8,128)} %damping.1), custom_call_target="tpu_custom_call" | custom-call | tf_op jit(solution)/shard_map/outer_rows/pallas_call | solution.py:392
  2.7 0.0 copy-start.17
  2.7 0.0 copy-start.16
  2.7 0.0 copy-start.2
  2.7 0.0 copy-start.5
  2.7 0.0 copy-start.10
  2.7 4.1 %columns.3 = (f32[3,50,8,1024]{3,2,1,0:T(8,128)S(1)}, f32[56,1024]{1,0:T(8,128)S(1)}, f32[56,1024]{1,0:T(8,128)S(1)}, f32[4,56,1024]{2,1,0:T(8,128)S(1)}) custom-call(s32[1]{0:T(128)S(6)} %copy.17.seam, f32[50]{0:T(128)} %thickness_from.1, f32[2,50,8,1024]{3,2,1,0:T(8,128)} %tracer.1, f32[49,8,1024]{2,1,0:T(8,128)} %mixing.1, f32[50,8,1024]{2,1,0:T(8,128)} %velocity_y.3, ...), custom_call_target="tpu_custom_call" | custom-call | flops 40000000 | bytes 13000000 | tf_op jit(solution)/shard_map/columns/pallas_call | solution.py:413
  6.8 0.6 %collective-permute-start.14 = (f32[56,1024]{1,0:T(8,128)S(1)}, f32[56,1024]{1,0:T(8,128)S(1)}, u32[]{:S(2)}, u32[]{:S(2)}) collective-permute-start(f32[56,1024]{1,0:T(8,128)S(1)} %get-tuple-element.84), channel_id=1, source_target_pairs={{0,1},{1,2},{2,3},{3,4},{4,5},{5,6},{6,7},{7,8},{8,9},{9,10},{10,1... | collective-permute-start | bytes 688136 | tf_op jit(solution)/shard_map/ppermute | solution.py:465
  7.4 5.0 %collective-permute-start.15 = (f32[56,1024]{1,0:T(8,128)S(1)}, f32[56,1024]{1,0:T(8,128)S(1)}, u32[]{:S(2)}, u32[]{:S(2)}) collective-permute-start(f32[56,1024]{1,0:T(8,128)S(1)} %get-tuple-element.85), channel_id=1, source_target_pairs={{1,0},{2,1},{3,2},{4,3},{5,4},{6,5},{7,6},{8,7},{9,8},{10,9},{11,1... | collective-permute-start | bytes 688136 | tf_op jit(solution)/shard_map/ppermute | solution.py:465
  12.3 0.0 copy-done.17
  12.4 0.0 collective-permute-start.12
  12.4 0.0 copy-done.16
  12.4 4.4 %collective-permute-start.13 = (f32[8,1024]{1,0:T(8,128)S(1)}, f32[8,1024]{1,0:T(8,128)S(1)}, u32[]{:S(2)}, u32[]{:S(2)}) collective-permute-start(f32[8,1024]{1,0:T(8,128)S(1)} %copy-done.16), channel_id=1, source_target_pairs={{1,0},{2,1},{3,2},{4,3},{5,4},{6,5},{7,6},{8,7},{9,8},{10,9},{11,1... | collective-permute-start | bytes 98312 | tf_op jit(solution)/shard_map/ppermute | solution.py:405
  16.8 1.7 %collective-permute-done.12.below = f32[8,1024]{1,0:T(8,128)S(1)} collective-permute-done((f32[8,1024]{1,0:T(8,128)S(1)}, f32[8,1024]{1,0:T(8,128)S(1)}, u32[]{:S(2)}, u32[]{:S(2)}) %collective-permute-start.12) | collective-permute-done | bytes 32800 | tf_op jit(solution)/shard_map/ppermute | solution.py:404
  18.5 0.0 collective-permute-done.13.above
  18.5 0.5 %surface_basis.1 = (f32[4,16,1024]{2,1,0:T(8,128)S(1)}, f32[16,8,128]{2,1,0:T(8,128)S(1)}) custom-call(s32[1]{0:T(128)S(6)} %copy.17.seam, f32[16,1024]{1,0:T(8,128)S(1)} %get-tuple-element.79.own_rows, f32[8,1024]{1,0:T(8,128)S(1)} %collective-permute-done.12.below, f32[8,1024]{1,0:T(8,128)S(1)} %collective-permute-done.13.above), custom_call_target="tpu_custom_call" | custom-call | tf_op jit(solution)/shard_map/surface_basis/pallas_call | solution.py:467
  19.0 12.4 %all_to_all.5.sums = f32[16,8,128]{2,1,0:T(8,128)S(1)} all-to-all(f32[16,8,128]{2,1,0:T(8,128)S(1)} %get-tuple-element.82), channel_id=1, replica_groups=mesh['ens'=2,'face'=16] {'face'}, dimensions={0} | all-to-all | bytes 131072 | tf_op jit(solution)/shard_map/all_to_all | solution.py:478
  31.4 0.0 collective-permute-done.14
  31.4 0.0 copy-start.14
  31.4 0.0 collective-permute-done.15
  31.4 0.0 copy-start.15
  31.4 0.9 %surface.1 = (f32[8,1024]{1,0:T(8,128)}, f32[56,1024]{1,0:T(8,128)S(1)}, f32[56,1024]{1,0:T(8,128)S(1)}, s32[1]{0:T(128)}) custom-call(s32[1]{0:T(128)S(6)} %copy.17.seam, f32[16,8,128]{2,1,0:T(8,128)S(1)} %all_to_all.5.sums, f32[4,16,1024]{2,1,0:T(8,128)S(1)} %get-tuple-element.87.basis, f32[4,56,1024]{2,1,0:T(8,128)S(1)} %get-tuple-element.88.edges), custom_call_target="tpu_custom_call" | custom-call | tf_op jit(solution)/shard_map/surface/pallas_call | solution.py:484
  32.3 0.1 collective-permute-start.16
  32.4 4.4 %collective-permute-start.17 = (f32[56,1024]{1,0:T(8,128)S(1)}, f32[56,1024]{1,0:T(8,128)S(1)}, u32[]{:S(2)}, u32[]{:S(2)}) collective-permute-start(f32[56,1024]{1,0:T(8,128)S(1)} %get-tuple-element.93), channel_id=1, source_target_pairs={{1,0},{2,1},{3,2},{4,3},{5,4},{6,5},{7,6},{8,7},{9,8},{10,9},{11,1... | collective-permute-start | bytes 688136 | tf_op jit(solution)/shard_map/ppermute | solution.py:465
  36.8 0.0 copy-done.14
  36.8 0.0 copy-done.15
  36.8 0.0 copy-done.2
  36.8 0.0 copy-done.5
  36.8 0.0 copy-done.10
  36.8 0.0 copy-start.7
  36.8 0.0 copy-start.13
  36.9 3.3 %inside.3 = f32[2,50,8,1024]{3,2,1,0:T(8,128)S(1)} custom-call(f32[3,50,8,1024]{3,2,1,0:T(8,128)S(1)} %get-tuple-element.90.solved, f32[50,8,1024]{2,1,0:T(8,128)S(1)} %copy-done.5, f32[50,8,1024]{2,1,0:T(8,128)S(1)} %copy-done.2, s32[8,1024]{1,0:T(8,128)S(1)} %copy-done.10, f32[8,1024]{1,0:T(8,128)} %get-tuple-element.91.surface), custom_call_target="tpu_custom_call" | custom-call | flops 1000 | bytes 1000 | tf_op jit(solution)/shard_map/inside/pallas_call | solution.py:440
  40.8 0.0 collective-permute-done.16
  40.9 0.0 collective-permute-done.17
  40.9 0.0 copy-done.7
  40.9 0.0 copy-done.13
  40.9 3.6 %conditional.1 = (f32[8,1024]{1,0:T(8,128)}, f32[2,50,8,1024]{3,2,1,0:T(8,128)}) conditional(s32[]{:T(128)} %bitcast.1, (s32[1]{0:T(128)}, f32[50]{0:T(128)}, f32[2,50,8,1024]{3,2,1,0:T(8,128)}, f32[49,8,1024]{2,1,0:T(8,128)}, f32[50,8,1024]{2,1,0:T(8,128)S(1)}, /*index=5*/s32[8,1024]{1,0:T(8,128)S(1)}, f32[8,128]{1,0:T(8,128)}, ...), branch_computations={%region_0.17_spmd, %region_17.18_spmd} | conditional | flops 40672752 | bytes 79160584 | solution.py:512
  40.9 3.6 %rims.3 = f32[2,50,8,1024]{3,2,1,0:T(8,128)} custom-call(s32[1]{0:T(128)} %get-tuple-element.52.seam, f32[2,50,8,1024]{3,2,1,0:T(8,128)S(1)} %get-tuple-element.53.inside, s32[8,1024]{1,0:T(8,128)S(1)} %get-tuple-element.54.wet, f32[56,1024]{1,0:T(8,128)S(1)} %get-tuple-element.55.south0, f32[56,1024]{1,0:T(8,128)S(1)} %get-tuple-element.56.north0, ...), custom_call_target="tpu_custom_call" | custom-call | tf_op jit(solution)/shard_map/cond/branch_1_fun/rims/pallas_call | solution.py:451
Async XLA Ops:
  2.7 9.7 %copy-start.17 = (f32[8,1024]{1,0:T(8,128)S(1)}, f32[8,1024]{1,0:T(8,128)}, u32[]{:S(2)}) copy-start(f32[8,1024]{1,0:T(8,128)} %get-tuple-element.80) | copy-start | bytes 98308
  2.7 9.7 %copy-start.16 = (f32[8,1024]{1,0:T(8,128)S(1)}, f32[8,1024]{1,0:T(8,128)}, u32[]{:S(2)}) copy-start(f32[8,1024]{1,0:T(8,128)} %get-tuple-element.81) | copy-start | bytes 98308
  2.7 34.1 %copy-start.2 = (f32[50,8,1024]{2,1,0:T(8,128)S(1)}, f32[50,8,1024]{2,1,0:T(8,128)}, u32[]{:S(2)}) copy-start(f32[50,8,1024]{2,1,0:T(8,128)} %velocity_y.3) | copy-start | bytes 4915204
  2.7 34.1 %copy-start.5 = (f32[50,8,1024]{2,1,0:T(8,128)S(1)}, f32[50,8,1024]{2,1,0:T(8,128)}, u32[]{:S(2)}) copy-start(f32[50,8,1024]{2,1,0:T(8,128)} %velocity_x.1) | copy-start | bytes 4915204
  2.7 34.1 %copy-start.10 = (s32[8,1024]{1,0:T(8,128)S(1)}, s32[8,1024]{1,0:T(8,128)}, u32[]{:S(2)}) copy-start(s32[8,1024]{1,0:T(8,128)} %wet.3) | copy-start | bytes 98308
  6.8 24.6 %collective-permute-start.14 = (f32[56,1024]{1,0:T(8,128)S(1)}, f32[56,1024]{1,0:T(8,128)S(1)}, u32[]{:S(2)}, u32[]{:S(2)}) collective-permute-start(f32[56,1024]{1,0:T(8,128)S(1)} %get-tuple-element.84), channel_id=1, source_target_pairs={{0,1},{1,2},{2,3},{3,4},{4,5},{5,6},{6,7},{7,8},{8,9},{9,10},{10,1... | collective-permute-start | bytes 688136 | tf_op jit(solution)/shard_map/ppermute | solution.py:465
  7.4 24.0 %collective-permute-start.15 = (f32[56,1024]{1,0:T(8,128)S(1)}, f32[56,1024]{1,0:T(8,128)S(1)}, u32[]{:S(2)}, u32[]{:S(2)}) collective-permute-start(f32[56,1024]{1,0:T(8,128)S(1)} %get-tuple-element.85), channel_id=1, source_target_pairs={{1,0},{2,1},{3,2},{4,3},{5,4},{6,5},{7,6},{8,7},{9,8},{10,9},{11,1... | collective-permute-start | bytes 688136 | tf_op jit(solution)/shard_map/ppermute | solution.py:465
  12.4 6.1 %collective-permute-start.12 = (f32[8,1024]{1,0:T(8,128)S(1)}, f32[8,1024]{1,0:T(8,128)S(1)}, u32[]{:S(2)}, u32[]{:S(2)}) collective-permute-start(f32[8,1024]{1,0:T(8,128)S(1)} %copy-done.17), channel_id=1, source_target_pairs={{0,1},{1,2},{2,3},{3,4},{4,5},{5,6},{6,7},{7,8},{8,9},{9,10},{10,1... | collective-permute-start | bytes 98312 | tf_op jit(solution)/shard_map/ppermute | solution.py:404
  12.4 6.1 %collective-permute-start.13 = (f32[8,1024]{1,0:T(8,128)S(1)}, f32[8,1024]{1,0:T(8,128)S(1)}, u32[]{:S(2)}, u32[]{:S(2)}) collective-permute-start(f32[8,1024]{1,0:T(8,128)S(1)} %copy-done.16), channel_id=1, source_target_pairs={{1,0},{2,1},{3,2},{4,3},{5,4},{6,5},{7,6},{8,7},{9,8},{10,9},{11,1... | collective-permute-start | bytes 98312 | tf_op jit(solution)/shard_map/ppermute | solution.py:405
  31.4 5.4 %copy-start.14 = (f32[56,1024]{1,0:T(8,128)}, f32[56,1024]{1,0:T(8,128)S(1)}, u32[]{:S(2)}) copy-start(f32[56,1024]{1,0:T(8,128)S(1)} %collective-permute-done.14) | copy-start | bytes 688132
  31.4 5.4 %copy-start.15 = (f32[56,1024]{1,0:T(8,128)}, f32[56,1024]{1,0:T(8,128)S(1)}, u32[]{:S(2)}) copy-start(f32[56,1024]{1,0:T(8,128)S(1)} %collective-permute-done.15) | copy-start | bytes 688132
  32.3 8.5 %collective-permute-start.16 = (f32[56,1024]{1,0:T(8,128)S(1)}, f32[56,1024]{1,0:T(8,128)S(1)}, u32[]{:S(2)}, u32[]{:S(2)}) collective-permute-start(f32[56,1024]{1,0:T(8,128)S(1)} %get-tuple-element.92), channel_id=1, source_target_pairs={{0,1},{1,2},{2,3},{3,4},{4,5},{5,6},{6,7},{7,8},{8,9},{9,10},{10,1... | collective-permute-start | bytes 688136 | tf_op jit(solution)/shard_map/ppermute | solution.py:465
  32.4 8.5 %collective-permute-start.17 = (f32[56,1024]{1,0:T(8,128)S(1)}, f32[56,1024]{1,0:T(8,128)S(1)}, u32[]{:S(2)}, u32[]{:S(2)}) collective-permute-start(f32[56,1024]{1,0:T(8,128)S(1)} %get-tuple-element.93), channel_id=1, source_target_pairs={{1,0},{2,1},{3,2},{4,3},{5,4},{6,5},{7,6},{8,7},{9,8},{10,9},{11,1... | collective-permute-start | bytes 688136 | tf_op jit(solution)/shard_map/ppermute | solution.py:465
  36.8 4.0 %copy-start.7 = (f32[8,1024]{1,0:T(8,128)S(1)}, f32[8,1024]{1,0:T(8,128)}, u32[]{:S(2)}) copy-start(f32[8,1024]{1,0:T(8,128)} %eta.1) | copy-start | bytes 98308
  36.8 4.0 %copy-start.13 = (f32[8,1024]{1,0:T(8,128)S(1)}, f32[8,1024]{1,0:T(8,128)}, u32[]{:S(2)}) copy-start(f32[8,1024]{1,0:T(8,128)} %damping.1) | copy-start | bytes 98308

commit v8 on v7

--- a/solution.py
+++ b/solution.py
@@ -475,9 +475,9 @@
         compiler_params=PARAMS,
         name="surface_basis",
     )(seam_codes, own, below, above)
+    solved, up1, down1, edges = columns_after(in_hbm(mark), pltpu.VMEM)
+    sums, up1, down1 = lax.optimization_barrier((sums, up1, down1))
     sums = lax.all_to_all(sums, "face", 0, 0)
-
-    solved, up1, down1, edges = columns_after(in_hbm(mark), pltpu.VMEM)
     south1, north1 = across(up1, down1)
     sums, south1, north1 = lax.optimization_barrier((sums, south1, north1))
 

time: 44.9 us -> 40.2 us (0.90)
  blocking collectives: 12.4 us -> 9.47 us
  waiting for transfers between devices: 1.71 us -> 0.02 us
    all_to_all x1, blocking collectives: 12.4 us -> 9.47 us  [shards(): sums = lax.all_to_all(sums, 'face', 0, 0)]
    ppermute x1, waiting for transfers between devices: 1.7 us -> 0.01 us  [shards(): below = lax.ppermute(up, 'face', upward)]
    ppermute x1, starting transfers between devices: 4.44 us -> 4.99 us  [shards(): above = lax.ppermute(down, 'face', downward)]
    ppermute x2, starting transfers between devices: 9.41 us -> 8.86 us  [across(): lax.ppermute(down, 'face', downward)]
    ppermute x2, starting transfers between devices: 0.64 us -> 0.12 us  [across(): lax.ppermute(up, 'face', upward)]
    ppermute x1, starting transfers between devices: 0.01 us -> 0.45 us  [shards(): below = lax.ppermute(up, 'face', upward)]
  transfers between devices with their start and end apart: 6 -> 6, of which waited for: 1 -> 0; matrix products, arithmetic and copies ran while one was open for 0% -> 0% of each run, Pallas kernels for 9% -> 18%
where the time goes in v8:
time: 40.2 us; the launch traced here: 39.9 us
  starting transfers between devices  14.4 us (36%)
  Pallas kernels  13.9 us (35%)
  blocking collectives  9.47 us (24%)
  between operations  2.06 us (5%)
    all_to_all x1, blocking collectives, shards(): sums = lax.all_to_all(sums, 'face', 0, 0)  9.47 us
    ppermute x2, starting transfers between devices, across(): lax.ppermute(down, 'face', downward)  8.86 us
    ppermute x1, starting transfers between devices, shards(): above = lax.ppermute(down, 'face', downward)  4.99 us
    pallas_call x1, Pallas kernels, columns_after(): pl.pallas_call(column_kernel, out_shape=(place((3, levels, rows, width),...  4.05 us
    pallas_call x1, Pallas kernels, with_rims(): pl.pallas_call(rim_kernel, out_shape=pltpu.HBM((tracers, levels, rows, wi...  3.61 us
    pallas_call x1, Pallas kernels, inside_of(): pl.pallas_call(inside_kernel, out_shape=place((tracers, levels, rows, wid...  3.33 us
    pallas_call x1, Pallas kernels, shards(): pl.pallas_call(outer_kernel, out_shape=(tile, tile, pltpu.VMEM((2 * rows,...  1.5 us
    pallas_call x1, Pallas kernels, shards(): pl.pallas_call(surface_kernel, out_shape=(tile, line, line, jax.ShapeDtyp...  0.91 us
  transfers between devices with their start and end apart: 6, of which 0 were waited for; matrix products, arithmetic and copies ran while one was open for 0% of the time, Pallas kernels for 18%

profile of v8, /device:TPU:0, one launch (start us, length us, event | category | flops | bytes accessed | tf_op | source)
XLA Modules:
  0.0 39.9 jit_solution(9508977871151643047)
XLA Ops:
  1.3 1.5 %outer_rows.1 = (f32[8,1024]{1,0:T(8,128)}, f32[8,1024]{1,0:T(8,128)}, f32[16,1024]{1,0:T(8,128)S(1)}, f32[8,128]{1,0:T(8,128)}) custom-call(s32[1]{0:T(128)S(6)} %copy.17.seam, f32[8,1024]{1,0:T(8,128)} %eta.1, f32[8,1024]{1,0:T(8,128)} %damping.1), custom_call_target="tpu_custom_call" | custom-call | tf_op jit(solution)/shard_map/outer_rows/pallas_call | solution.py:392
  2.8 0.5 %collective-permute-start.12 = (f32[8,1024]{1,0:T(8,128)}, f32[8,1024]{1,0:T(8,128)S(1)}, u32[]{:S(2)}, u32[]{:S(2)}) collective-permute-start(f32[8,1024]{1,0:T(8,128)} %get-tuple-element.83), channel_id=1, source_target_pairs={{0,1},{1,2},{2,3},{3,4},{4,5},{5,6},{6,7},{7,8},{8,9},{9,10},{10,1... | collective-permute-start | bytes 98312 | tf_op jit(solution)/shard_map/ppermute | solution.py:404
  3.2 5.0 %collective-permute-start.13 = (f32[8,1024]{1,0:T(8,128)}, f32[8,1024]{1,0:T(8,128)S(1)}, u32[]{:S(2)}, u32[]{:S(2)}) collective-permute-start(f32[8,1024]{1,0:T(8,128)} %get-tuple-element.84), channel_id=1, source_target_pairs={{1,0},{2,1},{3,2},{4,3},{5,4},{6,5},{7,6},{8,7},{9,8},{10,9},{11,1... | collective-permute-start | bytes 98312 | tf_op jit(solution)/shard_map/ppermute | solution.py:405
  8.2 0.0 copy-start.2
  8.2 0.0 copy-start.5
  8.2 0.0 copy-start.10
  8.2 4.0 %columns.3 = (f32[3,50,8,1024]{3,2,1,0:T(8,128)S(1)}, f32[56,1024]{1,0:T(8,128)S(1)}, f32[56,1024]{1,0:T(8,128)S(1)}, f32[4,56,1024]{2,1,0:T(8,128)S(1)}) custom-call(s32[1]{0:T(128)S(6)} %copy.17.seam, f32[50]{0:T(128)} %thickness_from.1, f32[2,50,8,1024]{3,2,1,0:T(8,128)} %tracer.1, f32[49,8,1024]{2,1,0:T(8,128)} %mixing.1, f32[50,8,1024]{2,1,0:T(8,128)} %velocity_y.3, ...), custom_call_target="tpu_custom_call" | custom-call | flops 40000000 | bytes 13000000 | tf_op jit(solution)/shard_map/columns/pallas_call | solution.py:413
  12.3 0.0 collective-permute-done.12.below
  12.3 0.0 collective-permute-done.13.above
  12.3 0.5 %surface_basis.1 = (f32[4,16,1024]{2,1,0:T(8,128)S(1)}, f32[16,8,128]{2,1,0:T(8,128)S(1)}) custom-call(s32[1]{0:T(128)S(6)} %copy.17.seam, f32[16,1024]{1,0:T(8,128)S(1)} %get-tuple-element.82.own_rows, f32[8,1024]{1,0:T(8,128)S(1)} %collective-permute-done.12.below, f32[8,1024]{1,0:T(8,128)S(1)} %collective-permute-done.13.above), custom_call_target="tpu_custom_call" | custom-call | tf_op jit(solution)/shard_map/surface_basis/pallas_call | solution.py:467
  12.8 0.1 collective-permute-start.14
  12.8 4.4 %collective-permute-start.15 = (f32[56,1024]{1,0:T(8,128)S(1)}, f32[56,1024]{1,0:T(8,128)S(1)}, u32[]{:S(2)}, u32[]{:S(2)}) collective-permute-start(f32[56,1024]{1,0:T(8,128)S(1)} %get-tuple-element.91), channel_id=1, source_target_pairs={{1,0},{2,1},{3,2},{4,3},{5,4},{6,5},{7,6},{8,7},{9,8},{10,9},{11,1... | collective-permute-start | bytes 688136 | tf_op jit(solution)/shard_map/ppermute | solution.py:465
  17.3 9.5 %all_to_all.5.sums = f32[16,8,128]{2,1,0:T(8,128)S(1)} all-to-all(f32[16,8,128]{2,1,0:T(8,128)S(1)} %get-tuple-element.89), channel_id=1, replica_groups=mesh['ens'=2,'face'=16] {'face'}, dimensions={0} | all-to-all | bytes 131072 | tf_op jit(solution)/shard_map/all_to_all | solution.py:480
  26.7 0.0 collective-permute-done.14
  26.7 0.0 copy-start.14
  26.7 0.0 collective-permute-done.15
  26.7 0.0 copy-start.15
  26.8 0.9 %surface.1 = (f32[8,1024]{1,0:T(8,128)}, f32[56,1024]{1,0:T(8,128)S(1)}, f32[56,1024]{1,0:T(8,128)S(1)}, s32[1]{0:T(128)}) custom-call(s32[1]{0:T(128)S(6)} %copy.17.seam, f32[16,8,128]{2,1,0:T(8,128)S(1)} %all_to_all.5.sums, f32[4,16,1024]{2,1,0:T(8,128)S(1)} %get-tuple-element.93.basis, f32[4,56,1024]{2,1,0:T(8,128)S(1)} %get-tuple-element.94.edges), custom_call_target="tpu_custom_call" | custom-call | tf_op jit(solution)/shard_map/surface/pallas_call | solution.py:484
  27.7 0.1 collective-permute-start.16
  27.7 4.4 %collective-permute-start.17 = (f32[56,1024]{1,0:T(8,128)S(1)}, f32[56,1024]{1,0:T(8,128)S(1)}, u32[]{:S(2)}, u32[]{:S(2)}) collective-permute-start(f32[56,1024]{1,0:T(8,128)S(1)} %get-tuple-element.99), channel_id=1, source_target_pairs={{1,0},{2,1},{3,2},{4,3},{5,4},{6,5},{7,6},{8,7},{9,8},{10,9},{11,1... | collective-permute-start | bytes 688136 | tf_op jit(solution)/shard_map/ppermute | solution.py:465
  32.2 0.0 copy-done.14
  32.2 0.0 copy-done.15
  32.2 0.0 copy-done.2
  32.2 0.0 copy-done.5
  32.2 0.0 copy-done.10
  32.2 0.0 copy-start.7
  32.2 0.0 copy-start.13
  32.2 3.3 %inside.3 = f32[2,50,8,1024]{3,2,1,0:T(8,128)S(1)} custom-call(f32[3,50,8,1024]{3,2,1,0:T(8,128)S(1)} %get-tuple-element.96.solved, f32[50,8,1024]{2,1,0:T(8,128)S(1)} %copy-done.5, f32[50,8,1024]{2,1,0:T(8,128)S(1)} %copy-done.2, s32[8,1024]{1,0:T(8,128)S(1)} %copy-done.10, f32[8,1024]{1,0:T(8,128)} %get-tuple-element.97.surface), custom_call_target="tpu_custom_call" | custom-call | flops 1000 | bytes 1000 | tf_op jit(solution)/shard_map/inside/pallas_call | solution.py:440
  36.2 0.0 collective-permute-done.16
  36.2 0.0 collective-permute-done.17
  36.2 0.0 copy-done.7
  36.2 0.0 copy-done.13
  36.2 3.6 %conditional.1 = (f32[8,1024]{1,0:T(8,128)}, f32[2,50,8,1024]{3,2,1,0:T(8,128)}) conditional(s32[]{:T(128)} %bitcast.1, (s32[1]{0:T(128)}, f32[50]{0:T(128)}, f32[2,50,8,1024]{3,2,1,0:T(8,128)}, f32[49,8,1024]{2,1,0:T(8,128)}, f32[50,8,1024]{2,1,0:T(8,128)S(1)}, /*index=5*/s32[8,1024]{1,0:T(8,128)S(1)}, f32[8,128]{1,0:T(8,128)}, ...), branch_computations={%region_0.17_spmd, %region_17.18_spmd} | conditional | flops 40672752 | bytes 79160584 | solution.py:512
  36.3 3.6 %rims.3 = f32[2,50,8,1024]{3,2,1,0:T(8,128)} custom-call(s32[1]{0:T(128)} %get-tuple-element.52.seam, f32[2,50,8,1024]{3,2,1,0:T(8,128)S(1)} %get-tuple-element.53.inside, s32[8,1024]{1,0:T(8,128)S(1)} %get-tuple-element.54.wet, f32[56,1024]{1,0:T(8,128)S(1)} %get-tuple-element.55.south0, f32[56,1024]{1,0:T(8,128)S(1)} %get-tuple-element.56.north0, ...), custom_call_target="tpu_custom_call" | custom-call | tf_op jit(solution)/shard_map/cond/branch_1_fun/rims/pallas_call | solution.py:451
Async XLA Ops:
  2.8 9.5 %collective-permute-start.12 = (f32[8,1024]{1,0:T(8,128)}, f32[8,1024]{1,0:T(8,128)S(1)}, u32[]{:S(2)}, u32[]{:S(2)}) collective-permute-start(f32[8,1024]{1,0:T(8,128)} %get-tuple-element.83), channel_id=1, source_target_pairs={{0,1},{1,2},{2,3},{3,4},{4,5},{5,6},{6,7},{7,8},{8,9},{9,10},{10,1... | collective-permute-start | bytes 98312 | tf_op jit(solution)/shard_map/ppermute | solution.py:404
  3.2 9.1 %collective-permute-start.13 = (f32[8,1024]{1,0:T(8,128)}, f32[8,1024]{1,0:T(8,128)S(1)}, u32[]{:S(2)}, u32[]{:S(2)}) collective-permute-start(f32[8,1024]{1,0:T(8,128)} %get-tuple-element.84), channel_id=1, source_target_pairs={{1,0},{2,1},{3,2},{4,3},{5,4},{6,5},{7,6},{8,7},{9,8},{10,9},{11,1... | collective-permute-start | bytes 98312 | tf_op jit(solution)/shard_map/ppermute | solution.py:405
  8.2 24.0 %copy-start.2 = (f32[50,8,1024]{2,1,0:T(8,128)S(1)}, f32[50,8,1024]{2,1,0:T(8,128)}, u32[]{:S(2)}) copy-start(f32[50,8,1024]{2,1,0:T(8,128)} %velocity_y.3) | copy-start | bytes 4915204
  8.2 24.0 %copy-start.5 = (f32[50,8,1024]{2,1,0:T(8,128)S(1)}, f32[50,8,1024]{2,1,0:T(8,128)}, u32[]{:S(2)}) copy-start(f32[50,8,1024]{2,1,0:T(8,128)} %velocity_x.1) | copy-start | bytes 4915204
  8.2 24.0 %copy-start.10 = (s32[8,1024]{1,0:T(8,128)S(1)}, s32[8,1024]{1,0:T(8,128)}, u32[]{:S(2)}) copy-start(s32[8,1024]{1,0:T(8,128)} %wet.3) | copy-start | bytes 98308
  12.8 14.0 %collective-permute-start.14 = (f32[56,1024]{1,0:T(8,128)S(1)}, f32[56,1024]{1,0:T(8,128)S(1)}, u32[]{:S(2)}, u32[]{:S(2)}) collective-permute-start(f32[56,1024]{1,0:T(8,128)S(1)} %get-tuple-element.90), channel_id=1, source_target_pairs={{0,1},{1,2},{2,3},{3,4},{4,5},{5,6},{6,7},{7,8},{8,9},{9,10},{10,1... | collective-permute-start | bytes 688136 | tf_op jit(solution)/shard_map/ppermute | solution.py:465
  12.8 13.9 %collective-permute-start.15 = (f32[56,1024]{1,0:T(8,128)S(1)}, f32[56,1024]{1,0:T(8,128)S(1)}, u32[]{:S(2)}, u32[]{:S(2)}) collective-permute-start(f32[56,1024]{1,0:T(8,128)S(1)} %get-tuple-element.91), channel_id=1, source_target_pairs={{1,0},{2,1},{3,2},{4,3},{5,4},{6,5},{7,6},{8,7},{9,8},{10,9},{11,1... | collective-permute-start | bytes 688136 | tf_op jit(solution)/shard_map/ppermute | solution.py:465
  26.7 5.4 %copy-start.14 = (f32[56,1024]{1,0:T(8,128)}, f32[56,1024]{1,0:T(8,128)S(1)}, u32[]{:S(2)}) copy-start(f32[56,1024]{1,0:T(8,128)S(1)} %collective-permute-done.14) | copy-start | bytes 688132
  26.7 5.4 %copy-start.15 = (f32[56,1024]{1,0:T(8,128)}, f32[56,1024]{1,0:T(8,128)S(1)}, u32[]{:S(2)}) copy-start(f32[56,1024]{1,0:T(8,128)S(1)} %collective-permute-done.15) | copy-start | bytes 688132
  27.7 8.5 %collective-permute-start.16 = (f32[56,1024]{1,0:T(8,128)S(1)}, f32[56,1024]{1,0:T(8,128)S(1)}, u32[]{:S(2)}, u32[]{:S(2)}) collective-permute-start(f32[56,1024]{1,0:T(8,128)S(1)} %get-tuple-element.98), channel_id=1, source_target_pairs={{0,1},{1,2},{2,3},{3,4},{4,5},{5,6},{6,7},{7,8},{8,9},{9,10},{10,1... | collective-permute-start | bytes 688136 | tf_op jit(solution)/shard_map/ppermute | solution.py:465
  27.7 8.5 %collective-permute-start.17 = (f32[56,1024]{1,0:T(8,128)S(1)}, f32[56,1024]{1,0:T(8,128)S(1)}, u32[]{:S(2)}, u32[]{:S(2)}) collective-permute-start(f32[56,1024]{1,0:T(8,128)S(1)} %get-tuple-element.99), channel_id=1, source_target_pairs={{1,0},{2,1},{3,2},{4,3},{5,4},{6,5},{7,6},{8,7},{9,8},{10,9},{11,1... | collective-permute-start | bytes 688136 | tf_op jit(solution)/shard_map/ppermute | solution.py:465
  32.2 4.0 %copy-start.7 = (f32[8,1024]{1,0:T(8,128)S(1)}, f32[8,1024]{1,0:T(8,128)}, u32[]{:S(2)}) copy-start(f32[8,1024]{1,0:T(8,128)} %eta.1) | copy-start | bytes 98308
  32.2 4.0 %copy-start.13 = (f32[8,1024]{1,0:T(8,128)S(1)}, f32[8,1024]{1,0:T(8,128)}, u32[]{:S(2)}) copy-start(f32[8,1024]{1,0:T(8,128)} %damping.1) | copy-start | bytes 98308

commit v9 on v7

--- a/solution.py
+++ b/solution.py
@@ -200,11 +200,13 @@
 
 def outer_lines(seam, fields, edges, up, down):
     turned = seam[0] == 1
-    for k in range(0, up.shape[0], SUBLANES):
+    for k in range(0, up.shape[1], SUBLANES):
         at = slice(k, k + SUBLANES)
         top = edges[0, at, :] + fields[SUBLANES - 1 : SUBLANES, :] * edges[1, at, :]
-        up[at, :] = jnp.where(turned, flip_lanes(top), top)
-        down[at, :] = edges[2, at, :] + fields[:1, :] * edges[3, at, :]
+        up[0, at, :] = jnp.where(turned, flip_lanes(top), top)
+        down[0, at, :] = edges[2, at, :] + fields[:1, :] * edges[3, at, :]
+        up[1, at, :] = edges[4, at, :]
+        down[1, at, :] = edges[5, at, :]
 
 
 def surface_kernel(seam, sums, basis, edges, surface, up, down, sound):
@@ -231,7 +233,7 @@
 
 
 def column_kernel(
-    seam, thickness_from, tracer, mixing, velocity_y, wet, after, solved, up, down, edges,
+    seam, thickness_from, tracer, mixing, velocity_y, wet, after, solved, edges,
     thickness, depth_at, tracer_at, mixing_at, velocity_at, ratio_at, sems,
 ):
     levels = tracer.shape[1]
@@ -306,8 +308,8 @@
         to_up = diffusion - advection * velocity_at[pl.ds(k, n), SUBLANES - 1, :]
         to_down = diffusion + advection * velocity_at[pl.ds(k, n), 0, :]
         top = solved[1, pl.ds(k, n), SUBLANES - 1, :] * to_up
-        up[at, :] = jnp.where(turned, flip_some(top), top)
-        down[at, :] = solved[1, pl.ds(k, n), 0, :] * to_down
+        edges[4, at, :] = jnp.where(turned, flip_some(top), top)
+        edges[5, at, :] = solved[1, pl.ds(k, n), 0, :] * to_down
         for t in range(2):
             edges[t, at, :] = solved[2 * t, pl.ds(k, n), SUBLANES - 1, :] * to_up
             edges[2 + t, at, :] = solved[2 * t, pl.ds(k, n), 0, :] * to_down
@@ -345,7 +347,7 @@
     lax.fori_loop(0, levels, level, 0, unroll=5)
 
 
-def rim_kernel(seam, inside, wet, south0, north0, south1, north1, result, result_at, out_sems):
+def rim_kernel(seam, inside, wet, below, above, result, result_at, out_sems):
     levels = inside.shape[1]
     width = wet.shape[1]
     turned = seam[0] == 1
@@ -356,9 +358,9 @@
         at = pl.ds(k, n)
         index = k + lax.broadcasted_iota(jnp.int32, (n, width), 0)
         result_at[:, at] = inside[:, at]
-        for t, (south_from, north_from) in enumerate(((south0, north0), (south1, north1))):
-            south = south_from[k : k + n, :]
-            north = north_from[k : k + n, :]
+        for t in range(2):
+            south = below[t, k : k + n, :]
+            north = above[t, k : k + n, :]
             north = jnp.where(turned, flip_some(north), north)
             result_at[t, at, 0, :] += jnp.where(index < depth_south, south, 0.0)
             result_at[t, at, SUBLANES - 1, :] += jnp.where(index < depth_north, north, 0.0)
@@ -387,7 +389,7 @@
     tile = jax.ShapeDtypeStruct((rows, width), f32)
     ext = pltpu.VMEM((ITERS, 2 * rows, width), f32)
     lines = -(-levels // SUBLANES) * SUBLANES
-    line = jax.ShapeDtypeStruct((lines, width), f32)
+    line = jax.ShapeDtypeStruct((tracers, lines, width), f32)
 
     up, down, own, mark = pl.pallas_call(
         outer_kernel,
@@ -414,12 +416,10 @@
             column_kernel,
             out_shape=(
                 place((3, levels, rows, width), f32),
-                line,
-                line,
-                place((4, lines, width), f32),
+                place((6, lines, width), f32),
             ),
             in_specs=[SMEM] + [HBM] * 6,
-            out_specs=(VMEM, VMEM, VMEM, VMEM),
+            out_specs=(VMEM, VMEM),
             scratch_shapes=[
                 pltpu.SMEM((levels,), f32),
                 pltpu.VMEM((rows, width), jnp.int32),
@@ -451,7 +451,7 @@
         return pl.pallas_call(
             rim_kernel,
             out_shape=pltpu.HBM((tracers, levels, rows, width), f32),
-            in_specs=[SMEM] + [VMEM] * 6,
+            in_specs=[SMEM] + [VMEM] * 4,
             out_specs=HBM,
             scratch_shapes=[
                 pltpu.VMEM((tracers, levels, rows, width), f32),
@@ -475,13 +475,9 @@
         compiler_params=PARAMS,
         name="surface_basis",
     )(seam_codes, own, below, above)
+    solved, edges = columns_after(in_hbm(mark), pltpu.VMEM)
     sums = lax.all_to_all(sums, "face", 0, 0)
-
-    solved, up1, down1, edges = columns_after(in_hbm(mark), pltpu.VMEM)
-    south1, north1 = across(up1, down1)
-    sums, south1, north1 = lax.optimization_barrier((sums, south1, north1))
-
-    surface, up0, down0, sound = pl.pallas_call(
+    surface, up, down, sound = pl.pallas_call(
         surface_kernel,
         out_shape=(tile, line, line, jax.ShapeDtypeStruct((1,), jnp.int32)),
         in_specs=[SMEM, VMEM, VMEM, VMEM],
@@ -489,16 +485,16 @@
         compiler_params=PARAMS,
         name="surface",
     )(seam_codes, sums, basis, edges)
-    south0, north0 = across(up0, down0)
+    below, above = across(up, down)
     inside = inside_of(solved, surface, pltpu.VMEM)
 
-    def by_moments(surface, inside, south0, north0, south1, north1):
-        return with_rims(inside, south0, north0, south1, north1), surface
-
-    def by_steps(surface, inside, south0, north0, south1, north1):
+    def by_moments(surface, inside, below, above):
+        return with_rims(inside, below, above), surface
+
+    def by_steps(surface, inside, below, above):
         surface = stepwise_surface(eta_adjoint, surface_damping, seam_codes[0] == 1)
-        solved, up1, down1, edges = columns_after(in_hbm(mark), jax.ShapeDtypeStruct)
-        up0, down0 = pl.pallas_call(
+        solved, edges = columns_after(in_hbm(mark), jax.ShapeDtypeStruct)
+        up, down = pl.pallas_call(
             outer_lines,
             out_shape=(line, line),
             in_specs=[SMEM, VMEM, VMEM],
@@ -507,11 +503,9 @@
             name="outer_lines",
         )(seam_codes, surface, edges)
         inside = inside_of(solved, surface, jax.ShapeDtypeStruct)
-        return with_rims(inside, *across(up0, down0), *across(up1, down1)), surface
-
-    return lax.cond(
-        sound[0] == 1, by_moments, by_steps, surface, inside, south0, north0, south1, north1
-    )
+        return with_rims(inside, *across(up, down)), surface
+
+    return lax.cond(sound[0] == 1, by_moments, by_steps, surface, inside, below, above)
 
 
 def solution(mesh):

time: 44.9 us -> 41.3 us (0.920)
  the two profiles are of different devices: /device:TPU:0 before, /device:TPU:1 now
where the time goes in v9:
time: 41.3 us; the launch traced here: 41 us
  Pallas kernels  14.4 us (35%)
  starting transfers between devices  11 us (27%)
  waiting for transfers between devices  9.1 us (22%)
  local copies, waits for them, and re-layouts  4.6 us (11%)
  between operations  1.97 us (5%)
    all_to_all x1, starting transfers between devices, shards(): sums = lax.all_to_all(sums, 'face', 0, 0)  6.64 us
    unnamed x10, local copies, waits for them, and re-layouts  4.6 us
    pallas_call x1, Pallas kernels, inside_of(): pl.pallas_call(inside_kernel, out_shape=place((tracers, levels, rows, wid...  4.5 us
    pallas_call x1, Pallas kernels, columns_after(): pl.pallas_call(column_kernel, out_shape=(place((3, levels, rows, width),...  3.91 us
    ppermute x1, waiting for transfers between devices, across(): lax.ppermute(up, 'face', upward)  2.78 us
    ppermute x1, starting transfers between devices, shards(): below = lax.ppermute(up, 'face', upward)  2.63 us
    pallas_call x1, Pallas kernels, with_rims(): pl.pallas_call(rim_kernel, out_shape=pltpu.HBM((tracers, levels, rows, wi...  2.56 us
    ppermute x1, waiting for transfers between devices, shards(): above = lax.ppermute(down, 'face', downward)  2.5 us
  transfers between devices with their start and end apart: 5, of which 4 were waited for; matrix products, arithmetic and copies ran while one was open for 0% of the time, Pallas kernels for 21%

profile of v9, /device:TPU:1, one launch (start us, length us, event | category | flops | bytes accessed | tf_op | source)
XLA Modules:
  0.0 41.0 jit_solution(14645587566976815611)
XLA Ops:
  1.3 1.4 %outer_rows.1 = (f32[8,1024]{1,0:T(8,128)}, f32[8,1024]{1,0:T(8,128)}, f32[16,1024]{1,0:T(8,128)S(1)}, f32[8,128]{1,0:T(8,128)}) custom-call(s32[1]{0:T(128)S(6)} %copy.17.seam, f32[8,1024]{1,0:T(8,128)} %eta.1, f32[8,1024]{1,0:T(8,128)} %damping.1), custom_call_target="tpu_custom_call" | custom-call | tf_op jit(solution)/shard_map/outer_rows/pallas_call | solution.py:394
  2.7 2.6 %collective-permute-start.10 = (f32[8,1024]{1,0:T(8,128)}, f32[8,1024]{1,0:T(8,128)S(1)}, u32[]{:S(2)}, u32[]{:S(2)}) collective-permute-start(f32[8,1024]{1,0:T(8,128)} %get-tuple-element.67), channel_id=1, source_target_pairs={{0,1},{1,2},{2,3},{3,4},{4,5},{5,6},{6,7},{7,8},{8,9},{9,10},{10,1... | collective-permute-start | bytes 98312 | tf_op jit(solution)/shard_map/ppermute | solution.py:406
  5.3 0.0 collective-permute-start.11
  5.3 1.3 %collective-permute-done.10.below = f32[8,1024]{1,0:T(8,128)S(1)} collective-permute-done((f32[8,1024]{1,0:T(8,128)}, f32[8,1024]{1,0:T(8,128)S(1)}, u32[]{:S(2)}, u32[]{:S(2)}) %collective-permute-start.10) | collective-permute-done | bytes 32800 | tf_op jit(solution)/shard_map/ppermute | solution.py:406
  6.7 2.5 %collective-permute-done.11.above = f32[8,1024]{1,0:T(8,128)S(1)} collective-permute-done((f32[8,1024]{1,0:T(8,128)}, f32[8,1024]{1,0:T(8,128)S(1)}, u32[]{:S(2)}, u32[]{:S(2)}) %collective-permute-start.11) | collective-permute-done | bytes 32800 | tf_op jit(solution)/shard_map/ppermute | solution.py:407
  9.2 1.1 %surface_basis.1 = (f32[4,16,1024]{2,1,0:T(8,128)S(1)}, f32[16,8,128]{2,1,0:T(8,128)}) custom-call(s32[1]{0:T(128)S(6)} %copy.17.seam, f32[16,1024]{1,0:T(8,128)S(1)} %get-tuple-element.66.own_rows, f32[8,1024]{1,0:T(8,128)S(1)} %collective-permute-done.10.below, f32[8,1024]{1,0:T(8,128)S(1)} %collective-permute-done.11.above), custom_call_target="tpu_custom_call" | custom-call | tf_op jit(solution)/shard_map/surface_basis/pallas_call | solution.py:467
  10.3 6.6 %all-to-all-start = ((f32[16,8,128]{2,1,0:T(8,128)}), f32[16,8,128]{2,1,0:T(8,128)S(1)}, u32[]{:S(2)}, u32[]{:S(2)}) async-start(f32[16,8,128]{2,1,0:T(8,128)} %get-tuple-element.69), calls=%async_computation | async-start | bytes 131072 | tf_op jit(solution)/shard_map/all_to_all | solution.py:479
  16.9 0.0 copy-start.5
  16.9 3.9 %columns.3 = (f32[3,50,8,1024]{3,2,1,0:T(8,128)S(1)}, f32[6,56,1024]{2,1,0:T(8,128)S(1)}) custom-call(s32[1]{0:T(128)S(6)} %copy.17.seam, f32[50]{0:T(128)} %thickness_from.1, f32[2,50,8,1024]{3,2,1,0:T(8,128)} %tracer.1, f32[49,8,1024]{2,1,0:T(8,128)} %mixing.1, f32[50,8,1024]{2,1,0:T(8,128)} %velocity_y.3, s32[8,1024]{1,0:T(8,128)} %wet.3, ...), custom_call_target="tpu_custom_call" | custom-call | flops 40000000 | bytes 13000000 | tf_op jit(solution)/shard_map/columns/pallas_call | solution.py:415
  20.8 0.0 copy-start.2
  20.8 2.2 %copy-done.2 = f32[3,50,8,1024]{3,2,1,0:T(8,128)} copy-done((f32[3,50,8,1024]{3,2,1,0:T(8,128)}, f32[3,50,8,1024]{3,2,1,0:T(8,128)S(1)}, u32[]{:S(2)}) %copy-start.2) | copy-done | bytes 4915224
  23.0 0.0 all-to-all-done.sums
  23.0 0.9 %surface.1 = (f32[8,1024]{1,0:T(8,128)}, f32[2,56,1024]{2,1,0:T(8,128)S(1)}, f32[2,56,1024]{2,1,0:T(8,128)S(1)}, s32[1]{0:T(128)}) custom-call(s32[1]{0:T(128)S(6)} %copy.17.seam, f32[16,8,128]{2,1,0:T(8,128)S(1)} %all-to-all-done.sums, f32[4,16,1024]{2,1,0:T(8,128)S(1)} %get-tuple-element.70.basis, f32[6,56,1024]{2,1,0:T(8,128)S(1)} %get-tuple-element.72.edges), custom_call_target="tpu_custom_call" | custom-call | tf_op jit(solution)/shard_map/surface/pallas_call | solution.py:480
  24.0 1.7 %collective-permute-start.12 = (f32[2,56,1024]{2,1,0:T(8,128)S(1)}, f32[2,56,1024]{2,1,0:T(8,128)S(1)}, u32[]{:S(2)}, u32[]{:S(2)}) collective-permute-start(f32[2,56,1024]{2,1,0:T(8,128)S(1)} %get-tuple-element.76), channel_id=1, source_target_pairs={{0,1},{1,2},{2,3},{3,4},{4,5},{5,6},{6,7},{7,8},{8,9},{9,10},{10,1... | collective-permute-start | bytes 1376264 | tf_op jit(solution)/shard_map/ppermute | solution.py:465
  25.6 0.0 collective-permute-start.13
  25.6 0.0 copy-done.5
  25.6 0.0 copy-start.3
  25.6 2.4 %copy-done.3 = f32[3,50,8,1024]{3,2,1,0:T(8,128)S(1)} copy-done((f32[3,50,8,1024]{3,2,1,0:T(8,128)S(1)}, f32[3,50,8,1024]{3,2,1,0:T(8,128)}, u32[]{:S(2)}) %copy-start.3) | copy-done | bytes 4915224
  28.0 0.0 copy-start.4
  28.0 0.0 copy-start.8
  28.0 4.5 %inside.3 = f32[2,50,8,1024]{3,2,1,0:T(8,128)S(1)} custom-call(f32[3,50,8,1024]{3,2,1,0:T(8,128)S(1)} %copy-done.3, f32[50,8,1024]{2,1,0:T(8,128)} %velocity_x.1, f32[50,8,1024]{2,1,0:T(8,128)} %velocity_y.3, s32[8,1024]{1,0:T(8,128)S(1)} %copy-done.5, f32[8,1024]{1,0:T(8,128)} %get-tuple-element.75.surface), custom_call_target="tpu_custom_call" | custom-call | flops 1000 | bytes 1000 | tf_op jit(solution)/shard_map/inside/pallas_call | solution.py:440
  33.2 2.8 %collective-permute-done.12 = f32[2,56,1024]{2,1,0:T(8,128)S(1)} collective-permute-done((f32[2,56,1024]{2,1,0:T(8,128)S(1)}, f32[2,56,1024]{2,1,0:T(8,128)S(1)}, u32[]{:S(2)}, u32[]{:S(2)}) %collective-permute-start.12) | collective-permute-done | bytes 458784 | tf_op jit(solution)/shard_map/ppermute | solution.py:465
  36.0 2.5 %collective-permute-done.13 = f32[2,56,1024]{2,1,0:T(8,128)S(1)} collective-permute-done((f32[2,56,1024]{2,1,0:T(8,128)S(1)}, f32[2,56,1024]{2,1,0:T(8,128)S(1)}, u32[]{:S(2)}, u32[]{:S(2)}) %collective-permute-start.13) | collective-permute-done | bytes 458784 | tf_op jit(solution)/shard_map/ppermute | solution.py:465
  38.5 0.0 copy-done.4
  38.5 0.0 copy-done.8
  38.5 2.6 %conditional.1 = (f32[8,1024]{1,0:T(8,128)}, f32[2,50,8,1024]{3,2,1,0:T(8,128)}) conditional(s32[]{:T(128)} %bitcast.1, (s32[1]{0:T(128)}, f32[50]{0:T(128)}, f32[2,50,8,1024]{3,2,1,0:T(8,128)}, f32[49,8,1024]{2,1,0:T(8,128)}, f32[50,8,1024]{2,1,0:T(8,128)}, /*index=5*/s32[8,1024]{1,0:T(8,128)S(1)}, f32[8,128]{1,0:T(8,128)}, ...), branch_computations={%region_0.17_spmd, %region_17.18_spmd} | conditional | flops 40672752 | bytes 59237424 | solution.py:508
  38.5 2.6 %rims.3 = f32[2,50,8,1024]{3,2,1,0:T(8,128)} custom-call(s32[1]{0:T(128)} %get-tuple-element.46.seam, f32[2,50,8,1024]{3,2,1,0:T(8,128)S(1)} %get-tuple-element.47.inside, s32[8,1024]{1,0:T(8,128)S(1)} %get-tuple-element.48.wet, f32[2,56,1024]{2,1,0:T(8,128)S(1)} %get-tuple-element.49.below, f32[2,56,1024]{2,1,0:T(8,128)S(1)} %get-tuple-element.50.above), custom_call_target="tpu_custom_call" | custom-call | tf_op jit(solution)/shard_map/cond/branch_1_fun/rims/pallas_call | solution.py:451
Async XLA Ops:
  2.7 4.0 %collective-permute-start.10 = (f32[8,1024]{1,0:T(8,128)}, f32[8,1024]{1,0:T(8,128)S(1)}, u32[]{:S(2)}, u32[]{:S(2)}) collective-permute-start(f32[8,1024]{1,0:T(8,128)} %get-tuple-element.67), channel_id=1, source_target_pairs={{0,1},{1,2},{2,3},{3,4},{4,5},{5,6},{6,7},{7,8},{8,9},{9,10},{10,1... | collective-permute-start | bytes 98312 | tf_op jit(solution)/shard_map/ppermute | solution.py:406
  5.3 3.8 %collective-permute-start.11 = (f32[8,1024]{1,0:T(8,128)}, f32[8,1024]{1,0:T(8,128)S(1)}, u32[]{:S(2)}, u32[]{:S(2)}) collective-permute-start(f32[8,1024]{1,0:T(8,128)} %get-tuple-element.68), channel_id=1, source_target_pairs={{1,0},{2,1},{3,2},{4,3},{5,4},{6,5},{7,6},{8,7},{9,8},{10,9},{11,1... | collective-permute-start | bytes 98312 | tf_op jit(solution)/shard_map/ppermute | solution.py:407
  10.3 12.8 %all-to-all-start = ((f32[16,8,128]{2,1,0:T(8,128)}), f32[16,8,128]{2,1,0:T(8,128)S(1)}, u32[]{:S(2)}, u32[]{:S(2)}) async-start(f32[16,8,128]{2,1,0:T(8,128)} %get-tuple-element.69), calls=%async_computation | async-start | bytes 131072 | tf_op jit(solution)/shard_map/all_to_all | solution.py:479
  16.9 8.7 %copy-start.5 = (s32[8,1024]{1,0:T(8,128)S(1)}, s32[8,1024]{1,0:T(8,128)}, u32[]{:S(2)}) copy-start(s32[8,1024]{1,0:T(8,128)} %wet.3) | copy-start | bytes 98308
  20.8 2.2 %copy-start.2 = (f32[3,50,8,1024]{3,2,1,0:T(8,128)}, f32[3,50,8,1024]{3,2,1,0:T(8,128)S(1)}, u32[]{:S(2)}) copy-start(f32[3,50,8,1024]{3,2,1,0:T(8,128)S(1)} %get-tuple-element.74.solved) | copy-start | bytes 14745604
  24.0 12.0 %collective-permute-start.12 = (f32[2,56,1024]{2,1,0:T(8,128)S(1)}, f32[2,56,1024]{2,1,0:T(8,128)S(1)}, u32[]{:S(2)}, u32[]{:S(2)}) collective-permute-start(f32[2,56,1024]{2,1,0:T(8,128)S(1)} %get-tuple-element.76), channel_id=1, source_target_pairs={{0,1},{1,2},{2,3},{3,4},{4,5},{5,6},{6,7},{7,8},{8,9},{9,10},{10,1... | collective-permute-start | bytes 1376264 | tf_op jit(solution)/shard_map/ppermute | solution.py:465
  25.6 12.8 %collective-permute-start.13 = (f32[2,56,1024]{2,1,0:T(8,128)S(1)}, f32[2,56,1024]{2,1,0:T(8,128)S(1)}, u32[]{:S(2)}, u32[]{:S(2)}) collective-permute-start(f32[2,56,1024]{2,1,0:T(8,128)S(1)} %get-tuple-element.77), channel_id=1, source_target_pairs={{1,0},{2,1},{3,2},{4,3},{5,4},{6,5},{7,6},{8,7},{9,8},{10,9},{11,1... | collective-permute-start | bytes 1376264 | tf_op jit(solution)/shard_map/ppermute | solution.py:465
  25.6 2.4 %copy-start.3 = (f32[3,50,8,1024]{3,2,1,0:T(8,128)S(1)}, f32[3,50,8,1024]{3,2,1,0:T(8,128)}, u32[]{:S(2)}) copy-start(f32[3,50,8,1024]{3,2,1,0:T(8,128)} %copy-done.2) | copy-start | bytes 14745604
  28.0 10.4 %copy-start.4 = (f32[8,1024]{1,0:T(8,128)S(1)}, f32[8,1024]{1,0:T(8,128)}, u32[]{:S(2)}) copy-start(f32[8,1024]{1,0:T(8,128)} %eta.1) | copy-start | bytes 98308
  28.0 10.4 %copy-start.8 = (f32[8,1024]{1,0:T(8,128)S(1)}, f32[8,1024]{1,0:T(8,128)}, u32[]{:S(2)}) copy-start(f32[8,1024]{1,0:T(8,128)} %damping.1) | copy-start | bytes 98308

commit v10 on v8

--- a/solution.py
+++ b/solution.py
@@ -146,7 +146,11 @@
         for start in range(LANES, width, LANES):
             total = total + product[:, start : start + LANES]
         parts.append(jnp.sum(jnp.where(own, total, 0.0), axis=0, keepdims=True))
-    tile = jnp.concatenate(parts, axis=0)
+    tile = jnp.sum(jnp.concatenate(parts, axis=0), axis=1, keepdims=True)
+    shape = (2 * ITERS, LANES)
+    place = lax.broadcasted_iota(jnp.int32, shape, 0)
+    own_lane = place == lax.broadcasted_iota(jnp.int32, shape, 1)
+    tile = jnp.sum(jnp.where(own_lane, tile, 0.0), axis=0, keepdims=True)
     for i in range(sums.shape[0]):
         sums[i] = tile
 
@@ -213,8 +217,7 @@
     while len(parts) > 1:
         pairs = [a + b for a, b in zip(parts[::2], parts[1::2])]
         parts = pairs + parts[len(parts) - len(parts) % 2 :]
-    total = jnp.sum(parts[0], axis=1, keepdims=True)
-    raw = [total[j : j + 1, :] for j in range(2 * ITERS)]
+    raw = [parts[0][:, j : j + 1] for j in range(2 * ITERS)]
     moments = raw[:2]
     for j in range(2, 2 * ITERS):
         moments.append(2.0 * raw[j] - raw[j % 2])
@@ -468,7 +471,7 @@
         basis_kernel,
         out_shape=(
             ext,
-            jax.ShapeDtypeStruct((count, SUBLANES, LANES), f32),
+            jax.ShapeDtypeStruct((count, 1, LANES), f32),
         ),
         in_specs=[SMEM] + [VMEM] * 3,
         out_specs=(VMEM, VMEM),

time: 40.2 us -> 39.8 us (0.990)
  blocking collectives: 9.47 us -> 8.97 us
    all_to_all x1, blocking collectives: 9.47 us -> 8.97 us  [shards(): sums = lax.all_to_all(sums, 'face', 0, 0)]
  transfers between devices with their start and end apart: 6 -> 6, of which waited for: 0 -> 0; matrix products, arithmetic and copies ran while one was open for 0% -> 0% of each run, Pallas kernels for 18% -> 19%
where the time goes in v10:
time: 39.8 us; the launch traced here: 39.4 us
  starting transfers between devices  14.3 us (36%)
  Pallas kernels  14 us (35%)
  blocking collectives  8.97 us (23%)
  between operations  2.06 us (5%)
    all_to_all x1, blocking collectives, shards(): sums = lax.all_to_all(sums, 'face', 0, 0)  8.97 us
    ppermute x2, starting transfers between devices, across(): lax.ppermute(down, 'face', downward)  8.86 us
    ppermute x1, starting transfers between devices, shards(): above = lax.ppermute(down, 'face', downward)  4.91 us
    pallas_call x1, Pallas kernels, columns_after(): pl.pallas_call(column_kernel, out_shape=(place((3, levels, rows, width),...  4.05 us
    pallas_call x1, Pallas kernels, with_rims(): pl.pallas_call(rim_kernel, out_shape=pltpu.HBM((tracers, levels, rows, wi...  3.61 us
    pallas_call x1, Pallas kernels, inside_of(): pl.pallas_call(inside_kernel, out_shape=place((tracers, levels, rows, wid...  3.33 us
    pallas_call x1, Pallas kernels, shards(): pl.pallas_call(outer_kernel, out_shape=(tile, tile, pltpu.VMEM((2 * rows,...  1.5 us
    pallas_call x1, Pallas kernels, shards(): pl.pallas_call(surface_kernel, out_shape=(tile, line, line, jax.ShapeDtyp...  1.02 us
  transfers between devices with their start and end apart: 6, of which 0 were waited for; matrix products, arithmetic and copies ran while one was open for 0% of the time, Pallas kernels for 19%

profile of v10, /device:TPU:0, one launch (start us, length us, event | category | flops | bytes accessed | tf_op | source)
XLA Modules:
  0.0 39.4 jit_solution(11950576583179713361)
XLA Ops:
  1.3 1.5 %outer_rows.1 = (f32[8,1024]{1,0:T(8,128)}, f32[8,1024]{1,0:T(8,128)}, f32[16,1024]{1,0:T(8,128)S(1)}, f32[8,128]{1,0:T(8,128)}) custom-call(s32[1]{0:T(128)S(6)} %copy.17.seam, f32[8,1024]{1,0:T(8,128)} %eta.1, f32[8,1024]{1,0:T(8,128)} %damping.1), custom_call_target="tpu_custom_call" | custom-call | tf_op jit(solution)/shard_map/outer_rows/pallas_call | solution.py:395
  2.8 0.5 %collective-permute-start.12 = (f32[8,1024]{1,0:T(8,128)}, f32[8,1024]{1,0:T(8,128)S(1)}, u32[]{:S(2)}, u32[]{:S(2)}) collective-permute-start(f32[8,1024]{1,0:T(8,128)} %get-tuple-element.83), channel_id=1, source_target_pairs={{0,1},{1,2},{2,3},{3,4},{4,5},{5,6},{6,7},{7,8},{8,9},{9,10},{10,1... | collective-permute-start | bytes 98312 | tf_op jit(solution)/shard_map/ppermute | solution.py:407
  3.2 4.9 %collective-permute-start.13 = (f32[8,1024]{1,0:T(8,128)}, f32[8,1024]{1,0:T(8,128)S(1)}, u32[]{:S(2)}, u32[]{:S(2)}) collective-permute-start(f32[8,1024]{1,0:T(8,128)} %get-tuple-element.84), channel_id=1, source_target_pairs={{1,0},{2,1},{3,2},{4,3},{5,4},{6,5},{7,6},{8,7},{9,8},{10,9},{11,1... | collective-permute-start | bytes 98312 | tf_op jit(solution)/shard_map/ppermute | solution.py:408
  8.1 0.0 copy-start.2
  8.1 0.0 copy-start.5
  8.1 0.0 copy-start.10
  8.2 4.0 %columns.3 = (f32[3,50,8,1024]{3,2,1,0:T(8,128)S(1)}, f32[56,1024]{1,0:T(8,128)S(1)}, f32[56,1024]{1,0:T(8,128)S(1)}, f32[4,56,1024]{2,1,0:T(8,128)S(1)}) custom-call(s32[1]{0:T(128)S(6)} %copy.17.seam, f32[50]{0:T(128)} %thickness_from.1, f32[2,50,8,1024]{3,2,1,0:T(8,128)} %tracer.1, f32[49,8,1024]{2,1,0:T(8,128)} %mixing.1, f32[50,8,1024]{2,1,0:T(8,128)} %velocity_y.3, ...), custom_call_target="tpu_custom_call" | custom-call | flops 40000000 | bytes 13000000 | tf_op jit(solution)/shard_map/columns/pallas_call | solution.py:416
  12.2 0.0 collective-permute-done.12.below
  12.2 0.0 collective-permute-done.13.above
  12.2 0.5 %surface_basis.1 = (f32[4,16,1024]{2,1,0:T(8,128)S(1)}, f32[16,1,128]{2,1,0:T(1,128)S(1)}) custom-call(s32[1]{0:T(128)S(6)} %copy.17.seam, f32[16,1024]{1,0:T(8,128)S(1)} %get-tuple-element.82.own_rows, f32[8,1024]{1,0:T(8,128)S(1)} %collective-permute-done.12.below, f32[8,1024]{1,0:T(8,128)S(1)} %collective-permute-done.13.above), custom_call_target="tpu_custom_call" | custom-call | tf_op jit(solution)/shard_map/surface_basis/pallas_call | solution.py:470
  12.8 0.0 collective-permute-start.14
  12.8 4.4 %collective-permute-start.15 = (f32[56,1024]{1,0:T(8,128)S(1)}, f32[56,1024]{1,0:T(8,128)S(1)}, u32[]{:S(2)}, u32[]{:S(2)}) collective-permute-start(f32[56,1024]{1,0:T(8,128)S(1)} %get-tuple-element.91), channel_id=1, source_target_pairs={{1,0},{2,1},{3,2},{4,3},{5,4},{6,5},{7,6},{8,7},{9,8},{10,9},{11,1... | collective-permute-start | bytes 688136 | tf_op jit(solution)/shard_map/ppermute | solution.py:468
  17.2 9.0 %all_to_all.5.sums = f32[16,1,128]{2,1,0:T(1,128)S(1)} all-to-all(f32[16,1,128]{2,1,0:T(1,128)S(1)} %get-tuple-element.89), channel_id=1, replica_groups=mesh['ens'=2,'face'=16] {'face'}, dimensions={0} | all-to-all | bytes 16384 | tf_op jit(solution)/shard_map/all_to_all | solution.py:483
  26.2 0.0 collective-permute-done.14
  26.2 0.0 copy-start.14
  26.2 0.0 collective-permute-done.15
  26.2 0.0 copy-start.15
  26.2 1.0 %surface.1 = (f32[8,1024]{1,0:T(8,128)}, f32[56,1024]{1,0:T(8,128)S(1)}, f32[56,1024]{1,0:T(8,128)S(1)}, s32[1]{0:T(128)}) custom-call(s32[1]{0:T(128)S(6)} %copy.17.seam, f32[16,1,128]{2,1,0:T(1,128)S(1)} %all_to_all.5.sums, f32[4,16,1024]{2,1,0:T(8,128)S(1)} %get-tuple-element.93.basis, f32[4,56,1024]{2,1,0:T(8,128)S(1)} %get-tuple-element.94.edges), custom_call_target="tpu_custom_call" | custom-call | tf_op jit(solution)/shard_map/surface/pallas_call | solution.py:487
  27.2 0.1 collective-permute-start.16
  27.3 4.4 %collective-permute-start.17 = (f32[56,1024]{1,0:T(8,128)S(1)}, f32[56,1024]{1,0:T(8,128)S(1)}, u32[]{:S(2)}, u32[]{:S(2)}) collective-permute-start(f32[56,1024]{1,0:T(8,128)S(1)} %get-tuple-element.99), channel_id=1, source_target_pairs={{1,0},{2,1},{3,2},{4,3},{5,4},{6,5},{7,6},{8,7},{9,8},{10,9},{11,1... | collective-permute-start | bytes 688136 | tf_op jit(solution)/shard_map/ppermute | solution.py:468
  31.7 0.0 copy-done.14
  31.7 0.0 copy-done.15
  31.7 0.0 copy-done.2
  31.7 0.0 copy-done.5
  31.8 0.0 copy-done.10
  31.8 0.0 copy-start.7
  31.8 0.0 copy-start.13
  31.8 3.3 %inside.3 = f32[2,50,8,1024]{3,2,1,0:T(8,128)S(1)} custom-call(f32[3,50,8,1024]{3,2,1,0:T(8,128)S(1)} %get-tuple-element.96.solved, f32[50,8,1024]{2,1,0:T(8,128)S(1)} %copy-done.5, f32[50,8,1024]{2,1,0:T(8,128)S(1)} %copy-done.2, s32[8,1024]{1,0:T(8,128)S(1)} %copy-done.10, f32[8,1024]{1,0:T(8,128)} %get-tuple-element.97.surface), custom_call_target="tpu_custom_call" | custom-call | flops 1000 | bytes 1000 | tf_op jit(solution)/shard_map/inside/pallas_call | solution.py:443
  35.8 0.0 collective-permute-done.16
  35.8 0.0 collective-permute-done.17
  35.8 0.0 copy-done.7
  35.8 0.0 copy-done.13
  35.8 3.6 %conditional.1 = (f32[8,1024]{1,0:T(8,128)}, f32[2,50,8,1024]{3,2,1,0:T(8,128)}) conditional(s32[]{:T(128)} %bitcast.1, (s32[1]{0:T(128)}, f32[50]{0:T(128)}, f32[2,50,8,1024]{3,2,1,0:T(8,128)}, f32[49,8,1024]{2,1,0:T(8,128)}, f32[50,8,1024]{2,1,0:T(8,128)S(1)}, /*index=5*/s32[8,1024]{1,0:T(8,128)S(1)}, f32[8,128]{1,0:T(8,128)}, ...), branch_computations={%region_0.17_spmd, %region_17.18_spmd} | conditional | flops 40672752 | bytes 79160584 | solution.py:515
  35.8 3.6 %rims.3 = f32[2,50,8,1024]{3,2,1,0:T(8,128)} custom-call(s32[1]{0:T(128)} %get-tuple-element.52.seam, f32[2,50,8,1024]{3,2,1,0:T(8,128)S(1)} %get-tuple-element.53.inside, s32[8,1024]{1,0:T(8,128)S(1)} %get-tuple-element.54.wet, f32[56,1024]{1,0:T(8,128)S(1)} %get-tuple-element.55.south0, f32[56,1024]{1,0:T(8,128)S(1)} %get-tuple-element.56.north0, ...), custom_call_target="tpu_custom_call" | custom-call | tf_op jit(solution)/shard_map/cond/branch_1_fun/rims/pallas_call | solution.py:454
Async XLA Ops:
  2.8 9.4 %collective-permute-start.12 = (f32[8,1024]{1,0:T(8,128)}, f32[8,1024]{1,0:T(8,128)S(1)}, u32[]{:S(2)}, u32[]{:S(2)}) collective-permute-start(f32[8,1024]{1,0:T(8,128)} %get-tuple-element.83), channel_id=1, source_target_pairs={{0,1},{1,2},{2,3},{3,4},{4,5},{5,6},{6,7},{7,8},{8,9},{9,10},{10,1... | collective-permute-start | bytes 98312 | tf_op jit(solution)/shard_map/ppermute | solution.py:407
  3.2 9.0 %collective-permute-start.13 = (f32[8,1024]{1,0:T(8,128)}, f32[8,1024]{1,0:T(8,128)S(1)}, u32[]{:S(2)}, u32[]{:S(2)}) collective-permute-start(f32[8,1024]{1,0:T(8,128)} %get-tuple-element.84), channel_id=1, source_target_pairs={{1,0},{2,1},{3,2},{4,3},{5,4},{6,5},{7,6},{8,7},{9,8},{10,9},{11,1... | collective-permute-start | bytes 98312 | tf_op jit(solution)/shard_map/ppermute | solution.py:408
  8.1 23.6 %copy-start.2 = (f32[50,8,1024]{2,1,0:T(8,128)S(1)}, f32[50,8,1024]{2,1,0:T(8,128)}, u32[]{:S(2)}) copy-start(f32[50,8,1024]{2,1,0:T(8,128)} %velocity_y.3) | copy-start | bytes 4915204
  8.1 23.6 %copy-start.5 = (f32[50,8,1024]{2,1,0:T(8,128)S(1)}, f32[50,8,1024]{2,1,0:T(8,128)}, u32[]{:S(2)}) copy-start(f32[50,8,1024]{2,1,0:T(8,128)} %velocity_x.1) | copy-start | bytes 4915204
  8.1 23.6 %copy-start.10 = (s32[8,1024]{1,0:T(8,128)S(1)}, s32[8,1024]{1,0:T(8,128)}, u32[]{:S(2)}) copy-start(s32[8,1024]{1,0:T(8,128)} %wet.3) | copy-start | bytes 98308
  12.8 13.4 %collective-permute-start.14 = (f32[56,1024]{1,0:T(8,128)S(1)}, f32[56,1024]{1,0:T(8,128)S(1)}, u32[]{:S(2)}, u32[]{:S(2)}) collective-permute-start(f32[56,1024]{1,0:T(8,128)S(1)} %get-tuple-element.90), channel_id=1, source_target_pairs={{0,1},{1,2},{2,3},{3,4},{4,5},{5,6},{6,7},{7,8},{8,9},{9,10},{10,1... | collective-permute-start | bytes 688136 | tf_op jit(solution)/shard_map/ppermute | solution.py:468
  12.8 13.4 %collective-permute-start.15 = (f32[56,1024]{1,0:T(8,128)S(1)}, f32[56,1024]{1,0:T(8,128)S(1)}, u32[]{:S(2)}, u32[]{:S(2)}) collective-permute-start(f32[56,1024]{1,0:T(8,128)S(1)} %get-tuple-element.91), channel_id=1, source_target_pairs={{1,0},{2,1},{3,2},{4,3},{5,4},{6,5},{7,6},{8,7},{9,8},{10,9},{11,1... | collective-permute-start | bytes 688136 | tf_op jit(solution)/shard_map/ppermute | solution.py:468
  26.2 5.5 %copy-start.14 = (f32[56,1024]{1,0:T(8,128)}, f32[56,1024]{1,0:T(8,128)S(1)}, u32[]{:S(2)}) copy-start(f32[56,1024]{1,0:T(8,128)S(1)} %collective-permute-done.14) | copy-start | bytes 688132
  26.2 5.5 %copy-start.15 = (f32[56,1024]{1,0:T(8,128)}, f32[56,1024]{1,0:T(8,128)S(1)}, u32[]{:S(2)}) copy-start(f32[56,1024]{1,0:T(8,128)S(1)} %collective-permute-done.15) | copy-start | bytes 688132
  27.2 8.5 %collective-permute-start.16 = (f32[56,1024]{1,0:T(8,128)S(1)}, f32[56,1024]{1,0:T(8,128)S(1)}, u32[]{:S(2)}, u32[]{:S(2)}) collective-permute-start(f32[56,1024]{1,0:T(8,128)S(1)} %get-tuple-element.98), channel_id=1, source_target_pairs={{0,1},{1,2},{2,3},{3,4},{4,5},{5,6},{6,7},{7,8},{8,9},{9,10},{10,1... | collective-permute-start | bytes 688136 | tf_op jit(solution)/shard_map/ppermute | solution.py:468
  27.3 8.5 %collective-permute-start.17 = (f32[56,1024]{1,0:T(8,128)S(1)}, f32[56,1024]{1,0:T(8,128)S(1)}, u32[]{:S(2)}, u32[]{:S(2)}) collective-permute-start(f32[56,1024]{1,0:T(8,128)S(1)} %get-tuple-element.99), channel_id=1, source_target_pairs={{1,0},{2,1},{3,2},{4,3},{5,4},{6,5},{7,6},{8,7},{9,8},{10,9},{11,1... | collective-permute-start | bytes 688136 | tf_op jit(solution)/shard_map/ppermute | solution.py:468
  31.8 4.0 %copy-start.7 = (f32[8,1024]{1,0:T(8,128)S(1)}, f32[8,1024]{1,0:T(8,128)}, u32[]{:S(2)}) copy-start(f32[8,1024]{1,0:T(8,128)} %eta.1) | copy-start | bytes 98308
  31.8 4.0 %copy-start.13 = (f32[8,1024]{1,0:T(8,128)S(1)}, f32[8,1024]{1,0:T(8,128)}, u32[]{:S(2)}) copy-start(f32[8,1024]{1,0:T(8,128)} %damping.1) | copy-start | bytes 98308
